TPU v7x, 512 devices: a whole 4x4x16 slice. The times are simulated.
512 devices in a mesh: member: 16 (over y, x_lo, core), patch: 32 (over z, x_hi).
Axes of the slice: x: 4 (x_hi: 2, x_lo: 2; x = x_hi * 2 + x_lo), y: 4, z: 16, core: 2. Of those that a mesh axis runs over, the one named last changes fastest.
Arguments:
- kernel_rows: bfloat16 [8192, 8192], P('patch'), as said below
- row_scale: float32 [8192], P('patch'), may hold values from 0.3 to 1
- self_stiffness: float32 [8192], P('patch'), may hold values from 1 to 3
- base_stress: float32 [8192], P('patch'), may hold values from 0.5 to 2.5
- friction_rate: float32 [8192], P('patch'), may hold values from 0.5 to 2
- damping: float32 [8192], P('patch'), may hold values from 0.5 to 2
- deficit_start: float32 [96, 8192], P('member', 'patch'), may hold values from -3 to 3
- state_start: float32 [96, 8192], P('member', 'patch'), may hold values from -1 to 1
- obs_rate: float32 [8192], P('patch'), may hold values from -6 to 6
- obs_precision: float32 [8192], P('patch'), may hold values from 0.2 to 2
Outputs:
- analysis: float32 [3, 96, 32, 256], P(None, None, 'patch', 'member')
Inputs may be any that keep to these rules, and one draw needn't show every extreme that they name: `kernel_rows`: entries are independent with mean zero and root mean square of order 8192 ** -0.5 times a per-row factor.
All inputs are finite; a program needn't handle non-finite values.
Results may differ from a plain program's by a relative error of at most 0.0006.
Values may be sent and summed in bfloat16 or wider, within the bound.
No kernel may reach another device: no remote copies, remote signals or barrier semaphores. Data moves between devices by JAX's collectives and lax.ppermute only.
A program may use at most 64 MiB of HBM per device.

v0:
```python
import jax
import jax.numpy as jnp
from jax import lax
from jax.sharding import PartitionSpec as P

STEPS = 2
NEWTON = 4
NS_ITERS = 6
MARGIN = 8


time_step = 0.25
plate_rate = 1.0


def from_everyone(x, axis):
    copies = jnp.broadcast_to(x, (lax.axis_size(axis), *x.shape))
    return lax.all_to_all(copies, axis, split_axis=0, concat_axis=0, tiled=True)


def joined_along(blocks, dim):
    blocks = jnp.moveaxis(blocks, 0, dim)
    dims = blocks.shape
    return blocks.reshape(*dims[:dim], dims[dim] * dims[dim + 1], *dims[dim + 2 :])


def gather_directly(x, axis, dim):
    blocks = from_everyone(x, axis)
    return joined_along(blocks, dim)


def shifted(block, axis, distance):
    devices = range(lax.axis_size(axis))
    route = [((i - distance) % len(devices), i) for i in devices]
    return lax.ppermute(block, axis, route)


def shifted_2(value, axis, steps):
    count = lax.axis_size(axis)
    first, last = (max(0, -steps), min(count, count - steps))
    return lax.ppermute(value, axis, [(source, source + steps) for source in range(first, last)])


def padded(cells, sides, width):
    for axis, dim in sides:
        count = lax.axis_size(axis)
        ends = count - 1
        head = lax.slice_in_dim(cells, 0, width, axis=dim)
        tail = lax.slice_in_dim(cells, cells.shape[dim] - width, cells.shape[dim], axis=dim)
        cells = jnp.concatenate(
            [
                lax.ppermute(tail, axis, [(i, (i + 1) % count) for i in range(ends)]),
                cells,
                lax.ppermute(head, axis, [((i + 1) % count, i) for i in range(ends)]),
            ],
            axis=dim,
        )
    return cells


def inverse_sinh(value):
    magnitude = jnp.abs(value)
    result = jnp.log(magnitude + jnp.sqrt(magnitude * magnitude + 1.0))
    return jnp.where(value < 0, -result, result)


def slip_rate(stress, state_log, guess, friction_rate, damping):
    factor = 0.5 * jnp.exp(state_log / friction_rate)
    velocity = guess
    for _ in range(NEWTON):
        scaled = factor * velocity
        residual = friction_rate * inverse_sinh(scaled) + damping * velocity - stress
        derivative = friction_rate * factor / jnp.sqrt(1.0 + scaled * scaled) + damping
        velocity = velocity - residual / derivative
    return velocity


def analyse(local_state, rate_window, obs_window):
    ensemble = rate_window.shape[0]
    window_width = rate_window.shape[1]
    sub_block = local_state.shape[2]
    margin = (window_width - sub_block) // 2
    highest = lax.Precision.HIGHEST
    mean_rate = jnp.mean(rate_window, axis=0)
    anomalies = rate_window - mean_rate[None, :]
    innovation = obs_window[0] - mean_rate
    distance = jnp.abs(
        jnp.arange(sub_block, dtype=jnp.int32)[:, None]
        + margin
        - jnp.arange(window_width, dtype=jnp.int32)[None, :]
    ).astype(jnp.float32)
    tapering = jnp.where(distance <= margin, jnp.exp(-0.5 * (distance / margin) ** 2), 0.0)
    weights = tapering * obs_window[1][None, :]
    weighted = anomalies[None, :, :] * weights[:, None, :]
    cross_terms = jnp.einsum("imj,nj->imn", weighted, anomalies, precision=highest)
    drive_terms = jnp.einsum("imj,j->im", weighted, innovation, precision=highest)
    identity = jnp.eye(ensemble, dtype=jnp.float32)
    scaling = ensemble - 1.0 + jnp.trace(cross_terms, axis1=1, axis2=2)
    root_part = ((ensemble - 1.0) * identity[None] + cross_terms) / scaling[:, None, None]
    inverse_root = jnp.broadcast_to(identity, root_part.shape)
    for _ in range(NS_ITERS):
        mixing = 1.5 * identity[None] - 0.5 * jnp.matmul(inverse_root, root_part, precision=highest)
        root_part = jnp.matmul(root_part, mixing, precision=highest)
        inverse_root = jnp.matmul(mixing, inverse_root, precision=highest)
    half_step = jnp.einsum("imn,in->im", inverse_root, drive_terms, precision=highest)
    mean_weight = (
        jnp.einsum("imn,in->im", inverse_root, half_step, precision=highest) / scaling[:, None]
    )
    spread = jnp.sqrt(ensemble - 1.0) * inverse_root / jnp.sqrt(scaling)[:, None, None]
    combined = spread + mean_weight[:, :, None]
    state_mean = jnp.mean(local_state, axis=1)
    state_spread = local_state - state_mean[:, None, :]
    return state_mean[:, None, :] + jnp.einsum(
        "vmi,imk->vki", state_spread, combined, precision=highest
    )


def body(
    kernel_rows,
    row_scale,
    self_stiffness,
    base_stress,
    friction_rate,
    damping,
    deficit_start,
    state_start,
    obs_rate,
    obs_precision,
):
    groups = lax.axis_size("member")
    own_rows = kernel_rows.shape[0]
    members = deficit_start.shape[0]
    sub_block = own_rows // groups
    margin = MARGIN

    def coupling(deficit):
        rounded = deficit.astype(jnp.bfloat16)
        summed = lax.dot_general(
            gather_directly(rounded, "patch", 1),
            kernel_rows,
            (((1,), (1,)), ((), ())),
            preferred_element_type=jnp.float32,
        )
        return base_stress + self_stiffness * deficit + row_scale * summed

    def tendency(deficit, state_log, guess):
        velocity = slip_rate(coupling(deficit), state_log, guess, friction_rate, damping)
        return (plate_rate - velocity, jnp.exp(-state_log) - jnp.abs(velocity), velocity)

    deficit = deficit_start
    state_log = state_start
    velocity = jnp.zeros_like(deficit_start)
    for _ in range(STEPS):
        deficit_zero, state_zero = (deficit, state_log)
        change, state_change, velocity = tendency(deficit_zero, state_zero, velocity)
        deficit_one = deficit_zero + time_step * change
        state_one = state_zero + time_step * state_change
        change, state_change, velocity = tendency(deficit_one, state_one, velocity)
        deficit_two = 0.75 * deficit_zero + 0.25 * (deficit_one + time_step * change)
        state_two = 0.75 * state_zero + 0.25 * (state_one + time_step * state_change)
        change, state_change, velocity = tendency(deficit_two, state_two, velocity)
        deficit = deficit_zero / 3.0 + 2.0 / 3.0 * (deficit_two + time_step * change)
        state_log = state_zero / 3.0 + 2.0 / 3.0 * (state_two + time_step * state_change)
    velocity = slip_rate(coupling(deficit), state_log, velocity, friction_rate, damping)
    stacked = jnp.stack([deficit, state_log, velocity])
    observed = jnp.stack([obs_rate, obs_precision])
    group_index = lax.axis_index("member")
    regrouped = lax.all_to_all(
        stacked.reshape(3, members, groups, sub_block),
        "member",
        split_axis=2,
        concat_axis=1,
        tiled=True,
    )
    local_state = regrouped[:, :, 0, :]
    rate_core = local_state[2]
    upper_edge = rate_core[:, sub_block - margin :]
    lower_edge = rate_core[:, :margin]
    from_before = shifted(upper_edge, "member", 1)
    before_far = shifted_2(from_before, "patch", 1)
    lower_rim = jnp.where(group_index == 0, before_far, from_before)
    from_after = shifted(lower_edge, "member", -1)
    after_far = shifted_2(from_after, "patch", -1)
    upper_rim = jnp.where(group_index == groups - 1, after_far, from_after)
    rate_window = jnp.concatenate([lower_rim, rate_core, upper_rim], axis=1)
    padded_obs = padded(observed, (("patch", 1),), margin)
    obs_window = lax.dynamic_slice_in_dim(
        padded_obs, group_index * sub_block, sub_block + 2 * margin, 1
    )
    analysis = analyse(local_state, rate_window, obs_window)
    return analysis[:, :, None, :]


def solution(mesh):
    return jax.shard_map(
        body,
        mesh=mesh,
        in_specs=(
            P("patch", None),
            P("patch"),
            P("patch"),
            P("patch"),
            P("patch"),
            P("patch"),
            P("member", "patch"),
            P("member", "patch"),
            P("patch"),
            P("patch"),
        ),
        out_specs=P(None, None, "patch", "member"),
        check_vma=False,
    )
```

profile of v0, /device:TPU:4, one launch (start us, length us, event | category | flops | bytes accessed | tf_op | source)
XLA Modules:
  0.0 233.5 jit_solution(6095585863299872821)
XLA Ops:
  0.1 0.8 convert_element_type.35
  0.8 0.7 broadcast_in_dim.30
  1.5 18.2 %all-to-all-start = ((bf16[32,6,256]{2,1,0:T(8,128)(2,1)}), bf16[32,6,256]{2,1,0:T(8,128)(2,1)S(1)}, u32[]{:S(2)}, u32[]{:S(2)}) async-start(bf16[32,6,256]{2,1,0:T(8,128)(2,1)} %broadcast_in_dim.30), calls=%async_computation | async-start | bytes 262144 | tf_op jit(solution)/shard_map/all_to_all | solution.py:18
  19.7 0.7 broadcast_multiply_fusion.6
  20.4 15.3 %all-to-all-done = bf16[32,6,256]{2,1,0:T(8,128)(2,1)S(1)} async-done(((bf16[32,6,256]{2,1,0:T(8,128)(2,1)}), bf16[32,6,256]{2,1,0:T(8,128)(2,1)S(1)}, u32[]{:S(2)}, u32[]{:S(2)}) %all-to-all-start) | async-done | bytes 98336 | tf_op jit(solution)/shard_map/all_to_all | solution.py:18
  35.7 3.7 %fusion.193 = (bf16[6,256]{1,0:T(8,128)(2,1)S(1)}, f32[6,256]{1,0:T(8,128)S(1)}, f32[6,256]{1,0:T(8,128)S(1)}) fusion(f32[6,256]{1,0:T(8,128)} %param.16, f32[256]{0:T(256)} %param.15, f32[256]{0:T(256)S(1)} %get-tuple-element.37, f32[256]{0:T(256)S(1)} %get-tuple-element.38, f32[6,256]{1,0:T(8,128)} %param.17, f32[256]{0:T(256)} %param.14, ...), kind=kOutput, calls=%fused_computation.288 | convolution fusion | flops 25279488 | bytes 4327424 | tf_op jit(solution)/shard_map/dot_general | solution.py:138
  39.4 20.4 %all_to_all.50 = bf16[32,6,256]{2,1,0:T(8,128)(2,1)S(1)} all-to-all(bf16[32,6,256]{2,1,0:T(8,128)(2,1)S(1)} %broadcast_in_dim.31), channel_id=1, replica_groups=mesh['member'=16,'patch'=32] {'patch'}, dimensions={0} | all-to-all | bytes 196608 | tf_op jit(solution)/shard_map/all_to_all | solution.py:18
  59.9 1.3 fusion.192
  61.2 20.4 %all_to_all.51 = bf16[32,6,256]{2,1,0:T(8,128)(2,1)S(1)} all-to-all(bf16[32,6,256]{2,1,0:T(8,128)(2,1)S(1)} %broadcast_in_dim.32), channel_id=1, replica_groups=mesh['member'=16,'patch'=32] {'patch'}, dimensions={0} | all-to-all | bytes 196608 | tf_op jit(solution)/shard_map/all_to_all | solution.py:18
  81.6 1.3 fusion.191
  82.9 20.4 %all_to_all.52 = bf16[32,6,256]{2,1,0:T(8,128)(2,1)S(1)} all-to-all(bf16[32,6,256]{2,1,0:T(8,128)(2,1)S(1)} %broadcast_in_dim.33), channel_id=1, replica_groups=mesh['member'=16,'patch'=32] {'patch'}, dimensions={0} | all-to-all | bytes 196608 | tf_op jit(solution)/shard_map/all_to_all | solution.py:18
  103.3 1.3 fusion.190
  104.6 20.4 %all_to_all.53 = bf16[32,6,256]{2,1,0:T(8,128)(2,1)S(1)} all-to-all(bf16[32,6,256]{2,1,0:T(8,128)(2,1)S(1)} %broadcast_in_dim.34), channel_id=1, replica_groups=mesh['member'=16,'patch'=32] {'patch'}, dimensions={0} | all-to-all | bytes 196608 | tf_op jit(solution)/shard_map/all_to_all | solution.py:18
  125.0 1.3 fusion.189
  126.3 0.6 broadcast_in_dim.35
  126.9 5.1 %all-to-all-start.5 = ((bf16[32,6,256]{2,1,0:T(8,128)(2,1)}), bf16[32,6,256]{2,1,0:T(8,128)(2,1)S(1)}, u32[]{:S(2)}, u32[]{:S(2)}) async-start(bf16[32,6,256]{2,1,0:T(8,128)(2,1)} %broadcast_in_dim.35), calls=%async_computation.5 | async-start | bytes 262144 | tf_op jit(solution)/shard_map/all_to_all | solution.py:18
  132.1 2.2 collective-permute-start.5
  134.4 6.0 %collective-permute-start.4 = (f32[2,8]{1,0:T(2,128)S(1)}, f32[2,8]{1,0:T(2,128)S(1)}, u32[]{:S(2)}, u32[]{:S(2)}) collective-permute-start(f32[2,8]{1,0:T(2,128)S(1)} %get-tuple-element.26), channel_id=1, source_target_pairs={{0,1},{1,2},{2,3},{3,4},{4,5},{5,6},{6,7},{7,8},{8,9},{9,10},{10,1... | collective-permute-start | bytes 200 | tf_op jit(solution)/shard_map/ppermute | solution.py:52
  140.4 7.1 %all-to-all-done.5 = bf16[32,6,256]{2,1,0:T(8,128)(2,1)S(1)} async-done(((bf16[32,6,256]{2,1,0:T(8,128)(2,1)}), bf16[32,6,256]{2,1,0:T(8,128)(2,1)S(1)}, u32[]{:S(2)}, u32[]{:S(2)}) %all-to-all-start.5) | async-done | bytes 98336 | tf_op jit(solution)/shard_map/all_to_all | solution.py:18
  147.5 3.5 %multiply_add_fusion = (f32[6,256]{1,0:T(8,128)S(1)}, f32[6,256]{1,0:T(8,128)S(1)}, f32[6,256]{1,0:T(8,128)S(1)}) fusion(f32[6,256]{1,0:T(8,128)S(1)} %get-tuple-element.14, f32[6,256]{1,0:T(8,128)S(1)} %get-tuple-element.33, f32[6,256]{1,0:T(8,128)S(1)} %get-tuple-element.32, f32[6,256]{1,0:T(8,128)S(1)} %get-tuple-element.31, ...), kind=kOutput, calls=%fused_computation.234 | convolution fusion | flops 25812480 | bytes 4385792 | tf_op jit(solution)/shard_map/dot_general | solution.py:138
  151.0 0.6 fusion.188
  151.6 0.7 broadcast_in_dim.36
  152.3 7.6 %all-to-all-start.6 = ((bf16[32,6,256]{2,1,0:T(8,128)(2,1)}), bf16[32,6,256]{2,1,0:T(8,128)(2,1)S(1)}, u32[]{:S(2)}, u32[]{:S(2)}) async-start(bf16[32,6,256]{2,1,0:T(8,128)(2,1)} %broadcast_in_dim.36), calls=%async_computation.6 | async-start | bytes 262144 | tf_op jit(solution)/shard_map/all_to_all | solution.py:18
  159.9 0.1 fusion.182
  160.2 14.2 %all-to-all-done.6 = bf16[32,6,256]{2,1,0:T(8,128)(2,1)S(1)} async-done(((bf16[32,6,256]{2,1,0:T(8,128)(2,1)}), bf16[32,6,256]{2,1,0:T(8,128)(2,1)S(1)}, u32[]{:S(2)}, u32[]{:S(2)}) %all-to-all-start.6) | async-done | bytes 98336 | tf_op jit(solution)/shard_map/all_to_all | solution.py:18
  174.4 3.5 %fusion.179 = f32[6,256]{1,0:T(8,128)S(1)} fusion(bf16[6,8192]{1,0:T(8,128)(2,1)S(1)} %bitcast.127, bf16[256,8192]{1,0:T(8,128)(2,1)} %param.10, f32[6,256]{1,0:T(8,128)S(1)} %get-tuple-element.8, f32[6,256]{1,0:T(8,128)S(1)} %get-tuple-element.34, f32[6,256]{1,0:T(8,128)S(1)} %get-tuple-element.33, f32[6,256]{1,0:T(8,128)S(1)} %get-tuple-element.32, ...), kind=kOutput, calls=%fused_computation.230 | convolution fusion | flops 25903104 | bytes 4385792 | tf_op jit(solution)/shard_map/dot_general | solution.py:138
  178.0 0.7 reshape.161
  178.8 5.4 %all-to-all-start.7 = ((f32[16,1,288]{2,1,0:T(1,128)}), f32[16,1,288]{2,1,0:T(1,128)S(1)}, u32[]{:S(2)}, u32[]{:S(2)}) async-start(f32[16,1,288]{2,1,0:T(1,128)} %reshape.161), calls=%async_computation.7 | async-start | bytes 49152 | tf_op jit(solution)/shard_map/all_to_all | solution.py:168
  184.2 0.1 select_multiply_fusion
  184.3 6.0 %all-to-all-done.7 = f32[16,1,288]{2,1,0:T(1,128)S(1)} async-done(((f32[16,1,288]{2,1,0:T(1,128)}), f32[16,1,288]{2,1,0:T(1,128)S(1)}, u32[]{:S(2)}, u32[]{:S(2)}) %all-to-all-start.7) | async-done | bytes 18464 | tf_op jit(solution)/shard_map/all_to_all | solution.py:168
  190.3 0.5 broadcast.390
  190.8 0.7 reduce.1
  191.5 0.1 reshape.162
  191.7 2.0 collective-permute-start
  193.8 5.6 %collective-permute-start.2 = (f32[96,8]{1,0:T(8,128)S(1)}, f32[96,8]{1,0:T(8,128)S(1)}, u32[]{:S(2)}, u32[]{:S(2)}) collective-permute-start(f32[96,8]{1,0:T(8,128)S(1)} %get-tuple-element.24), channel_id=1, source_target_pairs={{32,0},{64,32},{96,64},{128,96},{160,128},{192,160},{224,192},{256... | collective-permute-start | bytes 9224 | tf_op jit(solution)/shard_map/ppermute | solution.py:35
  199.4 2.9 %collective-permute-start.1 = (f32[96,8]{1,0:T(8,128)S(1)}, f32[96,8]{1,0:T(8,128)S(1)}, u32[]{:S(2)}, u32[]{:S(2)}) collective-permute-start(f32[96,8]{1,0:T(8,128)S(1)} %collective-permute-done), channel_id=1, source_target_pairs={{0,1},{1,2},{2,3},{3,4},{4,5},{5,6},{6,7},{7,8},{8,9},{9,10},{10,1... | collective-permute-start | bytes 9224 | tf_op jit(solution)/shard_map/ppermute | solution.py:41
  202.6 0.1 copy.30
  202.7 4.6 %collective-permute-start.3 = (f32[96,8]{1,0:T(8,128)S(1)}, f32[96,8]{1,0:T(8,128)S(1)}, u32[]{:S(2)}, u32[]{:S(2)}) collective-permute-start(f32[96,8]{1,0:T(8,128)S(1)} %collective-permute-done.2), channel_id=1, source_target_pairs={{1,0},{2,1},{3,2},{4,3},{5,4},{6,5},{7,6},{8,7},{9,8},{10,9},{11,1... | collective-permute-start | bytes 9224 | tf_op jit(solution)/shard_map/ppermute | solution.py:41
  207.3 0.2 collective-permute-done.1
  207.5 3.6 %collective-permute-done.3 = f32[96,8]{1,0:T(8,128)S(1)} collective-permute-done((f32[96,8]{1,0:T(8,128)S(1)}, f32[96,8]{1,0:T(8,128)S(1)}, u32[]{:S(2)}, u32[]{:S(2)}) %collective-permute-start.3) | collective-permute-done | bytes 3104 | tf_op jit(solution)/shard_map/ppermute | solution.py:41
  211.2 0.1 fusion.39
  211.4 0.3 convolution_bitcast_fusion.2
  211.7 1.6 select_reduce_fusion
  213.4 0.9 fusion.5
  214.3 1.0 fusion.31
  215.3 0.8 fusion.21
  216.1 0.9 fusion.4
  217.0 0.9 fusion.197
  217.9 0.9 fusion.196
  218.8 0.9 fusion.3
  219.8 0.9 fusion.199
  220.7 0.9 fusion.198
  221.6 0.9 fusion.2
  222.5 1.1 fusion.201
  223.7 0.9 fusion.200
  224.6 0.9 fusion.1
  225.5 0.9 fusion.202
  226.4 0.9 fusion.203
  227.4 0.9 fusion
  228.3 0.9 fusion.204
  229.2 1.3 convolution_bitcast_fusion.1
  230.5 1.3 fusion.205
  231.9 1.0 fusion.7
  232.9 0.6 copy.31
  (59 shorter events, 1.1 us)
Async XLA Ops:
  0.0 59.8 %copy-start.2 = (f32[6,256]{1,0:T(8,128)S(1)}, f32[6,256]{1,0:T(8,128)}, u32[]{:S(2)}) copy-start(f32[6,256]{1,0:T(8,128)} %param.16) | copy-start | bytes 18436
  0.0 59.8 %copy-start.3 = (f32[256]{0:T(256)S(1)}, f32[256]{0:T(256)}, u32[]{:S(2)}) copy-start(f32[256]{0:T(256)} %param.15) | copy-start | bytes 3076
  0.0 59.8 %copy-start.4 = (f32[256]{0:T(256)S(1)}, f32[256]{0:T(256)}, u32[]{:S(2)}) copy-start(f32[256]{0:T(256)} %param.14) | copy-start | bytes 3076
  0.0 59.8 %copy-start.1 = (f32[6,256]{1,0:T(8,128)S(1)}, f32[6,256]{1,0:T(8,128)}, u32[]{:S(2)}) copy-start(f32[6,256]{1,0:T(8,128)} %param.17) | copy-start | bytes 18436
  0.0 59.8 %copy-start.7 = (f32[256]{0:T(256)S(1)}, f32[256]{0:T(256)}, u32[]{:S(2)}) copy-start(f32[256]{0:T(256)} %param.13) | copy-start | bytes 3076
  0.0 59.8 %copy-start.6 = (f32[256]{0:T(256)S(1)}, f32[256]{0:T(256)}, u32[]{:S(2)}) copy-start(f32[256]{0:T(256)} %param.12) | copy-start | bytes 3076
  0.0 59.8 %copy-start.5 = (f32[256]{0:T(256)S(1)}, f32[256]{0:T(256)}, u32[]{:S(2)}) copy-start(f32[256]{0:T(256)} %param.11) | copy-start | bytes 3076
  1.5 34.2 %all-to-all-start = ((bf16[32,6,256]{2,1,0:T(8,128)(2,1)}), bf16[32,6,256]{2,1,0:T(8,128)(2,1)S(1)}, u32[]{:S(2)}, u32[]{:S(2)}) async-start(bf16[32,6,256]{2,1,0:T(8,128)(2,1)} %broadcast_in_dim.30), calls=%async_computation | async-start | bytes 262144 | tf_op jit(solution)/shard_map/all_to_all | solution.py:18
  35.7 24.2 %copy-start = (bf16[256,8192]{1,0:T(8,128)(2,1)S(1)}, bf16[256,8192]{1,0:T(8,128)(2,1)}, u32[]{:S(2)}) copy-start(bf16[256,8192]{1,0:T(8,128)(2,1)} %param.10) | copy-start | bytes 12582916
  103.3 28.7 %copy-start.8 = (f32[256]{0:T(256)S(1)}, f32[256]{0:T(256)}, u32[]{:S(2)}) copy-start(f32[256]{0:T(256)} %param.19) | copy-start | bytes 3076
  103.3 28.8 %copy-start.9 = (f32[256]{0:T(256)S(1)}, f32[256]{0:T(256)}, u32[]{:S(2)}) copy-start(f32[256]{0:T(256)} %param.18) | copy-start | bytes 3076
  126.9 20.6 %all-to-all-start.5 = ((bf16[32,6,256]{2,1,0:T(8,128)(2,1)}), bf16[32,6,256]{2,1,0:T(8,128)(2,1)S(1)}, u32[]{:S(2)}, u32[]{:S(2)}) async-start(bf16[32,6,256]{2,1,0:T(8,128)(2,1)} %broadcast_in_dim.35), calls=%async_computation.5 | async-start | bytes 262144 | tf_op jit(solution)/shard_map/all_to_all | solution.py:18
  132.1 27.8 %collective-permute-start.5 = (f32[2,8]{1,0:T(2,128)S(1)}, f32[2,8]{1,0:T(2,128)S(1)}, u32[]{:S(2)}, u32[]{:S(2)}) collective-permute-start(f32[2,8]{1,0:T(2,128)S(1)} %get-tuple-element.25), channel_id=1, source_target_pairs={{1,0},{2,1},{3,2},{4,3},{5,4},{6,5},{7,6},{8,7},{9,8},{10,9},{11,1... | collective-permute-start | bytes 200 | tf_op jit(solution)/shard_map/ppermute | solution.py:54
  134.4 25.5 %collective-permute-start.4 = (f32[2,8]{1,0:T(2,128)S(1)}, f32[2,8]{1,0:T(2,128)S(1)}, u32[]{:S(2)}, u32[]{:S(2)}) collective-permute-start(f32[2,8]{1,0:T(2,128)S(1)} %get-tuple-element.26), channel_id=1, source_target_pairs={{0,1},{1,2},{2,3},{3,4},{4,5},{5,6},{6,7},{7,8},{8,9},{9,10},{10,1... | collective-permute-start | bytes 200 | tf_op jit(solution)/shard_map/ppermute | solution.py:52
  152.3 22.1 %all-to-all-start.6 = ((bf16[32,6,256]{2,1,0:T(8,128)(2,1)}), bf16[32,6,256]{2,1,0:T(8,128)(2,1)S(1)}, u32[]{:S(2)}, u32[]{:S(2)}) async-start(bf16[32,6,256]{2,1,0:T(8,128)(2,1)} %broadcast_in_dim.36), calls=%async_computation.6 | async-start | bytes 262144 | tf_op jit(solution)/shard_map/all_to_all | solution.py:18
  178.8 11.5 %all-to-all-start.7 = ((f32[16,1,288]{2,1,0:T(1,128)}), f32[16,1,288]{2,1,0:T(1,128)S(1)}, u32[]{:S(2)}, u32[]{:S(2)}) async-start(f32[16,1,288]{2,1,0:T(1,128)} %reshape.161), calls=%async_computation.7 | async-start | bytes 49152 | tf_op jit(solution)/shard_map/all_to_all | solution.py:168
  191.7 7.7 %collective-permute-start = (f32[96,8]{1,0:T(8,128)S(1)}, f32[96,8]{1,0:T(8,128)S(1)}, u32[]{:S(2)}, u32[]{:S(2)}) collective-permute-start(f32[96,8]{1,0:T(8,128)S(1)} %get-tuple-element.23), channel_id=1, source_target_pairs={{480,0},{0,32},{32,64},{64,96},{96,128},{128,160},{160,192},{192,2... | collective-permute-start | bytes 9224 | tf_op jit(solution)/shard_map/ppermute | solution.py:35
  193.8 8.9 %collective-permute-start.2 = (f32[96,8]{1,0:T(8,128)S(1)}, f32[96,8]{1,0:T(8,128)S(1)}, u32[]{:S(2)}, u32[]{:S(2)}) collective-permute-start(f32[96,8]{1,0:T(8,128)S(1)} %get-tuple-element.24), channel_id=1, source_target_pairs={{32,0},{64,32},{96,64},{128,96},{160,128},{192,160},{224,192},{256... | collective-permute-start | bytes 9224 | tf_op jit(solution)/shard_map/ppermute | solution.py:35
  199.4 8.0 %collective-permute-start.1 = (f32[96,8]{1,0:T(8,128)S(1)}, f32[96,8]{1,0:T(8,128)S(1)}, u32[]{:S(2)}, u32[]{:S(2)}) collective-permute-start(f32[96,8]{1,0:T(8,128)S(1)} %collective-permute-done), channel_id=1, source_target_pairs={{0,1},{1,2},{2,3},{3,4},{4,5},{5,6},{6,7},{7,8},{8,9},{9,10},{10,1... | collective-permute-start | bytes 9224 | tf_op jit(solution)/shard_map/ppermute | solution.py:41
  202.7 8.4 %collective-permute-start.3 = (f32[96,8]{1,0:T(8,128)S(1)}, f32[96,8]{1,0:T(8,128)S(1)}, u32[]{:S(2)}, u32[]{:S(2)}) collective-permute-start(f32[96,8]{1,0:T(8,128)S(1)} %collective-permute-done.2), channel_id=1, source_target_pairs={{1,0},{2,1},{3,2},{4,3},{5,4},{6,5},{7,6},{8,7},{9,8},{10,9},{11,1... | collective-permute-start | bytes 9224 | tf_op jit(solution)/shard_map/ppermute | solution.py:41
where the time goes:
time: 234 us
  blocking collectives  81.6 us (35%)
  starting transfers between devices  59.7 us (26%)
  waiting for transfers between devices  46.3 us (20%)
  matrix products  37 us (16%)
  local copies, waits for them, and re-layouts  4.79 us (2%)
  other arithmetic  3.42 us (1%)
    all_to_all x4, blocking collectives, from_everyone(): return lax.all_to_all(copies, axis, split_axis=0, concat_axis=0, tiled=True)  81.6 us
    all_to_all x3, waiting for transfers between devices, from_everyone(): return lax.all_to_all(copies, axis, split_axis=0, concat_axis=0, tiled=True)  36.6 us
    all_to_all x3, starting transfers between devices, from_everyone(): return lax.all_to_all(copies, axis, split_axis=0, concat_axis=0, tiled=True)  30.9 us
    dot_general x7, matrix products, coupling(): lax.dot_general(gather_directly(rounded, 'patch', 1), kernel_rows, (((1,)...  15.7 us
    ppermute x2, starting transfers between devices, shifted(): return lax.ppermute(block, axis, route)  7.66 us
    ppermute x2, starting transfers between devices, shifted_2(): lax.ppermute(value, axis, [(source, source + steps) for source in range(f...  7.53 us
    all_to_all x1, waiting for transfers between devices, body(): lax.all_to_all(stacked.reshape(3, members, groups, sub_block), 'member',...  6.01 us
    ppermute x1, starting transfers between devices, padded(): lax.ppermute(tail, axis, [(i, (i + 1) % count) for i in range(ends)])  5.99 us
  transfers between devices with their start and end apart: 10, of which 6 were waited for; matrix products, arithmetic and copies ran while one was open for 3% of the time, Pallas kernels for 0%

commit v1 on v0

v1 whole, which is shorter than its diff:
```python
import jax
import jax.numpy as jnp
from jax import lax
from jax.experimental import pallas as pl
from jax.experimental.pallas import tpu as pltpu
from jax.sharding import PartitionSpec as P

STEPS = 2
NEWTON = 4
NS_ITERS = 6
MARGIN = 8
F32, BF16 = jnp.float32, jnp.bfloat16


time_step = 0.25
plate_rate = 1.0

def from_everyone(x, axis):
    copies = jnp.broadcast_to(x, (lax.axis_size(axis), *x.shape))
    return lax.all_to_all(copies, axis, split_axis=0, concat_axis=0, tiled=True)


def joined_along(blocks, dim):
    blocks = jnp.moveaxis(blocks, 0, dim)
    dims = blocks.shape
    return blocks.reshape(*dims[:dim], dims[dim] * dims[dim + 1], *dims[dim + 2 :])


def gather_directly(x, axis, dim):
    blocks = from_everyone(x, axis)
    return joined_along(blocks, dim)


def inverse_sinh(value):
    magnitude = jnp.abs(value)
    result = jnp.log(magnitude + jnp.sqrt(magnitude * magnitude + 1.0))
    return jnp.where(value < 0, -result, result)


def slip_rate(stress, state_log, guess, friction_rate, damping):
    factor = 0.5 * jnp.exp(state_log / friction_rate)
    velocity = guess
    for _ in range(NEWTON):
        scaled = factor * velocity
        residual = friction_rate * inverse_sinh(scaled) + damping * velocity - stress
        derivative = friction_rate * factor / jnp.sqrt(1.0 + scaled * scaled) + damping
        velocity = velocity - residual / derivative
    return velocity


def split(x):
    high = x.astype(BF16)
    return high, (x - high.astype(F32)).astype(BF16)


def product(rows, blocks):
    row_high, row_low = split(rows)
    block_high, block_low = blocks
    count = rows.shape[0]
    both = jnp.dot(jnp.concatenate([row_high, row_low], 0), block_high, preferred_element_type=F32)
    rest = jnp.dot(row_high, block_low, preferred_element_type=F32)
    return both[:count] + (both[count:] + rest)


def product_nt(a, b):
    dims = (((1,), (1,)), ((), ()))
    ah, al = split(a)
    bh, bl = split(b)
    count = a.shape[0]
    both = lax.dot_general(jnp.concatenate([ah, al], 0), bh, dims, preferred_element_type=F32)
    rest = lax.dot_general(ah, bl, dims, preferred_element_type=F32)
    return both[:count] + (both[count:] + rest)


def tables(obs_window, sub_block, per_group):
    window = sub_block + 2 * MARGIN
    distance = jnp.abs(
        jnp.arange(sub_block, dtype=jnp.int32)[:, None]
        + MARGIN
        - jnp.arange(window, dtype=jnp.int32)[None, :]
    ).astype(F32)
    taper = jnp.where(distance <= MARGIN, jnp.exp(-0.5 * (distance / MARGIN) ** 2), 0.0)
    weights = taper * obs_window[1][None, :]
    groups = sub_block // per_group
    lanes = per_group * window
    w = weights.reshape(groups, per_group, window)
    root = jnp.sqrt(w)
    across = jnp.broadcast_to(
        jnp.transpose(root, (0, 2, 1))[:, :, :, None], (groups, window, per_group, window)
    ).reshape(groups, window, lanes)
    along = root.reshape(groups, 1, lanes)
    obs = jnp.tile(obs_window[0], per_group)[None, None, :]
    obs = jnp.broadcast_to(obs, (groups, 1, lanes))
    filler = jnp.zeros((groups, 6, lanes), F32)
    return jnp.concatenate([across * along, across * across, along, obs, filler], axis=1)


def analysis_kernel(got_ref, table_ref, out_ref, all_ref):
    groups_m, each, width = got_ref.shape
    ensemble = groups_m * each
    sub_block = (width - 2 * MARGIN) // 3
    window = sub_block + 2 * MARGIN
    halves, _, lanes = table_ref.shape
    count = lanes // window
    for g in range(groups_m):
        all_ref[g * each : (g + 1) * each, :] = got_ref[g]
    values = all_ref[...]
    mean = jnp.mean(values, axis=0, keepdims=True)
    anomaly = values - mean
    y = anomaly[:, 2 * sub_block :]
    y_tiled = jnp.concatenate([y] * count, axis=1)
    mean_tiled = jnp.concatenate([mean[:, 2 * sub_block :]] * count, axis=1)
    starts = (0, sub_block, 2 * sub_block + MARGIN)
    pieces = [y]
    for h in range(halves):
        pieces += [anomaly[:, s + h * count : s + (h + 1) * count] for s in starts]
    turned = jnp.transpose(jnp.concatenate(pieces, axis=1))
    grams = product(turned, split(y_tiled))
    gram = grams[:window]
    row = lax.broadcasted_iota(jnp.int32, (window, lanes), 0)
    lane = lax.broadcasted_iota(jnp.int32, (window, lanes), 1)
    eye = jnp.where(row == lane % window, 1.0, 0.0).astype(F32)
    block_row = lax.broadcasted_iota(jnp.int32, (lanes, lanes), 0) // window
    block_lane = lax.broadcasted_iota(jnp.int32, (lanes, lanes), 1) // window
    on_block = block_row == block_lane
    diag = jnp.sum(
        jnp.where(
            lax.broadcasted_iota(jnp.int32, (window, window), 0)
            == lax.broadcasted_iota(jnp.int32, (window, window), 1),
            gram[:, :window],
            0.0,
        ),
        axis=1,
        keepdims=True,
    )
    vrows = 3 * count
    own = lax.broadcasted_iota(jnp.int32, (vrows, lanes), 0) % count == (
        lax.broadcasted_iota(jnp.int32, (vrows, lanes), 1) // window
    )
    first = own & (lax.broadcasted_iota(jnp.int32, (vrows, lanes), 1) % window == 0)

    def blocks(x):
        return tuple(
            jnp.where(on_block, jnp.concatenate([part] * count, 0), jnp.zeros((), BF16))
            for part in split(x)
        )

    free = ensemble - 1.0
    state = []
    for h in range(halves):
        table = table_ref[h]
        cross = gram * table[:window]
        scale = free + jnp.sum(diag * table[window : 2 * window], axis=0, keepdims=True)
        inv = 1.0 / scale
        base = cross * inv
        root = table[2 * window : 2 * window + 1]
        obs = table[2 * window + 1 : 2 * window + 2]
        q = jnp.where(own, grams[window + h * vrows : window + (h + 1) * vrows] * root, 0.0)
        drive = (obs - mean_tiled) * root
        r = free * inv
        state.append(dict(base=base, inv=inv, root=root, q=q, drive=drive, r=r))
    for s in state:
        base, r = s["base"], s["r"]
        full_r = r * eye + base
        g = 1.5 - 0.5 * r
        gain = g * eye - 0.5 * base
        s["S"] = gain - 0.5 * r * eye
        s["T"] = -0.5 * eye
        s["r"], s["z"] = r * g, g
        s["fz"] = gain
        s["fr"] = product(full_r, blocks(gain))
    for it in range(1, NS_ITERS):
        last = it == NS_ITERS - 1
        for s in state:
            rb = blocks(s["fr"])
            if it == 1:
                zr, tr = product(s["fz"], rb), -0.5 * s["fr"]
            else:
                both = product(jnp.concatenate([s["fz"], s["T"]], 0), rb)
                zr, tr = both[:window], both[window:]
            s["G"] = 1.5 * eye - 0.5 * zr
            s["H"] = -0.5 * (s["z"] * s["S"] + tr)
        for s in state:
            g = 1.5 - 0.5 * s["z"] * s["r"]
            s["T"] = g * s["T"] + product(s["H"], blocks(s["fz"]))
            rows = [s["fz"]] if last else [s["fz"], s["fr"], s["S"]]
            both = product(jnp.concatenate(rows, 0), blocks(s["G"]))
            s["fz"] = both[:window]
            if not last:
                s["fr"] = both[window : 2 * window]
                s["S"] = both[2 * window :] + s["r"] * s["H"]
            s["r"], s["z"] = s["r"] * g, s["z"] * g
    ones = jnp.ones((ensemble, lanes), F32)
    results = []
    for h, s in enumerate(state):
        u = product(s["q"], blocks(s["T"])) * (s["root"] * s["inv"])
        pad = jnp.zeros((7, lanes), F32)
        rows = jnp.concatenate([s["q"], s["drive"], pad], 0)
        through = product(rows, blocks(s["fz"]))
        factor = jnp.sqrt(free * s["inv"])
        shift = through[:vrows] * (through[vrows : vrows + 1] * s["inv"])
        right = jnp.concatenate([u * factor, shift], axis=1)
        left = jnp.concatenate([y_tiled, ones], axis=1)
        part = product_nt(left, right)
        keep = jnp.where(first, s["z"] * factor, 0.0)
        weight = product_nt(jnp.ones((8, lanes), F32), keep)[:1]
        for v in range(3):
            c = slice(starts[v] + h * count, starts[v] + (h + 1) * count)
            d = slice(v * count, (v + 1) * count)
            out_ref[v, :, h * count : (h + 1) * count] = (
                mean[:, c] + anomaly[:, c] * weight[:, d] + part[:, d]
            )


def analyse(received, obs_window):
    groups_m, each, width = received.shape
    ensemble = groups_m * each
    sub_block = (width - 2 * MARGIN) // 3
    per_group = 256 // (sub_block + 2 * MARGIN)
    table = tables(obs_window, sub_block, per_group)
    return pl.pallas_call(
        analysis_kernel,
        out_shape=jax.ShapeDtypeStruct((3, ensemble, sub_block), F32),
        in_specs=[pl.BlockSpec(memory_space=pltpu.VMEM)] * 2,
        out_specs=pl.BlockSpec(memory_space=pltpu.VMEM),
        scratch_shapes=[pltpu.VMEM((ensemble, width), F32)],
        compiler_params=pltpu.CompilerParams(vmem_limit_bytes=32 * 1024 * 1024),
    )(received, table)


def from_neighbours(block, dim):
    count = lax.axis_size("patch")
    size = block.shape[dim]
    tail = lax.slice_in_dim(block, size - MARGIN, size, axis=dim)
    front = lax.slice_in_dim(block, 0, MARGIN, axis=dim)
    before = lax.ppermute(tail, "patch", [(i, i + 1) for i in range(count - 1)])
    after = lax.ppermute(front, "patch", [(i + 1, i) for i in range(count - 1)])
    return jnp.concatenate([before, after], axis=dim)


def body(
    kernel_rows,
    row_scale,
    self_stiffness,
    base_stress,
    friction_rate,
    damping,
    deficit_start,
    state_start,
    obs_rate,
    obs_precision,
):
    groups = lax.axis_size("member")
    own_rows = kernel_rows.shape[0]
    members = deficit_start.shape[0]
    sub_block = own_rows // groups
    params = jnp.stack(
        [row_scale, self_stiffness, base_stress, friction_rate, damping, obs_rate, obs_precision]
    )
    rim_rows = from_neighbours(kernel_rows, 0)
    rim_params = from_neighbours(params, 1)

    def summed(gathered, rows):
        return lax.dot_general(
            gathered, rows, (((1,), (1,)), ((), ())), preferred_element_type=jnp.float32
        )

    def gather(deficit):
        return gather_directly(deficit.astype(jnp.bfloat16), "patch", 1)

    def coupling(deficit):
        total = summed(gather(deficit), kernel_rows)
        return base_stress + self_stiffness * deficit + row_scale * total

    def tendency(deficit, state_log, guess):
        velocity = slip_rate(coupling(deficit), state_log, guess, friction_rate, damping)
        return (plate_rate - velocity, jnp.exp(-state_log) - jnp.abs(velocity), velocity)

    deficit = deficit_start
    state_log = state_start
    velocity = jnp.zeros_like(deficit_start)
    for _ in range(STEPS):
        deficit_zero, state_zero = (deficit, state_log)
        change, state_change, velocity = tendency(deficit_zero, state_zero, velocity)
        deficit_one = deficit_zero + time_step * change
        state_one = state_zero + time_step * state_change
        change, state_change, velocity = tendency(deficit_one, state_one, velocity)
        deficit_two = 0.75 * deficit_zero + 0.25 * (deficit_one + time_step * change)
        state_two = 0.75 * state_zero + 0.25 * (state_one + time_step * state_change)
        change, state_change, velocity = tendency(deficit_two, state_two, velocity)
        deficit = deficit_zero / 3.0 + 2.0 / 3.0 * (deficit_two + time_step * change)
        state_log = state_zero / 3.0 + 2.0 / 3.0 * (state_two + time_step * state_change)
    gathered = gather(deficit)
    rim = from_neighbours(jnp.stack([deficit, state_log, velocity]), 2)
    rim_scale, rim_stiffness, rim_base, rim_friction, rim_damping = rim_params[:5]
    stress = base_stress + self_stiffness * deficit + row_scale * summed(gathered, kernel_rows)
    forecast = slip_rate(stress, state_log, velocity, friction_rate, damping)
    rim_stress = rim_base + rim_stiffness * rim[0] + rim_scale * summed(gathered, rim_rows)
    there = rim_damping > 0
    rim_forecast = slip_rate(
        rim_stress,
        rim[1],
        rim[2],
        jnp.where(there, rim_friction, 1.0),
        jnp.where(there, rim_damping, 1.0),
    )
    rim_forecast = jnp.where(there, rim_forecast, 0.0)
    wide = jnp.concatenate([rim_forecast[:, :MARGIN], forecast, rim_forecast[:, MARGIN:]], axis=1)
    parts = [
        x.reshape(members, groups, sub_block)
        for x in (deficit, state_log, wide[:, :own_rows], wide[:, 2 * MARGIN :])
    ]
    sent = jnp.transpose(jnp.concatenate(parts, axis=2), (1, 0, 2))
    received = lax.all_to_all(sent, "member", split_axis=0, concat_axis=0, tiled=True)
    group_index = lax.axis_index("member")
    observed = jnp.concatenate(
        [rim_params[5:, :MARGIN], params[5:], rim_params[5:, MARGIN:]], axis=1
    )
    obs_window = lax.dynamic_slice_in_dim(
        observed, group_index * sub_block, sub_block + 2 * MARGIN, 1
    )
    analysis = analyse(received, obs_window)
    return analysis[:, :, None, :]


def solution(mesh):
    return jax.shard_map(
        body,
        mesh=mesh,
        in_specs=(
            P("patch", None),
            P("patch"),
            P("patch"),
            P("patch"),
            P("patch"),
            P("patch"),
            P("member", "patch"),
            P("member", "patch"),
            P("patch"),
            P("patch"),
        ),
        out_specs=P(None, None, "patch", "member"),
        check_vma=False,
    )
```

time: 234 us -> 212 us (0.906)
  the two profiles are of different devices: /device:TPU:4 before, /device:TPU:1 now
where the time goes in v1:
time: 212 us; the launch traced here: 211 us
  starting transfers between devices  85 us (40%)
  waiting for transfers between devices  83.9 us (40%)
  matrix products  24.6 us (12%)
  local copies, waits for them, and re-layouts  9.8 us (5%)
  Pallas kernels  3.73 us (2%)
  other arithmetic  3.3 us (2%)
    all_to_all x7, waiting for transfers between devices, from_everyone(): return lax.all_to_all(copies, axis, split_axis=0, concat_axis=0, tiled=True)  78.3 us
    all_to_all x7, starting transfers between devices, from_everyone(): return lax.all_to_all(copies, axis, split_axis=0, concat_axis=0, tiled=True)  50.3 us
    dot_general x8, matrix products, summed(): lax.dot_general(gathered, rows, (((1,), (1,)), ((), ())), preferred_eleme...  24.6 us
    ppermute x3, starting transfers between devices, from_neighbours(): before = lax.ppermute(tail, 'patch', [(i, i + 1) for i in range(count - 1)])  16.7 us
    all_to_all x1, starting transfers between devices, body(): lax.all_to_all(sent, 'member', split_axis=0, concat_axis=0, tiled=True)  14.1 us
    all_to_all x1, waiting for transfers between devices, body(): lax.all_to_all(sent, 'member', split_axis=0, concat_axis=0, tiled=True)  5.64 us
    broadcast_in_dim x7, local copies, waits for them, and re-layouts, from_everyone(): copies = jnp.broadcast_to(x, (lax.axis_size(axis), *x.shape))  4.57 us
  transfers between devices with their start and end apart: 14, of which 8 were waited for; matrix products, arithmetic and copies ran while one was open for 16% of the time, Pallas kernels for 0%

profile of v1, /device:TPU:1, one launch (start us, length us, event | category | flops | bytes accessed | tf_op | source)
XLA Modules:
  0.0 210.9 jit_solution(4912923337905953719)
XLA Ops:
  0.1 0.8 convert_element_type.38
  0.8 0.7 broadcast_in_dim.49
  1.5 18.5 %all-to-all-start = ((bf16[32,6,256]{2,1,0:T(8,128)(2,1)}), bf16[32,6,256]{2,1,0:T(8,128)(2,1)S(1)}, u32[]{:S(2)}, u32[]{:S(2)}) async-start(bf16[32,6,256]{2,1,0:T(8,128)(2,1)} %broadcast_in_dim.49), calls=%async_computation | async-start | bytes 262144 | tf_op jit(solution)/shard_map/all_to_all | solution.py:20
  20.0 0.8 stack.30
  20.8 1.3 collective-permute-start.1
  22.1 5.5 %collective-permute-start = (f32[7,8]{1,0:T(8,128)S(1)}, f32[7,8]{1,0:T(8,128)S(1)}, u32[]{:S(2)}, u32[]{:S(2)}) collective-permute-start(f32[7,8]{1,0:T(8,128)S(1)} %get-tuple-element.34), channel_id=1, source_target_pairs={{0,1},{1,2},{2,3},{3,4},{4,5},{5,6},{6,7},{7,8},{8,9},{9,10},{10,1... | collective-permute-start | bytes 680 | tf_op jit(solution)/shard_map/ppermute | solution.py:236
  27.6 0.7 broadcast_multiply_fusion.8
  28.3 6.4 %all-to-all-done = bf16[32,6,256]{2,1,0:T(8,128)(2,1)S(1)} async-done(((bf16[32,6,256]{2,1,0:T(8,128)(2,1)}), bf16[32,6,256]{2,1,0:T(8,128)(2,1)S(1)}, u32[]{:S(2)}, u32[]{:S(2)}) %all-to-all-start) | async-done | bytes 98336 | tf_op jit(solution)/shard_map/all_to_all | solution.py:20
  34.7 3.5 %fusion.201 = (bf16[6,256]{1,0:T(8,128)(2,1)S(1)}, f32[6,256]{1,0:T(8,128)S(1)}, f32[6,256]{1,0:T(8,128)S(1)}) fusion(f32[6,256]{1,0:T(8,128)} %param.16, f32[256]{0:T(256)} %param.15, f32[256]{0:T(256)S(1)} %get-tuple-element.50, f32[256]{0:T(256)S(1)} %get-tuple-element.51, f32[6,256]{1,0:T(8,128)} %param.17, f32[256]{0:T(256)} %param.14, ...), kind=kOutput, calls=%fused_computation.296 | convolution fusion | flops 25279488 | bytes 4327424 | tf_op jit(solution)/shard_map/dot_general | solution.py:264
  38.3 0.7 broadcast_in_dim.50
  38.9 8.5 %all-to-all-start.1 = ((bf16[32,6,256]{2,1,0:T(8,128)(2,1)}), bf16[32,6,256]{2,1,0:T(8,128)(2,1)S(1)}, u32[]{:S(2)}, u32[]{:S(2)}) async-start(bf16[32,6,256]{2,1,0:T(8,128)(2,1)} %broadcast_in_dim.50), calls=%async_computation.1 | async-start | bytes 262144 | tf_op jit(solution)/shard_map/all_to_all | solution.py:20
  47.5 1.0 fusion.202
  48.5 1.3 collective-permute-start.5
  49.8 5.5 %collective-permute-start.4 = (bf16[8,8192]{1,0:T(8,128)(2,1)S(1)}, bf16[8,8192]{1,0:T(8,128)(2,1)S(1)}, u32[]{:S(2)}, u32[]{:S(2)}) collective-permute-start(bf16[8,8192]{1,0:T(8,128)(2,1)S(1)} %get-tuple-element.24), channel_id=1, source_target_pairs={{0,1},{1,2},{2,3},{3,4},{4,5},{5,6},{6,7},{7,8},{8,9},{9,10},{10,1... | collective-permute-start | bytes 393224 | tf_op jit(solution)/shard_map/ppermute | solution.py:236
  55.3 7.0 %all-to-all-done.1 = bf16[32,6,256]{2,1,0:T(8,128)(2,1)S(1)} async-done(((bf16[32,6,256]{2,1,0:T(8,128)(2,1)}), bf16[32,6,256]{2,1,0:T(8,128)(2,1)S(1)}, u32[]{:S(2)}, u32[]{:S(2)}) %all-to-all-start.1) | async-done | bytes 98336 | tf_op jit(solution)/shard_map/all_to_all | solution.py:20
  62.3 3.5 %fusion.200 = (bf16[6,256]{1,0:T(8,128)(2,1)S(1)}, f32[6,256]{1,0:T(8,128)S(1)}, f32[6,256]{1,0:T(8,128)S(1)}, f32[6,256]{1,0:T(8,128)S(1)}) fusion(f32[6,256]{1,0:T(8,128)S(1)} %get-tuple-element.23, f32[6,256]{1,0:T(8,128)S(1)} %get-tuple-element.44, f32[256]{0:T(256)S(1)} %copy-done.2, f32[256]{0:T(256)S(1)} %get-tuple-element.50, ...), kind=kOutput, calls=%fused_computation.295 | convolution fusion | flops 25394688 | bytes 4345856 | tf_op jit(solution)/shard_map/dot_general | solution.py:264
  65.8 0.7 broadcast_in_dim.51
  66.4 8.0 %all-to-all-start.2 = ((bf16[32,6,256]{2,1,0:T(8,128)(2,1)}), bf16[32,6,256]{2,1,0:T(8,128)(2,1)S(1)}, u32[]{:S(2)}, u32[]{:S(2)}) async-start(bf16[32,6,256]{2,1,0:T(8,128)(2,1)} %broadcast_in_dim.51), calls=%async_computation.2 | async-start | bytes 262144 | tf_op jit(solution)/shard_map/all_to_all | solution.py:20
  74.5 0.1 sub.355
  74.6 0.1 sub.360
  74.7 0.1 sub.357
  74.8 0.1 fusion.188
  74.9 14.3 %all-to-all-done.2 = bf16[32,6,256]{2,1,0:T(8,128)(2,1)S(1)} async-done(((bf16[32,6,256]{2,1,0:T(8,128)(2,1)}), bf16[32,6,256]{2,1,0:T(8,128)(2,1)S(1)}, u32[]{:S(2)}, u32[]{:S(2)}) %all-to-all-start.2) | async-done | bytes 98336 | tf_op jit(solution)/shard_map/all_to_all | solution.py:20
  89.2 3.5 %fusion.199 = (bf16[6,256]{1,0:T(8,128)(2,1)S(1)}, f32[6,256]{1,0:T(8,128)S(1)}, f32[6,256]{1,0:T(8,128)S(1)}, f32[6,256]{1,0:T(8,128)S(1)}) fusion(f32[6,256]{1,0:T(8,128)S(1)} %get-tuple-element.20, f32[6,256]{1,0:T(8,128)S(1)} %get-tuple-element.45, f32[6,256]{1,0:T(8,128)S(1)} %get-tuple-element.21, f32[6,256]{1,0:T(8,128)S(1)} %get-tuple-element.44, ...), kind=kOutput, calls=%fused_computation.294 | convolution fusion | flops 25502208 | bytes 4358144 | tf_op jit(solution)/shard_map/dot_general | solution.py:264
  92.6 0.7 broadcast_in_dim.52
  93.3 3.8 %all-to-all-start.3 = ((bf16[32,6,256]{2,1,0:T(8,128)(2,1)}), bf16[32,6,256]{2,1,0:T(8,128)(2,1)S(1)}, u32[]{:S(2)}, u32[]{:S(2)}) async-start(bf16[32,6,256]{2,1,0:T(8,128)(2,1)} %broadcast_in_dim.52), calls=%async_computation.3 | async-start | bytes 262144 | tf_op jit(solution)/shard_map/all_to_all | solution.py:20
  97.1 0.1 multiply_sqrt_fusion
  97.2 0.1 broadcast_in_dim.64
  97.3 0.1 reshape.171
  97.5 0.1 mul.1269
  97.6 0.1 pad_maximum_fusion.4
  97.7 14.3 %all-to-all-done.3 = bf16[32,6,256]{2,1,0:T(8,128)(2,1)S(1)} async-done(((bf16[32,6,256]{2,1,0:T(8,128)(2,1)}), bf16[32,6,256]{2,1,0:T(8,128)(2,1)S(1)}, u32[]{:S(2)}, u32[]{:S(2)}) %all-to-all-start.3) | async-done | bytes 98336 | tf_op jit(solution)/shard_map/all_to_all | solution.py:20
  111.9 3.5 %fusion.198 = (bf16[6,256]{1,0:T(8,128)(2,1)S(1)}, f32[6,256]{1,0:T(8,128)S(1)}, f32[6,256]{1,0:T(8,128)S(1)}, f32[6,256]{1,0:T(8,128)S(1)}) fusion(f32[6,256]{1,0:T(8,128)S(1)} %get-tuple-element.17, f32[6,256]{1,0:T(8,128)S(1)} %get-tuple-element.46, f32[6,256]{1,0:T(8,128)S(1)} %get-tuple-element.18, f32[6,256]{1,0:T(8,128)S(1)} %get-tuple-element.45, ...), kind=kOutput, calls=%fused_computation.293 | convolution fusion | flops 25600512 | bytes 4364288 | tf_op jit(solution)/shard_map/dot_general | solution.py:264
  115.4 0.7 broadcast_in_dim.53
  116.0 3.8 %all-to-all-start.4 = ((bf16[32,6,256]{2,1,0:T(8,128)(2,1)}), bf16[32,6,256]{2,1,0:T(8,128)(2,1)S(1)}, u32[]{:S(2)}, u32[]{:S(2)}) async-start(bf16[32,6,256]{2,1,0:T(8,128)(2,1)} %broadcast_in_dim.53), calls=%async_computation.4 | async-start | bytes 262144 | tf_op jit(solution)/shard_map/all_to_all | solution.py:20
  119.9 14.7 %all-to-all-done.4 = bf16[32,6,256]{2,1,0:T(8,128)(2,1)S(1)} async-done(((bf16[32,6,256]{2,1,0:T(8,128)(2,1)}), bf16[32,6,256]{2,1,0:T(8,128)(2,1)S(1)}, u32[]{:S(2)}, u32[]{:S(2)}) %all-to-all-start.4) | async-done | bytes 98336 | tf_op jit(solution)/shard_map/all_to_all | solution.py:20
  134.7 3.5 %fusion.197 = (bf16[6,256]{1,0:T(8,128)(2,1)S(1)}, f32[6,256]{1,0:T(8,128)S(1)}, f32[6,256]{1,0:T(8,128)S(1)}, f32[6,256]{1,0:T(8,128)S(1)}) fusion(f32[6,256]{1,0:T(8,128)S(1)} %get-tuple-element.14, f32[6,256]{1,0:T(8,128)S(1)} %get-tuple-element.47, f32[6,256]{1,0:T(8,128)S(1)} %get-tuple-element.15, f32[6,256]{1,0:T(8,128)S(1)} %get-tuple-element.46, ...), kind=kOutput, calls=%fused_computation.292 | convolution fusion | flops 25703424 | bytes 4382720 | tf_op jit(solution)/shard_map/dot_general | solution.py:264
  138.1 0.7 broadcast_in_dim.54
  138.8 3.8 %all-to-all-start.5 = ((bf16[32,6,256]{2,1,0:T(8,128)(2,1)}), bf16[32,6,256]{2,1,0:T(8,128)(2,1)S(1)}, u32[]{:S(2)}, u32[]{:S(2)}) async-start(bf16[32,6,256]{2,1,0:T(8,128)(2,1)} %broadcast_in_dim.54), calls=%async_computation.5 | async-start | bytes 262144 | tf_op jit(solution)/shard_map/all_to_all | solution.py:20
  142.7 14.8 %all-to-all-done.5 = bf16[32,6,256]{2,1,0:T(8,128)(2,1)S(1)} async-done(((bf16[32,6,256]{2,1,0:T(8,128)(2,1)}), bf16[32,6,256]{2,1,0:T(8,128)(2,1)S(1)}, u32[]{:S(2)}, u32[]{:S(2)}) %all-to-all-start.5) | async-done | bytes 98336 | tf_op jit(solution)/shard_map/all_to_all | solution.py:20
  157.4 3.5 %fusion.195 = (bf16[6,256]{1,0:T(8,128)(2,1)S(1)}, f32[6,256]{1,0:T(8,128)S(1)}, f32[6,256]{1,0:T(8,128)S(1)}, f32[6,256]{1,0:T(8,128)S(1)}) fusion(f32[6,256]{1,0:T(8,128)S(1)} %get-tuple-element.11, f32[6,256]{1,0:T(8,128)S(1)} %get-tuple-element.48, f32[6,256]{1,0:T(8,128)S(1)} %get-tuple-element.12, f32[6,256]{1,0:T(8,128)S(1)} %get-tuple-element.47, ...), kind=kOutput, calls=%fused_computation.291 | convolution fusion | flops 25810944 | bytes 4395008 | tf_op jit(solution)/shard_map/dot_general | solution.py:264
  160.9 0.7 broadcast_in_dim.62
  161.6 3.8 %all-to-all-start.6 = ((bf16[32,6,256]{2,1,0:T(8,128)(2,1)}), bf16[32,6,256]{2,1,0:T(8,128)(2,1)S(1)}, u32[]{:S(2)}, u32[]{:S(2)}) async-start(bf16[32,6,256]{2,1,0:T(8,128)(2,1)} %broadcast_in_dim.62), calls=%async_computation.6 | async-start | bytes 262144 | tf_op jit(solution)/shard_map/all_to_all | solution.py:20
  165.4 0.6 multiply_add_fusion
  166.0 0.1 reshape.167
  166.1 0.1 reshape.166
  166.3 1.3 collective-permute-start.3
  167.6 5.7 %collective-permute-start.2 = (f32[3,6,8]{2,1,0:T(8,128)S(1)}, f32[3,6,8]{2,1,0:T(8,128)S(1)}, u32[]{:S(2)}, u32[]{:S(2)}) collective-permute-start(f32[3,6,8]{2,1,0:T(8,128)S(1)} %get-tuple-element.30), channel_id=1, source_target_pairs={{0,1},{1,2},{2,3},{3,4},{4,5},{5,6},{6,7},{7,8},{8,9},{9,10},{10,1... | collective-permute-start | bytes 1736 | tf_op jit(solution)/shard_map/ppermute | solution.py:236
  173.3 6.9 %all-to-all-done.6 = bf16[32,6,256]{2,1,0:T(8,128)(2,1)S(1)} async-done(((bf16[32,6,256]{2,1,0:T(8,128)(2,1)}), bf16[32,6,256]{2,1,0:T(8,128)(2,1)S(1)}, u32[]{:S(2)}, u32[]{:S(2)}) %all-to-all-start.6) | async-done | bytes 98336 | tf_op jit(solution)/shard_map/all_to_all | solution.py:20
  180.2 3.5 %fusion.150 = f32[6,256]{1,0:T(8,128)S(1)} fusion(bf16[6,8192]{1,0:T(8,128)(2,1)S(1)} %bitcast.106, bf16[256,8192]{1,0:T(8,128)(2,1)} %param.10, f32[6,256]{1,0:T(8,128)S(1)} %get-tuple-element.6, f32[6,256]{1,0:T(8,128)S(1)} %get-tuple-element.28, f32[6,256]{1,0:T(8,128)S(1)} %get-tuple-element.49, f32[6,256]{1,0:T(8,128)S(1)} %get-tuple-element.48, ...), kind=kOutput, calls=%fused_computation.194 | convolution fusion | flops 25890816 | bytes 4391936 | tf_op jit(solution)/shard_map/dot_general | solution.py:264
  183.7 0.3 fusion.172
  184.0 0.1 pad_maximum_fusion.2
  184.1 0.1 reshape.170
  184.2 0.1 reshape.169
  184.4 0.1 maximum_bitcast_fusion
  184.5 0.7 reshape.172
  185.2 14.1 %all-to-all-start.7 = ((f32[16,1,384]{2,1,0:T(1,128)}), f32[16,1,384]{2,1,0:T(1,128)S(1)}, u32[]{:S(2)}, u32[]{:S(2)}) async-start(f32[16,1,384]{2,1,0:T(1,128)} %reshape.172), calls=%async_computation.7 | async-start | bytes 49152 | tf_op jit(solution)/shard_map/all_to_all | solution.py:314
  199.4 0.1 broadcast_in_dim.67
  199.5 5.6 %all-to-all-done.7 = f32[16,1,384]{2,1,0:T(1,128)S(1)} async-done(((f32[16,1,384]{2,1,0:T(1,128)}), f32[16,1,384]{2,1,0:T(1,128)S(1)}, u32[]{:S(2)}, u32[]{:S(2)}) %all-to-all-start.7) | async-done | bytes 24608 | tf_op jit(solution)/shard_map/all_to_all | solution.py:314
  205.1 0.5 broadcast.417
  205.6 0.7 reduce
  206.3 0.1 reshape.173.got_ref
  206.4 3.7 %shard_map.100 = f32[3,96,16]{2,1,0:T(8,128)S(1)} custom-call(f32[16,6,64]{2,1,0:T(8,128)S(1)} %reshape.173.got_ref, f32[2,72,256]{2,1,0:T(8,128)S(1)} %concatenate.33.table_ref), custom_call_target="tpu_custom_call" | custom-call | tf_op jit(solution)/shard_map/pallas_call | solution.py:221
  210.2 0.7 copy.16
  (49 shorter events, 0.6 us)
Async XLA Ops:
  0.0 62.2 %copy-start.1 = (f32[6,256]{1,0:T(8,128)S(1)}, f32[6,256]{1,0:T(8,128)}, u32[]{:S(2)}) copy-start(f32[6,256]{1,0:T(8,128)} %param.16) | copy-start | bytes 18436
  0.0 62.2 %copy-start.4 = (f32[256]{0:T(256)S(1)}, f32[256]{0:T(256)}, u32[]{:S(2)}) copy-start(f32[256]{0:T(256)} %param.11) | copy-start | bytes 3076
  0.0 62.2 %copy-start.5 = (f32[256]{0:T(256)S(1)}, f32[256]{0:T(256)}, u32[]{:S(2)}) copy-start(f32[256]{0:T(256)} %param.12) | copy-start | bytes 3076
  0.0 62.2 %copy-start.6 = (f32[256]{0:T(256)S(1)}, f32[256]{0:T(256)}, u32[]{:S(2)}) copy-start(f32[256]{0:T(256)} %param.13) | copy-start | bytes 3076
  0.0 62.2 %copy-start.3 = (f32[256]{0:T(256)S(1)}, f32[256]{0:T(256)}, u32[]{:S(2)}) copy-start(f32[256]{0:T(256)} %param.14) | copy-start | bytes 3076
  0.0 62.2 %copy-start.2 = (f32[256]{0:T(256)S(1)}, f32[256]{0:T(256)}, u32[]{:S(2)}) copy-start(f32[256]{0:T(256)} %param.15) | copy-start | bytes 3076
  0.0 62.2 %copy-start = (f32[6,256]{1,0:T(8,128)S(1)}, f32[6,256]{1,0:T(8,128)}, u32[]{:S(2)}) copy-start(f32[6,256]{1,0:T(8,128)} %param.17) | copy-start | bytes 18436
  1.5 33.2 %all-to-all-start = ((bf16[32,6,256]{2,1,0:T(8,128)(2,1)}), bf16[32,6,256]{2,1,0:T(8,128)(2,1)S(1)}, u32[]{:S(2)}, u32[]{:S(2)}) async-start(bf16[32,6,256]{2,1,0:T(8,128)(2,1)} %broadcast_in_dim.49), calls=%async_computation | async-start | bytes 262144 | tf_op jit(solution)/shard_map/all_to_all | solution.py:20
  20.8 53.9 %collective-permute-start.1 = (f32[7,8]{1,0:T(8,128)S(1)}, f32[7,8]{1,0:T(8,128)S(1)}, u32[]{:S(2)}, u32[]{:S(2)}) collective-permute-start(f32[7,8]{1,0:T(8,128)S(1)} %get-tuple-element.35), channel_id=1, source_target_pairs={{1,0},{2,1},{3,2},{4,3},{5,4},{6,5},{7,6},{8,7},{9,8},{10,9},{11,1... | collective-permute-start | bytes 680 | tf_op jit(solution)/shard_map/ppermute | solution.py:237
  22.1 52.6 %collective-permute-start = (f32[7,8]{1,0:T(8,128)S(1)}, f32[7,8]{1,0:T(8,128)S(1)}, u32[]{:S(2)}, u32[]{:S(2)}) collective-permute-start(f32[7,8]{1,0:T(8,128)S(1)} %get-tuple-element.34), channel_id=1, source_target_pairs={{0,1},{1,2},{2,3},{3,4},{4,5},{5,6},{6,7},{7,8},{8,9},{9,10},{10,1... | collective-permute-start | bytes 680 | tf_op jit(solution)/shard_map/ppermute | solution.py:236
  34.7 40.1 %copy-start.7 = (f32[256]{0:T(256)S(1)}, f32[256]{0:T(256)}, u32[]{:S(2)}) copy-start(f32[256]{0:T(256)} %param.18) | copy-start | bytes 3076
  34.7 40.1 %copy-start.8 = (f32[256]{0:T(256)S(1)}, f32[256]{0:T(256)}, u32[]{:S(2)}) copy-start(f32[256]{0:T(256)} %param.19) | copy-start | bytes 3076
  38.9 23.3 %all-to-all-start.1 = ((bf16[32,6,256]{2,1,0:T(8,128)(2,1)}), bf16[32,6,256]{2,1,0:T(8,128)(2,1)S(1)}, u32[]{:S(2)}, u32[]{:S(2)}) async-start(bf16[32,6,256]{2,1,0:T(8,128)(2,1)} %broadcast_in_dim.50), calls=%async_computation.1 | async-start | bytes 262144 | tf_op jit(solution)/shard_map/all_to_all | solution.py:20
  48.5 135.2 %collective-permute-start.5 = (bf16[8,8192]{1,0:T(8,128)(2,1)S(1)}, bf16[8,8192]{1,0:T(8,128)(2,1)S(1)}, u32[]{:S(2)}, u32[]{:S(2)}) collective-permute-start(bf16[8,8192]{1,0:T(8,128)(2,1)S(1)} %get-tuple-element.25), channel_id=1, source_target_pairs={{1,0},{2,1},{3,2},{4,3},{5,4},{6,5},{7,6},{8,7},{9,8},{10,9},{11,1... | collective-permute-start | bytes 393224 | tf_op jit(solution)/shard_map/ppermute | solution.py:237
  49.8 133.9 %collective-permute-start.4 = (bf16[8,8192]{1,0:T(8,128)(2,1)S(1)}, bf16[8,8192]{1,0:T(8,128)(2,1)S(1)}, u32[]{:S(2)}, u32[]{:S(2)}) collective-permute-start(bf16[8,8192]{1,0:T(8,128)(2,1)S(1)} %get-tuple-element.24), channel_id=1, source_target_pairs={{0,1},{1,2},{2,3},{3,4},{4,5},{5,6},{6,7},{7,8},{8,9},{9,10},{10,1... | collective-permute-start | bytes 393224 | tf_op jit(solution)/shard_map/ppermute | solution.py:236
  66.4 22.7 %all-to-all-start.2 = ((bf16[32,6,256]{2,1,0:T(8,128)(2,1)}), bf16[32,6,256]{2,1,0:T(8,128)(2,1)S(1)}, u32[]{:S(2)}, u32[]{:S(2)}) async-start(bf16[32,6,256]{2,1,0:T(8,128)(2,1)} %broadcast_in_dim.51), calls=%async_computation.2 | async-start | bytes 262144 | tf_op jit(solution)/shard_map/all_to_all | solution.py:20
  93.3 18.6 %all-to-all-start.3 = ((bf16[32,6,256]{2,1,0:T(8,128)(2,1)}), bf16[32,6,256]{2,1,0:T(8,128)(2,1)S(1)}, u32[]{:S(2)}, u32[]{:S(2)}) async-start(bf16[32,6,256]{2,1,0:T(8,128)(2,1)} %broadcast_in_dim.52), calls=%async_computation.3 | async-start | bytes 262144 | tf_op jit(solution)/shard_map/all_to_all | solution.py:20
  116.0 18.6 %all-to-all-start.4 = ((bf16[32,6,256]{2,1,0:T(8,128)(2,1)}), bf16[32,6,256]{2,1,0:T(8,128)(2,1)S(1)}, u32[]{:S(2)}, u32[]{:S(2)}) async-start(bf16[32,6,256]{2,1,0:T(8,128)(2,1)} %broadcast_in_dim.53), calls=%async_computation.4 | async-start | bytes 262144 | tf_op jit(solution)/shard_map/all_to_all | solution.py:20
  138.8 18.6 %all-to-all-start.5 = ((bf16[32,6,256]{2,1,0:T(8,128)(2,1)}), bf16[32,6,256]{2,1,0:T(8,128)(2,1)S(1)}, u32[]{:S(2)}, u32[]{:S(2)}) async-start(bf16[32,6,256]{2,1,0:T(8,128)(2,1)} %broadcast_in_dim.54), calls=%async_computation.5 | async-start | bytes 262144 | tf_op jit(solution)/shard_map/all_to_all | solution.py:20
  161.6 18.6 %all-to-all-start.6 = ((bf16[32,6,256]{2,1,0:T(8,128)(2,1)}), bf16[32,6,256]{2,1,0:T(8,128)(2,1)S(1)}, u32[]{:S(2)}, u32[]{:S(2)}) async-start(bf16[32,6,256]{2,1,0:T(8,128)(2,1)} %broadcast_in_dim.62), calls=%async_computation.6 | async-start | bytes 262144 | tf_op jit(solution)/shard_map/all_to_all | solution.py:20
  166.3 17.4 %collective-permute-start.3 = (f32[3,6,8]{2,1,0:T(8,128)S(1)}, f32[3,6,8]{2,1,0:T(8,128)S(1)}, u32[]{:S(2)}, u32[]{:S(2)}) collective-permute-start(f32[3,6,8]{2,1,0:T(8,128)S(1)} %get-tuple-element.31), channel_id=1, source_target_pairs={{1,0},{2,1},{3,2},{4,3},{5,4},{6,5},{7,6},{8,7},{9,8},{10,9},{11,1... | collective-permute-start | bytes 1736 | tf_op jit(solution)/shard_map/ppermute | solution.py:237
  167.6 16.1 %collective-permute-start.2 = (f32[3,6,8]{2,1,0:T(8,128)S(1)}, f32[3,6,8]{2,1,0:T(8,128)S(1)}, u32[]{:S(2)}, u32[]{:S(2)}) collective-permute-start(f32[3,6,8]{2,1,0:T(8,128)S(1)} %get-tuple-element.30), channel_id=1, source_target_pairs={{0,1},{1,2},{2,3},{3,4},{4,5},{5,6},{6,7},{7,8},{8,9},{9,10},{10,1... | collective-permute-start | bytes 1736 | tf_op jit(solution)/shard_map/ppermute | solution.py:236
  185.2 19.9 %all-to-all-start.7 = ((f32[16,1,384]{2,1,0:T(1,128)}), f32[16,1,384]{2,1,0:T(1,128)S(1)}, u32[]{:S(2)}, u32[]{:S(2)}) async-start(f32[16,1,384]{2,1,0:T(1,128)} %reshape.172), calls=%async_computation.7 | async-start | bytes 49152 | tf_op jit(solution)/shard_map/all_to_all | solution.py:314

commit v2 on v1

--- a/solution.py
+++ b/solution.py
@@ -10,6 +10,7 @@
 NS_ITERS = 6
 MARGIN = 8
 F32, BF16 = jnp.float32, jnp.bfloat16
+PARTS = (3, 2, 2, 3, 2, 3)
 
 
 time_step = 0.25
@@ -48,28 +49,25 @@
     return velocity
 
 
-def split(x):
-    high = x.astype(BF16)
-    return high, (x - high.astype(F32)).astype(BF16)
-
-
-def product(rows, blocks):
-    row_high, row_low = split(rows)
-    block_high, block_low = blocks
+def split(x, parts=2):
+    pieces = []
+    for _ in range(parts):
+        pieces.append(x.astype(BF16))
+        x = x - pieces[-1].astype(F32)
+    return pieces
+
+
+def product(rows, right, dims=(((1,), (0,)), ((), ()))):
+    left = split(rows, len(right))
     count = rows.shape[0]
-    both = jnp.dot(jnp.concatenate([row_high, row_low], 0), block_high, preferred_element_type=F32)
-    rest = jnp.dot(row_high, block_low, preferred_element_type=F32)
-    return both[:count] + (both[count:] + rest)
-
-
-def product_nt(a, b):
-    dims = (((1,), (1,)), ((), ()))
-    ah, al = split(a)
-    bh, bl = split(b)
-    count = a.shape[0]
-    both = lax.dot_general(jnp.concatenate([ah, al], 0), bh, dims, preferred_element_type=F32)
-    rest = lax.dot_general(ah, bl, dims, preferred_element_type=F32)
-    return both[:count] + (both[count:] + rest)
+    total = None
+    for i, piece in reversed(list(enumerate(right))):
+        stacked = jnp.concatenate(left[: len(right) - i], 0)
+        sums = lax.dot_general(stacked, piece, dims, preferred_element_type=F32)
+        for j in reversed(range(len(right) - i)):
+            term = sums[j * count : (j + 1) * count]
+            total = term if total is None else total + term
+    return total
 
 
 def tables(obs_window, sub_block, per_group):
@@ -95,27 +93,53 @@
     return jnp.concatenate([across * along, across * across, along, obs, filler], axis=1)
 
 
+def pack_kernel(deficit_ref, state_ref, rate_ref, rim_ref, out_ref):
+    count, rows, width = out_ref.shape
+    members, own = rate_ref.shape
+    sub_block = own // count
+    half = members // 2
+    rim = rim_ref[...]
+    wide = jnp.concatenate([rim[:, :MARGIN], rate_ref[...], rim[:, MARGIN:]], axis=1)
+    out_ref[...] = jnp.zeros(out_ref.shape, F32)
+    for g in range(count):
+        here = slice(g * sub_block, (g + 1) * sub_block)
+        piece = jnp.concatenate(
+            [
+                deficit_ref[:, here],
+                state_ref[:, here],
+                wide[:, g * sub_block : (g + 1) * sub_block + 2 * MARGIN],
+            ],
+            axis=1,
+        )
+        out_ref[g, :half, :] = jnp.concatenate([piece[:half], piece[half:]], axis=1)
+
+
 def analysis_kernel(got_ref, table_ref, out_ref, all_ref):
-    groups_m, each, width = got_ref.shape
-    ensemble = groups_m * each
+    groups_m, _, width = got_ref.shape
+    width = width // 2
+    ensemble = all_ref.shape[0]
+    half = ensemble // groups_m // 2
     sub_block = (width - 2 * MARGIN) // 3
     window = sub_block + 2 * MARGIN
     halves, _, lanes = table_ref.shape
     count = lanes // window
     for g in range(groups_m):
-        all_ref[g * each : (g + 1) * each, :] = got_ref[g]
+        for side in range(2):
+            at = (2 * g + side) * half
+            all_ref[at : at + half, :] = got_ref[g, :half, side * width : (side + 1) * width]
     values = all_ref[...]
-    mean = jnp.mean(values, axis=0, keepdims=True)
-    anomaly = values - mean
-    y = anomaly[:, 2 * sub_block :]
-    y_tiled = jnp.concatenate([y] * count, axis=1)
-    mean_tiled = jnp.concatenate([mean[:, 2 * sub_block :]] * count, axis=1)
+    rates = values[:, 2 * sub_block :]
     starts = (0, sub_block, 2 * sub_block + MARGIN)
-    pieces = [y]
+    pieces = [rates]
     for h in range(halves):
-        pieces += [anomaly[:, s + h * count : s + (h + 1) * count] for s in starts]
+        pieces += [values[:, s + h * count : s + (h + 1) * count] for s in starts]
     turned = jnp.transpose(jnp.concatenate(pieces, axis=1))
-    grams = product(turned, split(y_tiled))
+    turned_mean = jnp.mean(turned, axis=1, keepdims=True)
+    turned = turned - turned_mean
+    rates_tiled = jnp.concatenate([rates] * count, axis=1)
+    mean_tiled = jnp.mean(rates_tiled, axis=0, keepdims=True)
+    y = split(rates_tiled - mean_tiled, 3)
+    grams = product(turned, y)
     gram = grams[:window]
     row = lax.broadcasted_iota(jnp.int32, (window, lanes), 0)
     lane = lax.broadcasted_iota(jnp.int32, (window, lanes), 1)
@@ -139,10 +163,10 @@
     )
     first = own & (lax.broadcasted_iota(jnp.int32, (vrows, lanes), 1) % window == 0)
 
-    def blocks(x):
+    def blocks(x, parts=2):
         return tuple(
             jnp.where(on_block, jnp.concatenate([part] * count, 0), jnp.zeros((), BF16))
-            for part in split(x)
+            for part in split(x, parts)
         )
 
     free = ensemble - 1.0
@@ -168,11 +192,11 @@
         s["T"] = -0.5 * eye
         s["r"], s["z"] = r * g, g
         s["fz"] = gain
-        s["fr"] = product(full_r, blocks(gain))
+        s["fr"] = product(full_r, blocks(gain, PARTS[0]))
     for it in range(1, NS_ITERS):
         last = it == NS_ITERS - 1
         for s in state:
-            rb = blocks(s["fr"])
+            rb = blocks(s["fr"], PARTS[1])
             if it == 1:
                 zr, tr = product(s["fz"], rb), -0.5 * s["fr"]
             else:
@@ -182,49 +206,52 @@
             s["H"] = -0.5 * (s["z"] * s["S"] + tr)
         for s in state:
             g = 1.5 - 0.5 * s["z"] * s["r"]
-            s["T"] = g * s["T"] + product(s["H"], blocks(s["fz"]))
+            s["T"] = g * s["T"] + product(s["H"], blocks(s["fz"], PARTS[2]))
             rows = [s["fz"]] if last else [s["fz"], s["fr"], s["S"]]
-            both = product(jnp.concatenate(rows, 0), blocks(s["G"]))
+            both = product(jnp.concatenate(rows, 0), blocks(s["G"], PARTS[3]))
             s["fz"] = both[:window]
             if not last:
                 s["fr"] = both[window : 2 * window]
                 s["S"] = both[2 * window :] + s["r"] * s["H"]
             s["r"], s["z"] = s["r"] * g, s["z"] * g
-    ones = jnp.ones((ensemble, lanes), F32)
-    results = []
     for h, s in enumerate(state):
-        u = product(s["q"], blocks(s["T"])) * (s["root"] * s["inv"])
-        pad = jnp.zeros((7, lanes), F32)
-        rows = jnp.concatenate([s["q"], s["drive"], pad], 0)
-        through = product(rows, blocks(s["fz"]))
+        here = slice(window + h * vrows, window + (h + 1) * vrows)
+        u = product(s["q"], blocks(s["T"], PARTS[4])) * (s["root"] * s["inv"])
+        rows = jnp.concatenate([s["q"], s["drive"], jnp.zeros((7, lanes), F32)], 0)
+        through = product(rows, blocks(s["fz"], PARTS[5]))
         factor = jnp.sqrt(free * s["inv"])
         shift = through[:vrows] * (through[vrows : vrows + 1] * s["inv"])
-        right = jnp.concatenate([u * factor, shift], axis=1)
-        left = jnp.concatenate([y_tiled, ones], axis=1)
-        part = product_nt(left, right)
-        keep = jnp.where(first, s["z"] * factor, 0.0)
-        weight = product_nt(jnp.ones((8, lanes), F32), keep)[:1]
+        shift = jnp.sum(shift, axis=1, keepdims=True)
+        keep = jnp.sum(jnp.where(first, s["z"] * factor, 0.0), axis=1, keepdims=True)
+        spread = product(u * factor, y, (((1,), (1,)), ((), ())))
+        result = turned_mean[here] + shift + keep * turned[here] + spread
         for v in range(3):
-            c = slice(starts[v] + h * count, starts[v] + (h + 1) * count)
-            d = slice(v * count, (v + 1) * count)
-            out_ref[v, :, h * count : (h + 1) * count] = (
-                mean[:, c] + anomaly[:, c] * weight[:, d] + part[:, d]
-            )
-
-
-def analyse(received, obs_window):
-    groups_m, each, width = received.shape
-    ensemble = groups_m * each
+            out_ref[v, h * count : (h + 1) * count, :] = result[v * count : (v + 1) * count]
+
+
+def pack(deficit, state_log, rates, rim, count):
+    members, own = rates.shape
+    width = 2 * (3 * (own // count) + 2 * MARGIN)
+    rows = -(-members // 4) * 2
+    return pl.pallas_call(
+        pack_kernel,
+        out_shape=jax.ShapeDtypeStruct((count, rows, width), F32),
+        in_specs=[pl.BlockSpec(memory_space=pltpu.VMEM)] * 4,
+        out_specs=pl.BlockSpec(memory_space=pltpu.VMEM),
+        compiler_params=pltpu.CompilerParams(vmem_limit_bytes=8 * 1024 * 1024),
+    )(deficit, state_log, rates, rim)
+
+
+def analyse(received, table, ensemble):
+    width = received.shape[2] // 2
     sub_block = (width - 2 * MARGIN) // 3
-    per_group = 256 // (sub_block + 2 * MARGIN)
-    table = tables(obs_window, sub_block, per_group)
     return pl.pallas_call(
         analysis_kernel,
-        out_shape=jax.ShapeDtypeStruct((3, ensemble, sub_block), F32),
+        out_shape=jax.ShapeDtypeStruct((3, sub_block, ensemble), F32),
         in_specs=[pl.BlockSpec(memory_space=pltpu.VMEM)] * 2,
         out_specs=pl.BlockSpec(memory_space=pltpu.VMEM),
         scratch_shapes=[pltpu.VMEM((ensemble, width), F32)],
-        compiler_params=pltpu.CompilerParams(vmem_limit_bytes=32 * 1024 * 1024),
+        compiler_params=pltpu.CompilerParams(vmem_limit_bytes=16 * 1024 * 1024),
     )(received, table)
 
 
@@ -260,6 +287,28 @@
     rim_rows = from_neighbours(kernel_rows, 0)
     rim_params = from_neighbours(params, 1)
 
+    group_index = lax.axis_index("member")
+    observed = jnp.concatenate(
+        [rim_params[5:, :MARGIN], params[5:], rim_params[5:, MARGIN:]], axis=1
+    )
+    obs_window = lax.dynamic_slice_in_dim(
+        observed, group_index * sub_block, sub_block + 2 * MARGIN, 1
+    )
+    table = tables(obs_window, sub_block, 256 // (sub_block + 2 * MARGIN))
+    rim_scale, rim_stiffness, rim_base, rim_friction, rim_damping = rim_params[:5]
+    there = rim_damping > 0
+    rim_friction = jnp.where(there, rim_friction, 1.0)
+    rim_damping = jnp.where(there, rim_damping, 1.0)
+    rim_given = (
+        rim_rows,
+        rim_scale,
+        rim_stiffness,
+        rim_base,
+        rim_friction,
+        rim_damping,
+        there.astype(jnp.float32),
+    )
+
     def summed(gathered, rows):
         return lax.dot_general(
             gathered, rows, (((1,), (1,)), ((), ())), preferred_element_type=jnp.float32
@@ -268,58 +317,47 @@
     def gather(deficit):
         return gather_directly(deficit.astype(jnp.bfloat16), "patch", 1)
 
-    def coupling(deficit):
-        total = summed(gather(deficit), kernel_rows)
-        return base_stress + self_stiffness * deficit + row_scale * total
-
-    def tendency(deficit, state_log, guess):
-        velocity = slip_rate(coupling(deficit), state_log, guess, friction_rate, damping)
+    def tendency(gathered, deficit, state_log, guess):
+        total = summed(gathered, kernel_rows)
+        stress = base_stress + self_stiffness * deficit + row_scale * total
+        velocity = slip_rate(stress, state_log, guess, friction_rate, damping)
         return (plate_rate - velocity, jnp.exp(-state_log) - jnp.abs(velocity), velocity)
 
     deficit = deficit_start
     state_log = state_start
     velocity = jnp.zeros_like(deficit_start)
-    for _ in range(STEPS):
+    for step in range(STEPS):
         deficit_zero, state_zero = (deficit, state_log)
-        change, state_change, velocity = tendency(deficit_zero, state_zero, velocity)
+        change, state_change, velocity = tendency(
+            gather(deficit_zero), deficit_zero, state_zero, velocity
+        )
         deficit_one = deficit_zero + time_step * change
         state_one = state_zero + time_step * state_change
-        change, state_change, velocity = tendency(deficit_one, state_one, velocity)
+        rounded = deficit_one.astype(jnp.bfloat16)
+        if step == 0:
+            rounded, table, rim_given = lax.optimization_barrier((rounded, table, rim_given))
+        change, state_change, velocity = tendency(
+            gather_directly(rounded, "patch", 1), deficit_one, state_one, velocity
+        )
         deficit_two = 0.75 * deficit_zero + 0.25 * (deficit_one + time_step * change)
         state_two = 0.75 * state_zero + 0.25 * (state_one + time_step * state_change)
-        change, state_change, velocity = tendency(deficit_two, state_two, velocity)
+        change, state_change, velocity = tendency(
+            gather(deficit_two), deficit_two, state_two, velocity
+        )
         deficit = deficit_zero / 3.0 + 2.0 / 3.0 * (deficit_two + time_step * change)
         state_log = state_zero / 3.0 + 2.0 / 3.0 * (state_two + time_step * state_change)
-    gathered = gather(deficit)
+    rounded, rim_given = lax.optimization_barrier((deficit.astype(jnp.bfloat16), rim_given))
+    gathered = gather_directly(rounded, "patch", 1)
     rim = from_neighbours(jnp.stack([deficit, state_log, velocity]), 2)
-    rim_scale, rim_stiffness, rim_base, rim_friction, rim_damping = rim_params[:5]
+    rim_rows, rim_scale, rim_stiffness, rim_base, rim_friction, rim_damping, there = rim_given
     stress = base_stress + self_stiffness * deficit + row_scale * summed(gathered, kernel_rows)
     forecast = slip_rate(stress, state_log, velocity, friction_rate, damping)
     rim_stress = rim_base + rim_stiffness * rim[0] + rim_scale * summed(gathered, rim_rows)
-    there = rim_damping > 0
-    rim_forecast = slip_rate(
-        rim_stress,
-        rim[1],
-        rim[2],
-        jnp.where(there, rim_friction, 1.0),
-        jnp.where(there, rim_damping, 1.0),
-    )
-    rim_forecast = jnp.where(there, rim_forecast, 0.0)
-    wide = jnp.concatenate([rim_forecast[:, :MARGIN], forecast, rim_forecast[:, MARGIN:]], axis=1)
-    parts = [
-        x.reshape(members, groups, sub_block)
-        for x in (deficit, state_log, wide[:, :own_rows], wide[:, 2 * MARGIN :])
-    ]
-    sent = jnp.transpose(jnp.concatenate(parts, axis=2), (1, 0, 2))
+    rim_forecast = slip_rate(rim_stress, rim[1], rim[2], rim_friction, rim_damping)
+    rim_forecast = jnp.where(there > 0, rim_forecast, 0.0)
+    sent = pack(deficit, state_log, forecast, rim_forecast, groups)
     received = lax.all_to_all(sent, "member", split_axis=0, concat_axis=0, tiled=True)
-    group_index = lax.axis_index("member")
-    observed = jnp.concatenate(
-        [rim_params[5:, :MARGIN], params[5:], rim_params[5:, MARGIN:]], axis=1
-    )
-    obs_window = lax.dynamic_slice_in_dim(
-        observed, group_index * sub_block, sub_block + 2 * MARGIN, 1
-    )
-    analysis = analyse(received, obs_window)
+    analysis = jnp.transpose(analyse(received, table, members * groups), (0, 2, 1))
     return analysis[:, :, None, :]
 
 

time: 212 us -> 203 us (0.958)
  blocking collectives: 0 us -> 123 us
  waiting for transfers between devices: 83.9 us -> 9.14 us
  starting transfers between devices: 85 us -> 42.6 us
  matrix products: 24.6 us -> 13.7 us
  local copies, waits for them, and re-layouts: 9.8 us -> 4.16 us
    all_to_all x0 -> x6, blocking collectives: none -> 123 us  [the longest x5 103 us: from_everyone(): return lax.all_to_all(copies, axis, split_axis=0, concat_axis=0, tiled=True)]
    all_to_all x7 -> x2, waiting for transfers between devices: 78.3 us -> 7.7 us  [from_everyone(): return lax.all_to_all(copies, axis, split_axis=0, concat_axis=0, tiled=True)]
    all_to_all x7 -> x2, starting transfers between devices: 50.3 us -> 22.3 us  [from_everyone(): return lax.all_to_all(copies, axis, split_axis=0, concat_axis=0, tiled=True)]
    all_to_all x1 -> x0, starting transfers between devices: 14.1 us -> none  [body(): lax.all_to_all(sent, 'member', split_axis=0, concat_axis=0, tiled=True)]
    dot_general x8, matrix products: 24.6 us -> 13.7 us  [summed(): lax.dot_general(gathered, rows, (((1,), (1,)), ((), ())), preferred_eleme...]
    all_to_all x1 -> x0, waiting for transfers between devices: 5.64 us -> none  [body(): lax.all_to_all(sent, 'member', split_axis=0, concat_axis=0, tiled=True)]
    broadcast_in_dim x7, local copies, waits for them, and re-layouts: 4.57 us -> 1.39 us  [from_everyone(): copies = jnp.broadcast_to(x, (lax.axis_size(axis), *x.shape))]
    pallas_call x1 -> x2, Pallas kernels: 3.73 us -> 4.88 us  [the longest x1 4.65 us: analyse(): pl.pallas_call(analysis_kernel, out_shape=jax.ShapeDtypeStruct((3, sub_bl...]
  transfers between devices with their start and end apart: 14 -> 8, of which waited for: 8 -> 2; matrix products, arithmetic and copies ran while one was open for 16% -> 4% of each run, Pallas kernels for 0% -> 0%
where the time goes in v2:
time: 203 us; the launch traced here: 202 us
  blocking collectives  123 us (61%)
  starting transfers between devices  42.6 us (21%)
  matrix products  13.7 us (7%)
  waiting for transfers between devices  9.14 us (5%)
  Pallas kernels  4.88 us (2%)
  local copies, waits for them, and re-layouts  4.16 us (2%)
  other arithmetic  3.76 us (2%)
    all_to_all x5, blocking collectives, from_everyone(): return lax.all_to_all(copies, axis, split_axis=0, concat_axis=0, tiled=True)  103 us
    all_to_all x2, starting transfers between devices, from_everyone(): return lax.all_to_all(copies, axis, split_axis=0, concat_axis=0, tiled=True)  22.3 us
    all_to_all x1, blocking collectives, body(): lax.all_to_all(sent, 'member', split_axis=0, concat_axis=0, tiled=True)  20.4 us
    ppermute x3, starting transfers between devices, from_neighbours(): before = lax.ppermute(tail, 'patch', [(i, i + 1) for i in range(count - 1)])  16.4 us
    dot_general x8, matrix products, summed(): lax.dot_general(gathered, rows, (((1,), (1,)), ((), ())), preferred_eleme...  13.7 us
    all_to_all x2, waiting for transfers between devices, from_everyone(): return lax.all_to_all(copies, axis, split_axis=0, concat_axis=0, tiled=True)  7.7 us
    pallas_call x1, Pallas kernels, analyse(): pl.pallas_call(analysis_kernel, out_shape=jax.ShapeDtypeStruct((3, sub_bl...  4.65 us
  transfers between devices with their start and end apart: 8, of which 2 were waited for; matrix products, arithmetic and copies ran while one was open for 4% of the time, Pallas kernels for 0%

profile of v2, /device:TPU:1, one launch (start us, length us, event | category | flops | bytes accessed | tf_op | source)
XLA Modules:
  0.0 201.7 jit_solution(13575142824599933239)
XLA Ops:
  0.0 0.0 copy-start.5
  0.0 0.0 copy-start.7
  0.0 0.0 copy-start.6
  0.0 0.0 copy-start.1
  0.1 0.8 convert_element_type.41
  0.8 0.7 broadcast_in_dim.51
  1.5 18.5 %all-to-all-start = ((bf16[32,6,256]{2,1,0:T(8,128)(2,1)}), bf16[32,6,256]{2,1,0:T(8,128)(2,1)S(1)}, u32[]{:S(2)}, u32[]{:S(2)}) async-start(bf16[32,6,256]{2,1,0:T(8,128)(2,1)} %broadcast_in_dim.51), calls=%async_computation | async-start | bytes 262144 | tf_op jit(solution)/shard_map/all_to_all | solution.py:21
  20.0 0.8 stack.30
  20.8 0.1 fusion.194
  20.8 4.6 %collective-permute-start = (f32[7,8]{1,0:T(8,128)S(1)}, f32[7,8]{1,0:T(8,128)S(1)}, u32[]{:S(2)}, u32[]{:S(2)}) collective-permute-start(f32[7,8]{1,0:T(8,128)S(1)} %get-tuple-element.65), channel_id=1, source_target_pairs={{0,1},{1,2},{2,3},{3,4},{4,5},{5,6},{6,7},{7,8},{8,9},{9,10},{10,1... | collective-permute-start | bytes 680 | tf_op jit(solution)/shard_map/ppermute | solution.py:263
  25.5 1.3 collective-permute-start.1
  26.8 1.0 fusion.192
  27.8 1.3 collective-permute-start.3
  29.1 6.1 %collective-permute-start.2 = (bf16[8,8192]{1,0:T(8,128)(2,1)S(1)}, bf16[8,8192]{1,0:T(8,128)(2,1)S(1)}, u32[]{:S(2)}, u32[]{:S(2)}) collective-permute-start(bf16[8,8192]{1,0:T(8,128)(2,1)S(1)} %get-tuple-element.57), channel_id=1, source_target_pairs={{0,1},{1,2},{2,3},{3,4},{4,5},{5,6},{6,7},{7,8},{8,9},{9,10},{10,1... | collective-permute-start | bytes 393224 | tf_op jit(solution)/shard_map/ppermute | solution.py:263
  35.2 0.7 broadcast_multiply_fusion.8
  35.9 0.1 sub.288
  36.0 0.1 sub.289
  36.1 0.1 sub.294
  36.2 0.1 sub.291
  36.2 0.0 collective-permute-done
  36.2 0.0 collective-permute-done.1
  36.2 0.1 pad_maximum_fusion.3
  36.4 0.8 fusion.184
  37.1 0.1 multiply_sqrt_fusion
  37.2 0.1 broadcast_in_dim.58
  37.4 0.1 reshape.152
  37.5 0.1 mul.505
  37.7 0.1 broadcast_in_dim.61
  37.8 0.0 collective-permute-done.3
  37.8 1.4 collective-permute-done.2
  39.3 0.0 all-to-all-done
  39.3 0.0 copy-start
  39.3 3.7 %fusion.191 = (bf16[6,256]{1,0:T(8,128)(2,1)S(1)}, f32[6,256]{1,0:T(8,128)S(1)}, f32[6,256]{1,0:T(8,128)S(1)}) fusion(f32[6,256]{1,0:T(8,128)} %param.16, f32[256]{0:T(256)} %param.15, f32[256]{0:T(256)S(1)} %get-tuple-element.78, f32[256]{0:T(256)S(1)} %get-tuple-element.79, f32[6,256]{1,0:T(8,128)} %param.17, f32[256]{0:T(256)} %param.14, ...), kind=kOutput, calls=%fused_computation.289 | convolution fusion | flops 25279488 | bytes 4327424 | tf_op jit(solution)/shard_map/dot_general | solution.py:313
  43.0 29.7 %all_to_all.40 = bf16[32,6,256]{2,1,0:T(8,128)(2,1)S(1)} all-to-all(bf16[32,6,256]{2,1,0:T(8,128)(2,1)S(1)} %broadcast_in_dim.65), channel_id=1, replica_groups=mesh['member'=16,'patch'=32] {'patch'}, dimensions={0} | all-to-all | bytes 196608 | tf_op jit(solution)/shard_map/all_to_all | solution.py:21
  72.7 0.0 copy-done.2
  72.7 0.0 copy-done.3
  72.7 0.0 copy-done.4
  72.7 0.0 copy-done.5
  72.8 0.0 copy-done.7
  72.8 0.0 copy-done.6
  72.8 1.3 fusion.190
  74.1 18.2 %all_to_all.41 = bf16[32,6,256]{2,1,0:T(8,128)(2,1)S(1)} all-to-all(bf16[32,6,256]{2,1,0:T(8,128)(2,1)S(1)} %broadcast_in_dim.66), channel_id=1, replica_groups=mesh['member'=16,'patch'=32] {'patch'}, dimensions={0} | all-to-all | bytes 196608 | tf_op jit(solution)/shard_map/all_to_all | solution.py:21
  92.3 1.3 fusion.189
  93.6 18.3 %all_to_all.42 = bf16[32,6,256]{2,1,0:T(8,128)(2,1)S(1)} all-to-all(bf16[32,6,256]{2,1,0:T(8,128)(2,1)S(1)} %broadcast_in_dim.67), channel_id=1, replica_groups=mesh['member'=16,'patch'=32] {'patch'}, dimensions={0} | all-to-all | bytes 196608 | tf_op jit(solution)/shard_map/all_to_all | solution.py:21
  112.0 1.3 fusion.188
  113.3 18.2 %all_to_all.43 = bf16[32,6,256]{2,1,0:T(8,128)(2,1)S(1)} all-to-all(bf16[32,6,256]{2,1,0:T(8,128)(2,1)S(1)} %broadcast_in_dim.68), channel_id=1, replica_groups=mesh['member'=16,'patch'=32] {'patch'}, dimensions={0} | all-to-all | bytes 196608 | tf_op jit(solution)/shard_map/all_to_all | solution.py:21
  131.5 1.3 fusion.187
  132.8 18.1 %all_to_all.44 = bf16[32,6,256]{2,1,0:T(8,128)(2,1)S(1)} all-to-all(bf16[32,6,256]{2,1,0:T(8,128)(2,1)S(1)} %broadcast_in_dim.69), channel_id=1, replica_groups=mesh['member'=16,'patch'=32] {'patch'}, dimensions={0} | all-to-all | bytes 196608 | tf_op jit(solution)/shard_map/all_to_all | solution.py:21
  151.0 1.2 fusion.1
  152.1 0.6 fusion.147
  152.8 0.6 fusion.186
  153.4 0.7 broadcast_in_dim.70
  154.1 3.8 %all-to-all-start.6 = ((bf16[32,6,256]{2,1,0:T(8,128)(2,1)}), bf16[32,6,256]{2,1,0:T(8,128)(2,1)S(1)}, u32[]{:S(2)}, u32[]{:S(2)}) async-start(bf16[32,6,256]{2,1,0:T(8,128)(2,1)} %broadcast_in_dim.70), calls=%async_computation.6 | async-start | bytes 262144 | tf_op jit(solution)/shard_map/all_to_all | solution.py:21
  157.9 0.1 fusion.193
  158.0 1.3 collective-permute-start.5
  159.3 5.7 %collective-permute-start.4 = (f32[3,6,8]{2,1,0:T(8,128)S(1)}, f32[3,6,8]{2,1,0:T(8,128)S(1)}, u32[]{:S(2)}, u32[]{:S(2)}) collective-permute-start(f32[3,6,8]{2,1,0:T(8,128)S(1)} %get-tuple-element.62), channel_id=1, source_target_pairs={{0,1},{1,2},{2,3},{3,4},{4,5},{5,6},{6,7},{7,8},{8,9},{9,10},{10,1... | collective-permute-start | bytes 1736 | tf_op jit(solution)/shard_map/ppermute | solution.py:263
  165.0 7.7 %all-to-all-done.6 = bf16[32,6,256]{2,1,0:T(8,128)(2,1)S(1)} async-done(((bf16[32,6,256]{2,1,0:T(8,128)(2,1)}), bf16[32,6,256]{2,1,0:T(8,128)(2,1)S(1)}, u32[]{:S(2)}, u32[]{:S(2)}) %all-to-all-start.6) | async-done | bytes 98336 | tf_op jit(solution)/shard_map/all_to_all | solution.py:21
  172.7 3.5 %fusion.146.rate_ref = f32[6,256]{1,0:T(8,128)S(1)} fusion(bf16[6,8192]{1,0:T(8,128)(2,1)S(1)} %bitcast.103, bf16[256,8192]{1,0:T(8,128)(2,1)} %param.10, f32[6,256]{1,0:T(8,128)S(1)} %get-tuple-element.42.deficit_ref, f32[6,256]{1,0:T(8,128)S(1)} %get-tuple-element.61.state_ref, f32[6,256]{1,0:T(8,128)S(1)} %fusion.1, ...), kind=kOutput, calls=%fused_computation.191 | convolution fusion | flops 25890816 | bytes 4391936 | tf_op jit(solution)/shard_map/dot_general | solution.py:313
  176.2 0.0 collective-permute-done.5
  176.2 0.0 collective-permute-done.4
  176.2 0.3 fusion.168.rim_ref
  176.5 0.2 shard_map.100
  176.7 20.4 %all_to_all.45.got_ref = f32[16,4,128]{2,1,0:T(4,128)S(1)} all-to-all(f32[16,4,128]{2,1,0:T(4,128)S(1)} %shard_map.100), channel_id=1, replica_groups=mesh['member'=16,'patch'=32] {'member'}, dimensions={0} | all-to-all | bytes 65536 | tf_op jit(solution)/shard_map/all_to_all | solution.py:359
  197.1 4.7 %shard_map.101 = f32[3,16,96]{2,1,0:T(8,128)} custom-call(f32[16,4,128]{2,1,0:T(4,128)S(1)} %all_to_all.45.got_ref, f32[2,72,256]{2,1,0:T(8,128)S(1)} %concatenate.17.table_ref), custom_call_target="tpu_custom_call" | custom-call | tf_op jit(solution)/shard_map/pallas_call | solution.py:248
  (30 shorter events, 0.2 us)
Async XLA Ops:
  0.0 72.7 %copy-start.2 = (f32[6,256]{1,0:T(8,128)S(1)}, f32[6,256]{1,0:T(8,128)}, u32[]{:S(2)}) copy-start(f32[6,256]{1,0:T(8,128)} %param.16) | copy-start | bytes 18436
  0.0 72.7 %copy-start.3 = (f32[256]{0:T(256)S(1)}, f32[256]{0:T(256)}, u32[]{:S(2)}) copy-start(f32[256]{0:T(256)} %param.11) | copy-start | bytes 3076
  0.0 72.7 %copy-start.4 = (f32[256]{0:T(256)S(1)}, f32[256]{0:T(256)}, u32[]{:S(2)}) copy-start(f32[256]{0:T(256)} %param.12) | copy-start | bytes 3076
  0.0 72.7 %copy-start.5 = (f32[256]{0:T(256)S(1)}, f32[256]{0:T(256)}, u32[]{:S(2)}) copy-start(f32[256]{0:T(256)} %param.13) | copy-start | bytes 3076
  0.0 72.7 %copy-start.7 = (f32[256]{0:T(256)S(1)}, f32[256]{0:T(256)}, u32[]{:S(2)}) copy-start(f32[256]{0:T(256)} %param.14) | copy-start | bytes 3076
  0.0 72.7 %copy-start.6 = (f32[256]{0:T(256)S(1)}, f32[256]{0:T(256)}, u32[]{:S(2)}) copy-start(f32[256]{0:T(256)} %param.15) | copy-start | bytes 3076
  0.0 72.7 %copy-start.1 = (f32[6,256]{1,0:T(8,128)S(1)}, f32[6,256]{1,0:T(8,128)}, u32[]{:S(2)}) copy-start(f32[6,256]{1,0:T(8,128)} %param.17) | copy-start | bytes 18436
  1.5 37.8 %all-to-all-start = ((bf16[32,6,256]{2,1,0:T(8,128)(2,1)}), bf16[32,6,256]{2,1,0:T(8,128)(2,1)S(1)}, u32[]{:S(2)}, u32[]{:S(2)}) async-start(bf16[32,6,256]{2,1,0:T(8,128)(2,1)} %broadcast_in_dim.51), calls=%async_computation | async-start | bytes 262144 | tf_op jit(solution)/shard_map/all_to_all | solution.py:21
  20.8 15.4 %collective-permute-start = (f32[7,8]{1,0:T(8,128)S(1)}, f32[7,8]{1,0:T(8,128)S(1)}, u32[]{:S(2)}, u32[]{:S(2)}) collective-permute-start(f32[7,8]{1,0:T(8,128)S(1)} %get-tuple-element.65), channel_id=1, source_target_pairs={{0,1},{1,2},{2,3},{3,4},{4,5},{5,6},{6,7},{7,8},{8,9},{9,10},{10,1... | collective-permute-start | bytes 680 | tf_op jit(solution)/shard_map/ppermute | solution.py:263
  25.5 10.8 %collective-permute-start.1 = (f32[7,8]{1,0:T(8,128)S(1)}, f32[7,8]{1,0:T(8,128)S(1)}, u32[]{:S(2)}, u32[]{:S(2)}) collective-permute-start(f32[7,8]{1,0:T(8,128)S(1)} %get-tuple-element.64), channel_id=1, source_target_pairs={{1,0},{2,1},{3,2},{4,3},{5,4},{6,5},{7,6},{8,7},{9,8},{10,9},{11,1... | collective-permute-start | bytes 680 | tf_op jit(solution)/shard_map/ppermute | solution.py:264
  27.8 10.1 %collective-permute-start.3 = (bf16[8,8192]{1,0:T(8,128)(2,1)S(1)}, bf16[8,8192]{1,0:T(8,128)(2,1)S(1)}, u32[]{:S(2)}, u32[]{:S(2)}) collective-permute-start(bf16[8,8192]{1,0:T(8,128)(2,1)S(1)} %get-tuple-element.58), channel_id=1, source_target_pairs={{1,0},{2,1},{3,2},{4,3},{5,4},{6,5},{7,6},{8,7},{9,8},{10,9},{11,1... | collective-permute-start | bytes 393224 | tf_op jit(solution)/shard_map/ppermute | solution.py:264
  29.1 10.2 %collective-permute-start.2 = (bf16[8,8192]{1,0:T(8,128)(2,1)S(1)}, bf16[8,8192]{1,0:T(8,128)(2,1)S(1)}, u32[]{:S(2)}, u32[]{:S(2)}) collective-permute-start(bf16[8,8192]{1,0:T(8,128)(2,1)S(1)} %get-tuple-element.57), channel_id=1, source_target_pairs={{0,1},{1,2},{2,3},{3,4},{4,5},{5,6},{6,7},{7,8},{8,9},{9,10},{10,1... | collective-permute-start | bytes 393224 | tf_op jit(solution)/shard_map/ppermute | solution.py:263
  39.3 33.5 %copy-start = (bf16[256,8192]{1,0:T(8,128)(2,1)S(1)}, bf16[256,8192]{1,0:T(8,128)(2,1)}, u32[]{:S(2)}) copy-start(bf16[256,8192]{1,0:T(8,128)(2,1)} %param.10) | copy-start | bytes 12582916
  154.1 18.6 %all-to-all-start.6 = ((bf16[32,6,256]{2,1,0:T(8,128)(2,1)}), bf16[32,6,256]{2,1,0:T(8,128)(2,1)S(1)}, u32[]{:S(2)}, u32[]{:S(2)}) async-start(bf16[32,6,256]{2,1,0:T(8,128)(2,1)} %broadcast_in_dim.70), calls=%async_computation.6 | async-start | bytes 262144 | tf_op jit(solution)/shard_map/all_to_all | solution.py:21
  158.0 18.2 %collective-permute-start.5 = (f32[3,6,8]{2,1,0:T(8,128)S(1)}, f32[3,6,8]{2,1,0:T(8,128)S(1)}, u32[]{:S(2)}, u32[]{:S(2)}) collective-permute-start(f32[3,6,8]{2,1,0:T(8,128)S(1)} %get-tuple-element.63), channel_id=1, source_target_pairs={{1,0},{2,1},{3,2},{4,3},{5,4},{6,5},{7,6},{8,7},{9,8},{10,9},{11,1... | collective-permute-start | bytes 1736 | tf_op jit(solution)/shard_map/ppermute | solution.py:264
  159.3 16.9 %collective-permute-start.4 = (f32[3,6,8]{2,1,0:T(8,128)S(1)}, f32[3,6,8]{2,1,0:T(8,128)S(1)}, u32[]{:S(2)}, u32[]{:S(2)}) collective-permute-start(f32[3,6,8]{2,1,0:T(8,128)S(1)} %get-tuple-element.62), channel_id=1, source_target_pairs={{0,1},{1,2},{2,3},{3,4},{4,5},{5,6},{6,7},{7,8},{8,9},{9,10},{10,1... | collective-permute-start | bytes 1736 | tf_op jit(solution)/shard_map/ppermute | solution.py:263

commit v3 on v2

--- a/solution.py
+++ b/solution.py
@@ -1,4 +1,6 @@
+import functools
 import jax
+import numpy as np
 import jax.numpy as jnp
 from jax import lax
 from jax.experimental import pallas as pl
@@ -11,6 +13,7 @@
 MARGIN = 8
 F32, BF16 = jnp.float32, jnp.bfloat16
 PARTS = (3, 2, 2, 3, 2, 3)
+LANES = 128
 
 
 time_step = 0.25
@@ -25,11 +28,6 @@
     blocks = jnp.moveaxis(blocks, 0, dim)
     dims = blocks.shape
     return blocks.reshape(*dims[:dim], dims[dim] * dims[dim + 1], *dims[dim + 2 :])
-
-
-def gather_directly(x, axis, dim):
-    blocks = from_everyone(x, axis)
-    return joined_along(blocks, dim)
 
 
 def inverse_sinh(value):
@@ -70,36 +68,49 @@
     return total
 
 
-def tables(obs_window, sub_block, per_group):
+def tables(obs_window, sub_block, group_index, groups):
     window = sub_block + 2 * MARGIN
-    distance = jnp.abs(
-        jnp.arange(sub_block, dtype=jnp.int32)[:, None]
-        + MARGIN
-        - jnp.arange(window, dtype=jnp.int32)[None, :]
-    ).astype(F32)
-    taper = jnp.where(distance <= MARGIN, jnp.exp(-0.5 * (distance / MARGIN) ** 2), 0.0)
-    weights = taper * obs_window[1][None, :]
-    groups = sub_block // per_group
-    lanes = per_group * window
-    w = weights.reshape(groups, per_group, window)
-    root = jnp.sqrt(w)
-    across = jnp.broadcast_to(
-        jnp.transpose(root, (0, 2, 1))[:, :, :, None], (groups, window, per_group, window)
-    ).reshape(groups, window, lanes)
-    along = root.reshape(groups, 1, lanes)
-    obs = jnp.tile(obs_window[0], per_group)[None, None, :]
-    obs = jnp.broadcast_to(obs, (groups, 1, lanes))
-    filler = jnp.zeros((groups, 6, lanes), F32)
-    return jnp.concatenate([across * along, across * across, along, obs, filler], axis=1)
-
-
-def pack_kernel(deficit_ref, state_ref, rate_ref, rim_ref, out_ref):
+    together = LANES // window
+    sets = sub_block // together
+    distance = np.abs(np.arange(sub_block)[:, None] + MARGIN - np.arange(window)[None, :])
+    taper = np.where(distance <= MARGIN, np.exp(-0.5 * (distance / MARGIN) ** 2), 0.0)
+    taper = taper.reshape(sets, together, window)
+    across = np.broadcast_to(
+        np.transpose(taper, (0, 2, 1))[:, :, :, None], (sets, window, together, window)
+    ).reshape(sets, window, LANES)
+    along = taper.reshape(sets, 1, LANES)
+    root = np.sqrt(across * along).astype(np.float32)
+    root_along = np.sqrt(along).astype(np.float32)
+    across = across.astype(np.float32)
+    precision = obs_window[1]
+    root_precision = jnp.sqrt(precision)
+    root_tiled = jnp.tile(root_precision, together)[None, None, :]
+    lane = np.arange(LANES) % window
+    from_across = jnp.where(
+        group_index == 0,
+        lane < MARGIN,
+        jnp.where(group_index == groups - 1, lane >= window - MARGIN, False),
+    )
+    rows = jnp.stack([jnp.tile(obs_window[0], together), from_across.astype(F32)])
+    return jnp.concatenate(
+        [
+            root * root_precision[None, :, None] * root_tiled,
+            across * precision[None, :, None],
+            root_along * root_tiled,
+            jnp.broadcast_to(rows[None], (sets, 2, LANES)),
+            jnp.zeros((sets, 5, LANES), F32),
+        ],
+        axis=1,
+    )
+
+
+def pack_kernel(members, deficit_ref, state_ref, rate_ref, out_ref):
     count, rows, width = out_ref.shape
-    members, own = rate_ref.shape
+    own = rate_ref.shape[1]
     sub_block = own // count
     half = members // 2
-    rim = rim_ref[...]
-    wide = jnp.concatenate([rim[:, :MARGIN], rate_ref[...], rim[:, MARGIN:]], axis=1)
+    rim = jnp.zeros((rate_ref.shape[0], MARGIN), F32)
+    wide = jnp.concatenate([rim, rate_ref[...], rim], axis=1)
     out_ref[...] = jnp.zeros(out_ref.shape, F32)
     for g in range(count):
         here = slice(g * sub_block, (g + 1) * sub_block)
@@ -111,13 +122,13 @@
             ],
             axis=1,
         )
-        out_ref[g, :half, :] = jnp.concatenate([piece[:half], piece[half:]], axis=1)
-
-
-def analysis_kernel(got_ref, table_ref, out_ref, all_ref):
+        out_ref[g, :half, :] = jnp.concatenate([piece[:half], piece[half:members]], axis=1)
+
+
+def analysis_kernel(got_ref, across_ref, table_ref, out_ref, all_ref):
     groups_m, _, width = got_ref.shape
     width = width // 2
-    ensemble = all_ref.shape[0]
+    ensemble = all_ref.shape[1]
     half = ensemble // groups_m // 2
     sub_block = (width - 2 * MARGIN) // 3
     window = sub_block + 2 * MARGIN
@@ -126,9 +137,15 @@
     for g in range(groups_m):
         for side in range(2):
             at = (2 * g + side) * half
-            all_ref[at : at + half, :] = got_ref[g, :half, side * width : (side + 1) * width]
-    values = all_ref[...]
+            part = slice(side * width, (side + 1) * width)
+            all_ref[0, at : at + half, :] = got_ref[g, :half, part]
+            all_ref[1, at : at + half, :] = across_ref[g, :half, part]
+    values = all_ref[0]
     rates = values[:, 2 * sub_block :]
+    beyond = all_ref[1][:, 2 * sub_block :]
+    beyond = jnp.concatenate([beyond[:, sub_block:], beyond[:, :sub_block]], axis=1)
+    edge = table_ref[0, 2 * window + 2 : 2 * window + 3, :window]
+    rates = jnp.where(edge > 0, beyond, rates)
     starts = (0, sub_block, 2 * sub_block + MARGIN)
     pieces = [rates]
     for h in range(halves):
@@ -229,40 +246,38 @@
             out_ref[v, h * count : (h + 1) * count, :] = result[v * count : (v + 1) * count]
 
 
-def pack(deficit, state_log, rates, rim, count):
-    members, own = rates.shape
+def pack(deficit, state_log, rates, members, count):
+    own = rates.shape[1]
     width = 2 * (3 * (own // count) + 2 * MARGIN)
     rows = -(-members // 4) * 2
     return pl.pallas_call(
-        pack_kernel,
+        functools.partial(pack_kernel, members),
         out_shape=jax.ShapeDtypeStruct((count, rows, width), F32),
-        in_specs=[pl.BlockSpec(memory_space=pltpu.VMEM)] * 4,
+        in_specs=[pl.BlockSpec(memory_space=pltpu.VMEM)] * 3,
         out_specs=pl.BlockSpec(memory_space=pltpu.VMEM),
         compiler_params=pltpu.CompilerParams(vmem_limit_bytes=8 * 1024 * 1024),
-    )(deficit, state_log, rates, rim)
-
-
-def analyse(received, table, ensemble):
+    )(deficit, state_log, rates)
+
+
+def analyse(received, across, table, ensemble):
     width = received.shape[2] // 2
     sub_block = (width - 2 * MARGIN) // 3
     return pl.pallas_call(
         analysis_kernel,
         out_shape=jax.ShapeDtypeStruct((3, sub_block, ensemble), F32),
-        in_specs=[pl.BlockSpec(memory_space=pltpu.VMEM)] * 2,
+        in_specs=[pl.BlockSpec(memory_space=pltpu.VMEM)] * 3,
         out_specs=pl.BlockSpec(memory_space=pltpu.VMEM),
-        scratch_shapes=[pltpu.VMEM((ensemble, width), F32)],
+        scratch_shapes=[pltpu.VMEM((2, ensemble, width), F32)],
         compiler_params=pltpu.CompilerParams(vmem_limit_bytes=16 * 1024 * 1024),
-    )(received, table)
-
-
-def from_neighbours(block, dim):
-    count = lax.axis_size("patch")
-    size = block.shape[dim]
-    tail = lax.slice_in_dim(block, size - MARGIN, size, axis=dim)
-    front = lax.slice_in_dim(block, 0, MARGIN, axis=dim)
-    before = lax.ppermute(tail, "patch", [(i, i + 1) for i in range(count - 1)])
-    after = lax.ppermute(front, "patch", [(i + 1, i) for i in range(count - 1)])
-    return jnp.concatenate([before, after], axis=dim)
+    )(received, across, table)
+
+
+def in_pieces(x):
+    pieces = []
+    for _ in range(3):
+        pieces.append(lax.reduce_precision(x, exponent_bits=8, mantissa_bits=7))
+        x = x - pieces[-1]
+    return jnp.stack(pieces).astype(BF16)
 
 
 def body(
@@ -278,86 +293,94 @@
     obs_precision,
 ):
     groups = lax.axis_size("member")
+    blocks = lax.axis_size("patch")
     own_rows = kernel_rows.shape[0]
     members = deficit_start.shape[0]
     sub_block = own_rows // groups
-    params = jnp.stack(
-        [row_scale, self_stiffness, base_stress, friction_rate, damping, obs_rate, obs_precision]
-    )
-    rim_rows = from_neighbours(kernel_rows, 0)
-    rim_params = from_neighbours(params, 1)
-
-    group_index = lax.axis_index("member")
-    observed = jnp.concatenate(
-        [rim_params[5:, :MARGIN], params[5:], rim_params[5:, MARGIN:]], axis=1
-    )
-    obs_window = lax.dynamic_slice_in_dim(
-        observed, group_index * sub_block, sub_block + 2 * MARGIN, 1
-    )
-    table = tables(obs_window, sub_block, 256 // (sub_block + 2 * MARGIN))
-    rim_scale, rim_stiffness, rim_base, rim_friction, rim_damping = rim_params[:5]
-    there = rim_damping > 0
-    rim_friction = jnp.where(there, rim_friction, 1.0)
-    rim_damping = jnp.where(there, rim_damping, 1.0)
-    rim_given = (
-        rim_rows,
-        rim_scale,
-        rim_stiffness,
-        rim_base,
-        rim_friction,
-        rim_damping,
-        there.astype(jnp.float32),
-    )
-
-    def summed(gathered, rows):
-        return lax.dot_general(
-            gathered, rows, (((1,), (1,)), ((), ())), preferred_element_type=jnp.float32
-        )
-
-    def gather(deficit):
-        return gather_directly(deficit.astype(jnp.bfloat16), "patch", 1)
+    rows = -(-members // 8) * 8
+    assert rows > members
+
+    def gather(rounded):
+        return from_everyone(rounded, "patch")
 
     def tendency(gathered, deficit, state_log, guess):
-        total = summed(gathered, kernel_rows)
+        velocity = section_rate(gathered, deficit, state_log, guess)
+        return (plate_rate - velocity, jnp.exp(-state_log) - jnp.abs(velocity), velocity)
+
+    def section_rate(gathered, deficit, state_log, guess):
+        total = lax.dot_general(
+            joined_along(gathered, 1),
+            kernel_rows,
+            (((1,), (1,)), ((), ())),
+            preferred_element_type=F32,
+        )
         stress = base_stress + self_stiffness * deficit + row_scale * total
-        velocity = slip_rate(stress, state_log, guess, friction_rate, damping)
-        return (plate_rate - velocity, jnp.exp(-state_log) - jnp.abs(velocity), velocity)
-
-    deficit = deficit_start
-    state_log = state_start
-    velocity = jnp.zeros_like(deficit_start)
+        return slip_rate(stress, state_log, guess, friction_rate, damping)
+
+    observed = jnp.stack([obs_rate, obs_precision])
+    ends = jnp.stack([observed[:, :MARGIN], observed[:, own_rows - MARGIN :]])
+    spare = in_pieces(ends).reshape(1, -1)
+    spare = jnp.pad(spare, ((0, rows - members - 1), (0, own_rows - spare.shape[1])))
+    full = ((0, rows - members), (0, 0))
+    deficit = jnp.pad(deficit_start, full)
+    state_log = jnp.pad(state_start, full)
+    velocity = jnp.zeros_like(deficit)
+    rounded, group_index, block_index = lax.optimization_barrier(
+        (
+            jnp.concatenate([deficit_start.astype(BF16), spare], axis=0),
+            lax.axis_index("member"),
+            lax.axis_index("patch"),
+        )
+    )
+    first = gather(rounded)
+    first, friction_rate, damping, row_scale, self_stiffness, base_stress = lax.optimization_barrier(
+        (first, friction_rate, damping, row_scale, self_stiffness, base_stress)
+    )
+    gathered = first
     for step in range(STEPS):
         deficit_zero, state_zero = (deficit, state_log)
-        change, state_change, velocity = tendency(
-            gather(deficit_zero), deficit_zero, state_zero, velocity
-        )
+        if step > 0:
+            gathered = gather(deficit_zero.astype(BF16))
+        change, state_change, velocity = tendency(gathered, deficit_zero, state_zero, velocity)
         deficit_one = deficit_zero + time_step * change
         state_one = state_zero + time_step * state_change
-        rounded = deficit_one.astype(jnp.bfloat16)
-        if step == 0:
-            rounded, table, rim_given = lax.optimization_barrier((rounded, table, rim_given))
         change, state_change, velocity = tendency(
-            gather_directly(rounded, "patch", 1), deficit_one, state_one, velocity
+            gather(deficit_one.astype(BF16)), deficit_one, state_one, velocity
         )
         deficit_two = 0.75 * deficit_zero + 0.25 * (deficit_one + time_step * change)
         state_two = 0.75 * state_zero + 0.25 * (state_one + time_step * state_change)
         change, state_change, velocity = tendency(
-            gather(deficit_two), deficit_two, state_two, velocity
+            gather(deficit_two.astype(BF16)), deficit_two, state_two, velocity
         )
         deficit = deficit_zero / 3.0 + 2.0 / 3.0 * (deficit_two + time_step * change)
         state_log = state_zero / 3.0 + 2.0 / 3.0 * (state_two + time_step * state_change)
-    rounded, rim_given = lax.optimization_barrier((deficit.astype(jnp.bfloat16), rim_given))
-    gathered = gather_directly(rounded, "patch", 1)
-    rim = from_neighbours(jnp.stack([deficit, state_log, velocity]), 2)
-    rim_rows, rim_scale, rim_stiffness, rim_base, rim_friction, rim_damping, there = rim_given
-    stress = base_stress + self_stiffness * deficit + row_scale * summed(gathered, kernel_rows)
-    forecast = slip_rate(stress, state_log, velocity, friction_rate, damping)
-    rim_stress = rim_base + rim_stiffness * rim[0] + rim_scale * summed(gathered, rim_rows)
-    rim_forecast = slip_rate(rim_stress, rim[1], rim[2], rim_friction, rim_damping)
-    rim_forecast = jnp.where(there > 0, rim_forecast, 0.0)
-    sent = pack(deficit, state_log, forecast, rim_forecast, groups)
+    deficit, state_log, velocity = lax.optimization_barrier((deficit, state_log, velocity))
+    forecast = section_rate(gather(deficit.astype(BF16)), deficit, state_log, velocity)
+    sent = pack(deficit, state_log, forecast, members, groups)
     received = lax.all_to_all(sent, "member", split_axis=0, concat_axis=0, tiled=True)
-    analysis = jnp.transpose(analyse(received, table, members * groups), (0, 2, 1))
+    received, first, obs_rate, obs_precision, group_index, block_index = lax.optimization_barrier(
+        (received, first, obs_rate, obs_precision, group_index, block_index)
+    )
+    observed = jnp.stack([obs_rate, obs_precision])
+    spare = first[:, members]
+    pairs = [((groups - 1) * blocks + p, p + 1) for p in range(blocks - 1)]
+    pairs += [(b, a) for a, b in pairs]
+    across = lax.ppermute(received, ("member", "patch"), pairs)
+
+    def ends_of(block):
+        row = lax.dynamic_index_in_dim(spare, jnp.clip(block, 0, blocks - 1), 0, keepdims=False)
+        parts = row[: 3 * ends.size].astype(F32).reshape(3, *ends.shape)
+        there = (block >= 0) & (block < blocks)
+        return jnp.where(there, parts[0] + (parts[1] + parts[2]), 0.0)
+
+    observed = jnp.concatenate(
+        [ends_of(block_index - 1)[1], observed, ends_of(block_index + 1)[0]], axis=1
+    )
+    obs_window = lax.dynamic_slice_in_dim(
+        observed, group_index * sub_block, sub_block + 2 * MARGIN, 1
+    )
+    table = tables(obs_window, sub_block, group_index, groups)
+    analysis = jnp.transpose(analyse(received, across, table, members * groups), (0, 2, 1))
     return analysis[:, :, None, :]
 
 

time: 203 us -> 196 us (0.966)
  the two profiles are of different devices: /device:TPU:1 before, /device:TPU:32 now
where the time goes in v3:
time: 196 us
  blocking collectives  167 us (85%)
  matrix products  11.2 us (6%)
  starting transfers between devices  5.16 us (3%)
  Pallas kernels  4.53 us (2%)
  waiting for transfers between devices  3.83 us (2%)
  other arithmetic  3.2 us (2%)
    all_to_all x7, blocking collectives, from_everyone(): return lax.all_to_all(copies, axis, split_axis=0, concat_axis=0, tiled=True)  156 us
    dot_general x7, matrix products, section_rate(): lax.dot_general(joined_along(gathered, 1), kernel_rows, (((1,), (1,)), ((...  11.2 us
    all_to_all x1, blocking collectives, body(): lax.all_to_all(sent, 'member', split_axis=0, concat_axis=0, tiled=True)  10.5 us
    ppermute x1, starting transfers between devices, body(): across = lax.ppermute(received, ('member', 'patch'), pairs)  5.16 us
    pallas_call x1, Pallas kernels, analyse(): pl.pallas_call(analysis_kernel, out_shape=jax.ShapeDtypeStruct((3, sub_bl...  4.31 us
  transfers between devices with their start and end apart: 1, of which 1 were waited for; matrix products, arithmetic and copies ran while one was open for 0% of the time, Pallas kernels for 0%

profile of v3, /device:TPU:32, one launch (start us, length us, event | category | flops | bytes accessed | tf_op | source)
XLA Modules:
  0.0 195.9 jit_solution(1948431344872249112)
XLA Ops:
  0.0 0.0 copy-start.2
  0.0 0.0 copy-start.6
  0.0 0.0 copy-start.5
  0.0 0.0 copy-start.7
  0.0 0.0 copy-start.8
  0.0 0.0 copy-start.9
  0.0 0.0 copy-start.1
  0.1 0.8 fusion.152
  0.9 0.1 convert_element_type.53
  1.0 0.7 convert_element_type.52
  1.7 0.0 copy-start
  1.7 34.0 %all_to_all.40 = bf16[32,8,256]{2,1,0:T(8,128)(2,1)S(1)} all-to-all(bf16[32,8,256]{2,1,0:T(8,128)(2,1)S(1)} %broadcast_in_dim.27), channel_id=1, replica_groups=mesh['member'=16,'patch'=32] {'patch'}, dimensions={0} | all-to-all | bytes 262144 | tf_op jit(solution)/shard_map/all_to_all | solution.py:24
  35.7 0.7 broadcast_multiply_fusion.5
  36.4 3.5 %fusion.165 = (bf16[8,256]{1,0:T(8,128)(2,1)S(1)}, f32[8,256]{1,0:T(8,128)S(1)}, f32[8,256]{1,0:T(8,128)S(1)}) fusion(f32[256]{0:T(256)} %param.20, f32[256]{0:T(256)S(1)} %get-tuple-element.74, f32[256]{0:T(256)S(1)} %get-tuple-element.75, f32[6,256]{1,0:T(8,128)} %param.22, f32[256]{0:T(256)} %param.19, f32[6,256]{1,0:T(8,128)} %param.21, ...), kind=kOutput, calls=%fused_computation.252 | convolution fusion | flops 33705984 | bytes 4365312 | tf_op jit(solution)/shard_map/dot_general | solution.py:311
  40.0 20.3 %all_to_all.41 = bf16[32,8,256]{2,1,0:T(8,128)(2,1)S(1)} all-to-all(bf16[32,8,256]{2,1,0:T(8,128)(2,1)S(1)} %broadcast_in_dim.28), channel_id=1, replica_groups=mesh['member'=16,'patch'=32] {'patch'}, dimensions={0} | all-to-all | bytes 262144 | tf_op jit(solution)/shard_map/all_to_all | solution.py:24
  60.2 0.0 copy-done.2
  60.2 0.0 copy-done.6
  60.2 0.0 copy-done.5
  60.2 0.0 copy-done.7
  60.3 0.0 copy-done.8
  60.3 0.0 copy-done.9
  60.3 0.0 copy-done.1
  60.3 0.0 copy-done
  60.3 1.3 fusion.164
  61.6 20.4 %all_to_all.42 = bf16[32,8,256]{2,1,0:T(8,128)(2,1)S(1)} all-to-all(bf16[32,8,256]{2,1,0:T(8,128)(2,1)S(1)} %broadcast_in_dim.29), channel_id=1, replica_groups=mesh['member'=16,'patch'=32] {'patch'}, dimensions={0} | all-to-all | bytes 262144 | tf_op jit(solution)/shard_map/all_to_all | solution.py:24
  82.0 1.3 fusion.163
  83.3 20.4 %all_to_all.43 = bf16[32,8,256]{2,1,0:T(8,128)(2,1)S(1)} all-to-all(bf16[32,8,256]{2,1,0:T(8,128)(2,1)S(1)} %broadcast_in_dim.30), channel_id=1, replica_groups=mesh['member'=16,'patch'=32] {'patch'}, dimensions={0} | all-to-all | bytes 262144 | tf_op jit(solution)/shard_map/all_to_all | solution.py:24
  103.7 1.3 fusion.162
  105.0 20.4 %all_to_all.44 = bf16[32,8,256]{2,1,0:T(8,128)(2,1)S(1)} all-to-all(bf16[32,8,256]{2,1,0:T(8,128)(2,1)S(1)} %broadcast_in_dim.31), channel_id=1, replica_groups=mesh['member'=16,'patch'=32] {'patch'}, dimensions={0} | all-to-all | bytes 262144 | tf_op jit(solution)/shard_map/all_to_all | solution.py:24
  125.4 1.3 multiply_add_fusion.2
  126.7 0.5 fusion.161
  127.3 20.4 %all_to_all.45 = bf16[32,8,256]{2,1,0:T(8,128)(2,1)S(1)} all-to-all(bf16[32,8,256]{2,1,0:T(8,128)(2,1)S(1)} %broadcast_in_dim.32), channel_id=1, replica_groups=mesh['member'=16,'patch'=32] {'patch'}, dimensions={0} | all-to-all | bytes 262144 | tf_op jit(solution)/shard_map/all_to_all | solution.py:24
  147.7 0.0 copy-start.10
  147.7 0.0 copy-start.11
  147.7 0.0 copy-start.12
  147.7 0.0 copy-start.4
  147.7 0.0 copy-start.3
  147.7 0.0 copy-start.13
  147.7 0.0 copy-start.14
  147.7 1.3 multiply_add_fusion
  149.1 20.4 %all_to_all.46 = bf16[32,8,256]{2,1,0:T(8,128)(2,1)S(1)} all-to-all(bf16[32,8,256]{2,1,0:T(8,128)(2,1)S(1)} %broadcast_in_dim.33), channel_id=1, replica_groups=mesh['member'=16,'patch'=32] {'patch'}, dimensions={0} | all-to-all | bytes 262144 | tf_op jit(solution)/shard_map/all_to_all | solution.py:24
  169.4 1.3 fusion.146.rate_ref
  170.7 0.2 shard_map.145
  171.0 10.5 %all_to_all.47.got_ref = f32[16,4,128]{2,1,0:T(4,128)S(1)} all-to-all(f32[16,4,128]{2,1,0:T(4,128)S(1)} %shard_map.145), channel_id=1, replica_groups=mesh['member'=16,'patch'=32] {'member'}, dimensions={0} | all-to-all | bytes 65536 | tf_op jit(solution)/shard_map/all_to_all | solution.py:360
  181.6 0.1 broadcast_select_fusion.1
  181.6 0.1 slice_reduce_fusion.1
  181.7 0.1 squeeze.9
  181.8 0.1 broadcast_select_fusion
  181.9 0.1 squeeze.10
  182.0 0.0 copy-done.10
  182.0 0.0 copy-done.11
  182.0 0.1 fusion.154
  182.1 5.2 %collective-permute-start = (f32[16,4,128]{2,1,0:T(4,128)S(1)}, f32[16,4,128]{2,1,0:T(4,128)S(1)}, u32[]{:S(2)}, u32[]{:S(2)}) collective-permute-start(f32[16,4,128]{2,1,0:T(4,128)S(1)} %all_to_all.47.got_ref), channel_id=1, source_target_pairs={{480,1},{481,2},{482,3},{483,4},{484,5},{485,6},{486,7},{487,8},{4... | collective-permute-start | bytes 98312 | tf_op jit(solution)/shard_map/ppermute | solution.py:368
  187.3 0.1 mul.1064
  187.4 0.1 stack_tile.3
  187.5 0.0 copy-done.12
  187.5 0.0 copy-done.4
  187.5 0.1 multiply_multiply_fusion
  187.6 0.0 copy-done.3
  187.6 0.1 broadcast_multiply_fusion
  187.7 0.0 copy-done.13
  187.7 0.0 copy-done.14
  187.7 3.8 %collective-permute-done.across_ref = f32[16,4,128]{2,1,0:T(4,128)S(1)} collective-permute-done((f32[16,4,128]{2,1,0:T(4,128)S(1)}, f32[16,4,128]{2,1,0:T(4,128)S(1)}, u32[]{:S(2)}, u32[]{:S(2)}) %collective-permute-start) | collective-permute-done | bytes 32800 | tf_op jit(solution)/shard_map/ppermute | solution.py:368
  191.6 4.3 %shard_map.146 = f32[3,16,96]{2,1,0:T(8,128)} custom-call(f32[16,4,128]{2,1,0:T(4,128)S(1)} %all_to_all.47.got_ref, f32[16,4,128]{2,1,0:T(4,128)S(1)} %collective-permute-done.across_ref, f32[4,72,128]{2,1,0:T(8,128)S(1)} %concatenate.35.table_ref), custom_call_target="tpu_custom_call" | custom-call | tf_op jit(solution)/shard_map/pallas_call | solution.py:265
  (24 shorter events, 0.3 us)
Async XLA Ops:
  0.0 60.2 %copy-start.2 = (f32[6,256]{1,0:T(8,128)S(1)}, f32[6,256]{1,0:T(8,128)}, u32[]{:S(2)}) copy-start(f32[6,256]{1,0:T(8,128)} %param.21) | copy-start | bytes 18436
  0.0 60.2 %copy-start.6 = (f32[256]{0:T(256)S(1)}, f32[256]{0:T(256)}, u32[]{:S(2)}) copy-start(f32[256]{0:T(256)} %param.19) | copy-start | bytes 3076
  0.0 60.2 %copy-start.5 = (f32[256]{0:T(256)S(1)}, f32[256]{0:T(256)}, u32[]{:S(2)}) copy-start(f32[256]{0:T(256)} %param.20) | copy-start | bytes 3076
  0.0 60.2 %copy-start.7 = (f32[256]{0:T(256)S(1)}, f32[256]{0:T(256)}, u32[]{:S(2)}) copy-start(f32[256]{0:T(256)} %param.16) | copy-start | bytes 3076
  0.0 60.2 %copy-start.8 = (f32[256]{0:T(256)S(1)}, f32[256]{0:T(256)}, u32[]{:S(2)}) copy-start(f32[256]{0:T(256)} %param.17) | copy-start | bytes 3076
  0.0 60.2 %copy-start.9 = (f32[256]{0:T(256)S(1)}, f32[256]{0:T(256)}, u32[]{:S(2)}) copy-start(f32[256]{0:T(256)} %param.18) | copy-start | bytes 3076
  0.0 60.2 %copy-start.1 = (f32[6,256]{1,0:T(8,128)S(1)}, f32[6,256]{1,0:T(8,128)}, u32[]{:S(2)}) copy-start(f32[6,256]{1,0:T(8,128)} %param.22) | copy-start | bytes 18436
  1.7 58.6 %copy-start = (bf16[256,8192]{1,0:T(8,128)(2,1)S(1)}, bf16[256,8192]{1,0:T(8,128)(2,1)}, u32[]{:S(2)}) copy-start(bf16[256,8192]{1,0:T(8,128)(2,1)} %param.15) | copy-start | bytes 12582916
  147.7 34.3 %copy-start.10 = (f32[256]{0:T(256)S(1)}, f32[256]{0:T(256)}, u32[]{:S(2)}) copy-start(f32[256]{0:T(256)} %param.23) | copy-start | bytes 3076
  147.7 34.3 %copy-start.11 = (f32[256]{0:T(256)S(1)}, f32[256]{0:T(256)}, u32[]{:S(2)}) copy-start(f32[256]{0:T(256)} %param.24) | copy-start | bytes 3076
  147.7 39.8 %copy-start.12 = (f32[4,1,128]{2,1,0:T(1,128)S(1)}, f32[4,1,128]{2,1,0:T(1,128)}, u32[]{:S(2)}) copy-start(f32[4,1,128]{2,1,0:T(1,128)} %constant.84) | copy-start | bytes 6148
  147.7 39.8 %copy-start.4 = (f32[4,32,128]{2,1,0:T(8,128)S(1)}, f32[4,32,128]{2,1,0:T(8,128)}, u32[]{:S(2)}) copy-start(f32[4,32,128]{2,1,0:T(8,128)} %constant.73.clone) | copy-start | bytes 196612
  147.7 39.9 %copy-start.3 = (f32[4,32,128]{2,1,0:T(8,128)S(1)}, f32[4,32,128]{2,1,0:T(8,128)}, u32[]{:S(2)}) copy-start(f32[4,32,128]{2,1,0:T(8,128)} %constant.74.clone) | copy-start | bytes 196612
  147.7 40.0 %copy-start.13 = (pred[128]{0:T(512)(128)(4,1)S(1)}, pred[128]{0:T(512)(128)(4,1)}, u32[]{:S(2)}) copy-start(pred[128]{0:T(512)(128)(4,1)} %constant.72.clone) | copy-start | bytes 388
  147.7 39.9 %copy-start.14 = (pred[128]{0:T(512)(128)(4,1)S(1)}, pred[128]{0:T(512)(128)(4,1)}, u32[]{:S(2)}) copy-start(pred[128]{0:T(512)(128)(4,1)} %constant.71.clone) | copy-start | bytes 388
  182.1 9.5 %collective-permute-start = (f32[16,4,128]{2,1,0:T(4,128)S(1)}, f32[16,4,128]{2,1,0:T(4,128)S(1)}, u32[]{:S(2)}, u32[]{:S(2)}) collective-permute-start(f32[16,4,128]{2,1,0:T(4,128)S(1)} %all_to_all.47.got_ref), channel_id=1, source_target_pairs={{480,1},{481,2},{482,3},{483,4},{484,5},{485,6},{486,7},{487,8},{4... | collective-permute-start | bytes 98312 | tf_op jit(solution)/shard_map/ppermute | solution.py:368

commit v4 on v3

--- a/solution.py
+++ b/solution.py
@@ -297,11 +297,16 @@
     own_rows = kernel_rows.shape[0]
     members = deficit_start.shape[0]
     sub_block = own_rows // groups
-    rows = -(-members // 8) * 8
-    assert rows > members
+    pair = 2 if members % 2 == 0 else 1
+
+    def paired(rounded):
+        return jnp.stack([rounded[i : i + pair] for i in range(0, members, pair)])
+
+    def joined(blocks):
+        return joined_along(blocks.reshape(blocks.shape[0], members, own_rows), 1)
 
     def gather(rounded):
-        return from_everyone(rounded, "patch")
+        return joined(from_everyone(paired(rounded), "patch"))
 
     def tendency(gathered, deficit, state_log, guess):
         velocity = section_rate(gathered, deficit, state_log, guess)
@@ -309,7 +314,7 @@
 
     def section_rate(gathered, deficit, state_log, guess):
         total = lax.dot_general(
-            joined_along(gathered, 1),
+            gathered,
             kernel_rows,
             (((1,), (1,)), ((), ())),
             preferred_element_type=F32,
@@ -320,23 +325,22 @@
     observed = jnp.stack([obs_rate, obs_precision])
     ends = jnp.stack([observed[:, :MARGIN], observed[:, own_rows - MARGIN :]])
     spare = in_pieces(ends).reshape(1, -1)
-    spare = jnp.pad(spare, ((0, rows - members - 1), (0, own_rows - spare.shape[1])))
-    full = ((0, rows - members), (0, 0))
-    deficit = jnp.pad(deficit_start, full)
-    state_log = jnp.pad(state_start, full)
+    spare = jnp.pad(spare, ((0, pair - 1), (0, own_rows - spare.shape[1])))[None]
+    deficit = deficit_start
+    state_log = state_start
     velocity = jnp.zeros_like(deficit)
     rounded, group_index, block_index = lax.optimization_barrier(
         (
-            jnp.concatenate([deficit_start.astype(BF16), spare], axis=0),
+            jnp.concatenate([paired(deficit_start.astype(BF16)), spare], axis=0),
             lax.axis_index("member"),
             lax.axis_index("patch"),
         )
     )
-    first = gather(rounded)
+    first = from_everyone(rounded, "patch")
     first, friction_rate, damping, row_scale, self_stiffness, base_stress = lax.optimization_barrier(
         (first, friction_rate, damping, row_scale, self_stiffness, base_stress)
     )
-    gathered = first
+    gathered = joined(first[:, : members // pair])
     for step in range(STEPS):
         deficit_zero, state_zero = (deficit, state_log)
         if step > 0:
@@ -362,7 +366,7 @@
         (received, first, obs_rate, obs_precision, group_index, block_index)
     )
     observed = jnp.stack([obs_rate, obs_precision])
-    spare = first[:, members]
+    spare = first[:, members // pair, 0]
     pairs = [((groups - 1) * blocks + p, p + 1) for p in range(blocks - 1)]
     pairs += [(b, a) for a, b in pairs]
     across = lax.ppermute(received, ("member", "patch"), pairs)

time: 196 us -> 189 us (0.964)
  blocking collectives: 167 us -> 158 us
    all_to_all x7, blocking collectives: 156 us -> 147 us  [from_everyone(): return lax.all_to_all(copies, axis, split_axis=0, concat_axis=0, tiled=True)]
where the time goes in v4:
time: 189 us
  blocking collectives  158 us (84%)
  matrix products  11.2 us (6%)
  waiting for transfers between devices  4.69 us (2%)
  Pallas kernels  4.53 us (2%)
  starting transfers between devices  4.3 us (2%)
  other arithmetic  3.93 us (2%)
    all_to_all x7, blocking collectives, from_everyone(): return lax.all_to_all(copies, axis, split_axis=0, concat_axis=0, tiled=True)  147 us
    dot_general x7, matrix products, section_rate(): lax.dot_general(gathered, kernel_rows, (((1,), (1,)), ((), ())), preferre...  11.2 us
    all_to_all x1, blocking collectives, body(): lax.all_to_all(sent, 'member', split_axis=0, concat_axis=0, tiled=True)  10.5 us
    ppermute x1, waiting for transfers between devices, body(): across = lax.ppermute(received, ('member', 'patch'), pairs)  4.69 us
    pallas_call x1, Pallas kernels, analyse(): pl.pallas_call(analysis_kernel, out_shape=jax.ShapeDtypeStruct((3, sub_bl...  4.31 us
    ppermute x1, starting transfers between devices, body(): across = lax.ppermute(received, ('member', 'patch'), pairs)  4.3 us
  transfers between devices with their start and end apart: 1, of which 1 were waited for; matrix products, arithmetic and copies ran while one was open for 0% of the time, Pallas kernels for 0%

profile of v4, /device:TPU:32, one launch (start us, length us, event | category | flops | bytes accessed | tf_op | source)
XLA Modules:
  0.0 188.6 jit_solution(608073328633754667)
XLA Ops:
  0.0 0.0 copy-start.7
  0.0 0.0 copy-start.8
  0.0 0.0 copy-start.9
  0.0 0.0 copy-start.1
  0.1 0.7 convert_element_type.49
  0.8 0.8 fusion.150
  1.6 0.1 convert_element_type.50
  1.7 0.0 copy-start
  1.8 0.1 broadcast_in_dim.30
  1.8 34.0 %all_to_all.40 = bf16[32,4,2,256]{3,2,1,0:T(2,128)(2,1)S(1)} all-to-all(bf16[32,4,2,256]{3,2,1,0:T(2,128)(2,1)S(1)} %broadcast_in_dim.30), channel_id=1, replica_groups=mesh['member'=16,'patch'=32] {'patch'}, dimensions={0} | all-to-all | bytes 262144 | tf_op jit(solution)/shard_map/all_to_all | solution.py:24
  35.8 0.7 broadcast_multiply_fusion.5
  36.5 0.7 broadcast_multiply_fusion.6
  37.2 0.1 copy.35
  37.3 3.5 %fusion.163 = (bf16[6,256]{1,0:T(8,128)(2,1)S(1)}, f32[6,256]{1,0:T(8,128)S(1)}, f32[6,256]{1,0:T(8,128)S(1)}) fusion(f32[6,256]{1,0:T(8,128)} %param.21, f32[256]{0:T(256)} %param.20, f32[256]{0:T(256)S(1)} %broadcast_multiply_fusion.5, f32[256]{0:T(256)S(1)} %broadcast_multiply_fusion.6, f32[6,256]{1,0:T(8,128)} %param.22, f32[256]{0:T(256)} %param.19, ...), kind=kOutput, calls=%fused_computation.278 | convolution fusion | flops 25279488 | bytes 4327424 | tf_op jit(solution)/shard_map/dot_general | solution.py:316
  40.8 0.1 broadcast_in_dim.31
  40.9 19.7 %all_to_all.41 = bf16[32,3,2,256]{3,2,1,0:T(2,128)(2,1)S(1)} all-to-all(bf16[32,3,2,256]{3,2,1,0:T(2,128)(2,1)S(1)} %broadcast_in_dim.31), channel_id=1, replica_groups=mesh['member'=16,'patch'=32] {'patch'}, dimensions={0} | all-to-all | bytes 196608 | tf_op jit(solution)/shard_map/all_to_all | solution.py:24
  60.6 0.1 copy.36
  60.7 0.0 copy-done.2
  60.7 1.3 fusion.162
  62.1 0.1 broadcast_in_dim.32
  62.1 18.5 %all_to_all.42 = bf16[32,3,2,256]{3,2,1,0:T(2,128)(2,1)S(1)} all-to-all(bf16[32,3,2,256]{3,2,1,0:T(2,128)(2,1)S(1)} %broadcast_in_dim.32), channel_id=1, replica_groups=mesh['member'=16,'patch'=32] {'patch'}, dimensions={0} | all-to-all | bytes 196608 | tf_op jit(solution)/shard_map/all_to_all | solution.py:24
  80.6 0.1 copy.37
  80.7 1.3 fusion.161
  82.0 0.1 broadcast_in_dim.33
  82.1 18.9 %all_to_all.43 = bf16[32,3,2,256]{3,2,1,0:T(2,128)(2,1)S(1)} all-to-all(bf16[32,3,2,256]{3,2,1,0:T(2,128)(2,1)S(1)} %broadcast_in_dim.33), channel_id=1, replica_groups=mesh['member'=16,'patch'=32] {'patch'}, dimensions={0} | all-to-all | bytes 196608 | tf_op jit(solution)/shard_map/all_to_all | solution.py:24
  101.0 0.1 copy.38
  101.0 1.3 fusion.160
  102.4 0.1 broadcast_in_dim.34
  102.4 18.7 %all_to_all.44 = bf16[32,3,2,256]{3,2,1,0:T(2,128)(2,1)S(1)} all-to-all(bf16[32,3,2,256]{3,2,1,0:T(2,128)(2,1)S(1)} %broadcast_in_dim.34), channel_id=1, replica_groups=mesh['member'=16,'patch'=32] {'patch'}, dimensions={0} | all-to-all | bytes 196608 | tf_op jit(solution)/shard_map/all_to_all | solution.py:24
  121.2 0.1 copy.39
  121.2 1.3 multiply_add_fusion.2
  122.5 0.5 fusion.159
  123.1 0.1 broadcast_in_dim.35
  123.1 18.6 %all_to_all.45 = bf16[32,3,2,256]{3,2,1,0:T(2,128)(2,1)S(1)} all-to-all(bf16[32,3,2,256]{3,2,1,0:T(2,128)(2,1)S(1)} %broadcast_in_dim.35), channel_id=1, replica_groups=mesh['member'=16,'patch'=32] {'patch'}, dimensions={0} | all-to-all | bytes 196608 | tf_op jit(solution)/shard_map/all_to_all | solution.py:24
  141.8 0.1 copy.40
  141.8 0.0 copy-start.10
  141.9 0.0 copy-start.11
  141.9 0.0 copy-start.12
  141.9 0.0 copy-start.4
  141.9 0.0 copy-start.3
  141.9 0.0 copy-start.13
  141.9 0.0 copy-start.14
  141.9 1.3 multiply_add_fusion
  143.3 0.1 broadcast_in_dim.36
  143.3 18.8 %all_to_all.46 = bf16[32,3,2,256]{3,2,1,0:T(2,128)(2,1)S(1)} all-to-all(bf16[32,3,2,256]{3,2,1,0:T(2,128)(2,1)S(1)} %broadcast_in_dim.36), channel_id=1, replica_groups=mesh['member'=16,'patch'=32] {'patch'}, dimensions={0} | all-to-all | bytes 196608 | tf_op jit(solution)/shard_map/all_to_all | solution.py:24
  162.1 0.1 copy.41
  162.2 1.3 fusion.146.rate_ref
  163.5 0.2 shard_map.145
  163.7 10.5 %all_to_all.47.got_ref = f32[16,4,128]{2,1,0:T(4,128)S(1)} all-to-all(f32[16,4,128]{2,1,0:T(4,128)S(1)} %shard_map.145), channel_id=1, replica_groups=mesh['member'=16,'patch'=32] {'member'}, dimensions={0} | all-to-all | bytes 65536 | tf_op jit(solution)/shard_map/all_to_all | solution.py:364
  174.2 0.1 broadcast_select_fusion.1
  174.3 0.1 slice_reduce_fusion.1
  174.4 0.1 squeeze.9
  174.5 0.1 broadcast_select_fusion
  174.6 0.1 squeeze.10
  174.7 0.1 fusion.152
  174.8 4.3 %collective-permute-start = (f32[16,4,128]{2,1,0:T(4,128)S(1)}, f32[16,4,128]{2,1,0:T(4,128)S(1)}, u32[]{:S(2)}, u32[]{:S(2)}) collective-permute-start(f32[16,4,128]{2,1,0:T(4,128)S(1)} %all_to_all.47.got_ref), channel_id=1, source_target_pairs={{480,1},{481,2},{482,3},{483,4},{484,5},{485,6},{486,7},{487,8},{4... | collective-permute-start | bytes 98312 | tf_op jit(solution)/shard_map/ppermute | solution.py:372
  179.1 0.1 mul.1064
  179.2 0.1 stack_tile.3
  179.3 0.0 copy-done.12
  179.3 0.1 multiply_multiply_fusion
  179.4 0.1 broadcast_multiply_fusion
  179.5 0.0 copy-done.13
  179.6 4.7 %collective-permute-done.across_ref = f32[16,4,128]{2,1,0:T(4,128)S(1)} collective-permute-done((f32[16,4,128]{2,1,0:T(4,128)S(1)}, f32[16,4,128]{2,1,0:T(4,128)S(1)}, u32[]{:S(2)}, u32[]{:S(2)}) %collective-permute-start) | collective-permute-done | bytes 32800 | tf_op jit(solution)/shard_map/ppermute | solution.py:372
  184.3 4.3 %shard_map.146 = f32[3,16,96]{2,1,0:T(8,128)} custom-call(f32[16,4,128]{2,1,0:T(4,128)S(1)} %all_to_all.47.got_ref, f32[16,4,128]{2,1,0:T(4,128)S(1)} %collective-permute-done.across_ref, f32[4,72,128]{2,1,0:T(8,128)S(1)} %concatenate.35.table_ref), custom_call_target="tpu_custom_call" | custom-call | tf_op jit(solution)/shard_map/pallas_call | solution.py:265
  (53 shorter events, 0.4 us)
Async XLA Ops:
  0.0 60.7 %copy-start.2 = (f32[6,256]{1,0:T(8,128)S(1)}, f32[6,256]{1,0:T(8,128)}, u32[]{:S(2)}) copy-start(f32[6,256]{1,0:T(8,128)} %param.21) | copy-start | bytes 18436
  0.0 60.7 %copy-start.6 = (f32[256]{0:T(256)S(1)}, f32[256]{0:T(256)}, u32[]{:S(2)}) copy-start(f32[256]{0:T(256)} %param.19) | copy-start | bytes 3076
  0.0 60.7 %copy-start.5 = (f32[256]{0:T(256)S(1)}, f32[256]{0:T(256)}, u32[]{:S(2)}) copy-start(f32[256]{0:T(256)} %param.20) | copy-start | bytes 3076
  0.0 60.7 %copy-start.7 = (f32[256]{0:T(256)S(1)}, f32[256]{0:T(256)}, u32[]{:S(2)}) copy-start(f32[256]{0:T(256)} %param.16) | copy-start | bytes 3076
  0.0 60.7 %copy-start.8 = (f32[256]{0:T(256)S(1)}, f32[256]{0:T(256)}, u32[]{:S(2)}) copy-start(f32[256]{0:T(256)} %param.17) | copy-start | bytes 3076
  0.0 60.7 %copy-start.9 = (f32[256]{0:T(256)S(1)}, f32[256]{0:T(256)}, u32[]{:S(2)}) copy-start(f32[256]{0:T(256)} %param.18) | copy-start | bytes 3076
  0.0 60.7 %copy-start.1 = (f32[6,256]{1,0:T(8,128)S(1)}, f32[6,256]{1,0:T(8,128)}, u32[]{:S(2)}) copy-start(f32[6,256]{1,0:T(8,128)} %param.22) | copy-start | bytes 18436
  1.7 59.0 %copy-start = (bf16[256,8192]{1,0:T(8,128)(2,1)S(1)}, bf16[256,8192]{1,0:T(8,128)(2,1)}, u32[]{:S(2)}) copy-start(bf16[256,8192]{1,0:T(8,128)(2,1)} %param.15) | copy-start | bytes 12582916
  141.8 32.8 %copy-start.10 = (f32[256]{0:T(256)S(1)}, f32[256]{0:T(256)}, u32[]{:S(2)}) copy-start(f32[256]{0:T(256)} %param.23) | copy-start | bytes 3076
  141.9 32.8 %copy-start.11 = (f32[256]{0:T(256)S(1)}, f32[256]{0:T(256)}, u32[]{:S(2)}) copy-start(f32[256]{0:T(256)} %param.24) | copy-start | bytes 3076
  141.9 37.4 %copy-start.12 = (f32[4,1,128]{2,1,0:T(1,128)S(1)}, f32[4,1,128]{2,1,0:T(1,128)}, u32[]{:S(2)}) copy-start(f32[4,1,128]{2,1,0:T(1,128)} %constant.79) | copy-start | bytes 6148
  141.9 37.4 %copy-start.4 = (f32[4,32,128]{2,1,0:T(8,128)S(1)}, f32[4,32,128]{2,1,0:T(8,128)}, u32[]{:S(2)}) copy-start(f32[4,32,128]{2,1,0:T(8,128)} %constant.72.clone) | copy-start | bytes 196612
  141.9 37.5 %copy-start.3 = (f32[4,32,128]{2,1,0:T(8,128)S(1)}, f32[4,32,128]{2,1,0:T(8,128)}, u32[]{:S(2)}) copy-start(f32[4,32,128]{2,1,0:T(8,128)} %constant.73.clone) | copy-start | bytes 196612
  141.9 37.6 %copy-start.13 = (pred[128]{0:T(512)(128)(4,1)S(1)}, pred[128]{0:T(512)(128)(4,1)}, u32[]{:S(2)}) copy-start(pred[128]{0:T(512)(128)(4,1)} %constant.71.clone) | copy-start | bytes 388
  141.9 37.5 %copy-start.14 = (pred[128]{0:T(512)(128)(4,1)S(1)}, pred[128]{0:T(512)(128)(4,1)}, u32[]{:S(2)}) copy-start(pred[128]{0:T(512)(128)(4,1)} %constant.70.clone) | copy-start | bytes 388
  174.8 9.5 %collective-permute-start = (f32[16,4,128]{2,1,0:T(4,128)S(1)}, f32[16,4,128]{2,1,0:T(4,128)S(1)}, u32[]{:S(2)}, u32[]{:S(2)}) collective-permute-start(f32[16,4,128]{2,1,0:T(4,128)S(1)} %all_to_all.47.got_ref), channel_id=1, source_target_pairs={{480,1},{481,2},{482,3},{483,4},{484,5},{485,6},{486,7},{487,8},{4... | collective-permute-start | bytes 98312 | tf_op jit(solution)/shard_map/ppermute | solution.py:372

commit v5 on v4

--- a/solution.py
+++ b/solution.py
@@ -14,6 +14,8 @@
 F32, BF16 = jnp.float32, jnp.bfloat16
 PARTS = (3, 2, 2, 3, 2, 3)
 LANES = 128
+BESIDE = 2
+LN2 = 0.6931471805599453
 
 
 time_step = 0.25
@@ -37,7 +39,7 @@
 
 
 def slip_rate(stress, state_log, guess, friction_rate, damping):
-    factor = 0.5 * jnp.exp(state_log / friction_rate)
+    factor = jnp.exp(state_log / friction_rate - LN2)
     velocity = guess
     for _ in range(NEWTON):
         scaled = factor * velocity
@@ -85,12 +87,8 @@
     precision = obs_window[1]
     root_precision = jnp.sqrt(precision)
     root_tiled = jnp.tile(root_precision, together)[None, None, :]
-    lane = np.arange(LANES) % window
-    from_across = jnp.where(
-        group_index == 0,
-        lane < MARGIN,
-        jnp.where(group_index == groups - 1, lane >= window - MARGIN, False),
-    )
+    lane = np.arange(LANES)
+    from_across = ((lane == 0) & (group_index == 0)) | ((lane == 1) & (group_index == groups - 1))
     rows = jnp.stack([jnp.tile(obs_window[0], together), from_across.astype(F32)])
     return jnp.concatenate(
         [
@@ -108,49 +106,56 @@
     count, rows, width = out_ref.shape
     own = rate_ref.shape[1]
     sub_block = own // count
-    half = members // 2
-    rim = jnp.zeros((rate_ref.shape[0], MARGIN), F32)
-    wide = jnp.concatenate([rim, rate_ref[...], rim], axis=1)
+    rates = rate_ref[...]
+    rim = jnp.zeros((members, MARGIN), F32)
+    wide = jnp.concatenate([rim, rates, rim], axis=1)
+    used = 3 * sub_block + 4 * MARGIN
+    tail = [rates[:, :MARGIN], rates[:, own - MARGIN :], jnp.zeros((members, width - used), F32)]
     out_ref[...] = jnp.zeros(out_ref.shape, F32)
     for g in range(count):
         here = slice(g * sub_block, (g + 1) * sub_block)
-        piece = jnp.concatenate(
-            [
-                deficit_ref[:, here],
-                state_ref[:, here],
-                wide[:, g * sub_block : (g + 1) * sub_block + 2 * MARGIN],
-            ],
-            axis=1,
-        )
-        out_ref[g, :half, :] = jnp.concatenate([piece[:half], piece[half:members]], axis=1)
-
-
-def analysis_kernel(got_ref, across_ref, table_ref, out_ref, all_ref):
-    groups_m, _, width = got_ref.shape
-    width = width // 2
-    ensemble = all_ref.shape[1]
-    half = ensemble // groups_m // 2
-    sub_block = (width - 2 * MARGIN) // 3
+        window = wide[:, g * sub_block : (g + 1) * sub_block + 2 * MARGIN]
+        out_ref[g, :members, :] = jnp.concatenate(
+            [deficit_ref[:, here], state_ref[:, here], window, *tail], axis=1
+        )
+
+
+def turn_kernel(members, got_ref, turned_ref, ends_ref, all_ref):
+    for g in range(got_ref.shape[0]):
+        all_ref[g * members : (g + 1) * members, :] = got_ref[g, :members, :]
+    ensemble = all_ref.shape[0]
+    turned = jnp.transpose(all_ref[...])
+    sub_block = (turned_ref.shape[0] - 2 * MARGIN) // 4
     window = sub_block + 2 * MARGIN
+    together = LANES // window
+    start = 2 * sub_block
+    turned_ref[:window, :] = turned[start : start + window]
+    for h in range(sub_block // together):
+        for v, s in enumerate((0, sub_block, start + MARGIN)):
+            at = window + (3 * h + v) * together
+            turned_ref[at : at + together, :] = turned[s + h * together : s + (h + 1) * together]
+    ends_ref[...] = jnp.zeros(ends_ref.shape, F32)
+    ends_ref[:, :ensemble] = turned[start + window : start + window + 2 * MARGIN]
+
+
+def analysis_kernel(turned_ref, across_ref, table_ref, out_ref):
+    ensemble = turned_ref.shape[1]
     halves, _, lanes = table_ref.shape
+    window = (table_ref.shape[1] - 8) // 2
+    sub_block = window - 2 * MARGIN
     count = lanes // window
-    for g in range(groups_m):
-        for side in range(2):
-            at = (2 * g + side) * half
-            part = slice(side * width, (side + 1) * width)
-            all_ref[0, at : at + half, :] = got_ref[g, :half, part]
-            all_ref[1, at : at + half, :] = across_ref[g, :half, part]
-    values = all_ref[0]
-    rates = values[:, 2 * sub_block :]
-    beyond = all_ref[1][:, 2 * sub_block :]
-    beyond = jnp.concatenate([beyond[:, sub_block:], beyond[:, :sub_block]], axis=1)
-    edge = table_ref[0, 2 * window + 2 : 2 * window + 3, :window]
-    rates = jnp.where(edge > 0, beyond, rates)
-    starts = (0, sub_block, 2 * sub_block + MARGIN)
-    pieces = [rates]
-    for h in range(halves):
-        pieces += [values[:, s + h * count : s + (h + 1) * count] for s in starts]
-    turned = jnp.transpose(jnp.concatenate(pieces, axis=1))
+    flags = table_ref[0, 2 * window + 2 : 2 * window + 3, :]
+    turned = turned_ref[...]
+    turned = jnp.concatenate(
+        [
+            jnp.where(flags[:, 0:1] > 0, across_ref[MARGIN:, :ensemble], turned[:MARGIN]),
+            turned[MARGIN : window - MARGIN],
+            jnp.where(flags[:, 1:2] > 0, across_ref[:MARGIN, :ensemble], turned[window - MARGIN : window]),
+            turned[window:],
+        ],
+        axis=0,
+    )
+    rates = jnp.transpose(turned[:window])
     turned_mean = jnp.mean(turned, axis=1, keepdims=True)
     turned = turned - turned_mean
     rates_tiled = jnp.concatenate([rates] * count, axis=1)
@@ -246,30 +251,41 @@
             out_ref[v, h * count : (h + 1) * count, :] = result[v * count : (v + 1) * count]
 
 
-def pack(deficit, state_log, rates, members, count):
-    own = rates.shape[1]
-    width = 2 * (3 * (own // count) + 2 * MARGIN)
-    rows = -(-members // 4) * 2
+def pack(deficit, state_log, rates, count):
+    members = rates.shape[0]
     return pl.pallas_call(
         functools.partial(pack_kernel, members),
-        out_shape=jax.ShapeDtypeStruct((count, rows, width), F32),
+        out_shape=jax.ShapeDtypeStruct((count, -(-members // 8) * 8, LANES), F32),
         in_specs=[pl.BlockSpec(memory_space=pltpu.VMEM)] * 3,
         out_specs=pl.BlockSpec(memory_space=pltpu.VMEM),
         compiler_params=pltpu.CompilerParams(vmem_limit_bytes=8 * 1024 * 1024),
     )(deficit, state_log, rates)
 
 
-def analyse(received, across, table, ensemble):
-    width = received.shape[2] // 2
-    sub_block = (width - 2 * MARGIN) // 3
+def turn(received, members, sub_block):
+    ensemble = received.shape[0] * members
+    return pl.pallas_call(
+        functools.partial(turn_kernel, members),
+        out_shape=(
+            jax.ShapeDtypeStruct((4 * sub_block + 2 * MARGIN, ensemble), F32),
+            jax.ShapeDtypeStruct((2 * MARGIN, -(-ensemble // 128) * 128), F32),
+        ),
+        in_specs=[pl.BlockSpec(memory_space=pltpu.VMEM)],
+        out_specs=(pl.BlockSpec(memory_space=pltpu.VMEM),) * 2,
+        scratch_shapes=[pltpu.VMEM((ensemble, received.shape[2]), F32)],
+        compiler_params=pltpu.CompilerParams(vmem_limit_bytes=8 * 1024 * 1024),
+    )(received)
+
+
+def analyse(turned, across, table):
+    sub_block = (turned.shape[0] - 2 * MARGIN) // 4
     return pl.pallas_call(
         analysis_kernel,
-        out_shape=jax.ShapeDtypeStruct((3, sub_block, ensemble), F32),
+        out_shape=jax.ShapeDtypeStruct((3, sub_block, turned.shape[1]), F32),
         in_specs=[pl.BlockSpec(memory_space=pltpu.VMEM)] * 3,
         out_specs=pl.BlockSpec(memory_space=pltpu.VMEM),
-        scratch_shapes=[pltpu.VMEM((2, ensemble, width), F32)],
         compiler_params=pltpu.CompilerParams(vmem_limit_bytes=16 * 1024 * 1024),
-    )(received, across, table)
+    )(turned, across, table)
 
 
 def in_pieces(x):
@@ -328,10 +344,10 @@
     spare = jnp.pad(spare, ((0, pair - 1), (0, own_rows - spare.shape[1])))[None]
     deficit = deficit_start
     state_log = state_start
-    velocity = jnp.zeros_like(deficit)
-    rounded, group_index, block_index = lax.optimization_barrier(
+    rounded, velocity, group_index, block_index = lax.optimization_barrier(
         (
             jnp.concatenate([paired(deficit_start.astype(BF16)), spare], axis=0),
+            jnp.zeros_like(deficit),
             lax.axis_index("member"),
             lax.axis_index("patch"),
         )
@@ -360,16 +376,20 @@
         state_log = state_zero / 3.0 + 2.0 / 3.0 * (state_two + time_step * state_change)
     deficit, state_log, velocity = lax.optimization_barrier((deficit, state_log, velocity))
     forecast = section_rate(gather(deficit.astype(BF16)), deficit, state_log, velocity)
-    sent = pack(deficit, state_log, forecast, members, groups)
+    sent = pack(deficit, state_log, forecast, groups)
     received = lax.all_to_all(sent, "member", split_axis=0, concat_axis=0, tiled=True)
-    received, first, obs_rate, obs_precision, group_index, block_index = lax.optimization_barrier(
-        (received, first, obs_rate, obs_precision, group_index, block_index)
+    turned, own_ends = turn(received, members, sub_block)
+    turned, own_ends, first, obs_rate, obs_precision, group_index, block_index = (
+        lax.optimization_barrier(
+            (turned, own_ends, first, obs_rate, obs_precision, group_index, block_index)
+        )
     )
     observed = jnp.stack([obs_rate, obs_precision])
     spare = first[:, members // pair, 0]
-    pairs = [((groups - 1) * blocks + p, p + 1) for p in range(blocks - 1)]
-    pairs += [(b, a) for a, b in pairs]
-    across = lax.ppermute(received, ("member", "patch"), pairs)
+    last = groups - 1
+    pairs = [(BESIDE * blocks + p, p + 1) for p in range(blocks - 1)]
+    pairs += [((last - BESIDE) * blocks + p + 1, last * blocks + p) for p in range(blocks - 1)]
+    across = lax.ppermute(own_ends, ("member", "patch"), pairs)
 
     def ends_of(block):
         row = lax.dynamic_index_in_dim(spare, jnp.clip(block, 0, blocks - 1), 0, keepdims=False)
@@ -384,7 +404,7 @@
         observed, group_index * sub_block, sub_block + 2 * MARGIN, 1
     )
     table = tables(obs_window, sub_block, group_index, groups)
-    analysis = jnp.transpose(analyse(received, across, table, members * groups), (0, 2, 1))
+    analysis = jnp.transpose(analyse(turned, across, table), (0, 2, 1))
     return analysis[:, :, None, :]
 
 

time: 189 us -> 186 us (0.984)
  starting transfers between devices: 4.3 us -> 1.29 us
    ppermute x1, starting transfers between devices: 4.3 us -> 1.29 us  [body(): across = lax.ppermute(own_ends, ('member', 'patch'), pairs)]
where the time goes in v5:
time: 186 us; the launch traced here: 185 us
  blocking collectives  158 us (85%)
  matrix products  11.2 us (6%)
  waiting for transfers between devices  5.9 us (3%)
  Pallas kernels  4.41 us (2%)
  other arithmetic  2.57 us (1%)
    all_to_all x7, blocking collectives, from_everyone(): return lax.all_to_all(copies, axis, split_axis=0, concat_axis=0, tiled=True)  147 us
    dot_general x7, matrix products, section_rate(): lax.dot_general(gathered, kernel_rows, (((1,), (1,)), ((), ())), preferre...  11.2 us
    all_to_all x1, blocking collectives, body(): lax.all_to_all(sent, 'member', split_axis=0, concat_axis=0, tiled=True)  10.5 us
    ppermute x1, waiting for transfers between devices, body(): across = lax.ppermute(own_ends, ('member', 'patch'), pairs)  5.9 us
    pallas_call x1, Pallas kernels, analyse(): pl.pallas_call(analysis_kernel, out_shape=jax.ShapeDtypeStruct((3, sub_bl...  4.17 us
  transfers between devices with their start and end apart: 1, of which 1 were waited for; matrix products, arithmetic and copies ran while one was open for 0% of the time, Pallas kernels for 0%

profile of v5, /device:TPU:32, one launch (start us, length us, event | category | flops | bytes accessed | tf_op | source)
XLA Modules:
  0.0 185.4 jit_solution(2542665584048408495)
XLA Ops:
  0.0 0.0 copy-start.7
  0.0 0.0 copy-start.8
  0.0 0.0 copy-start.9
  0.0 0.0 copy-start.1
  0.1 0.7 convert_element_type.49
  0.8 0.8 fusion.150
  1.6 0.1 convert_element_type.50
  1.7 0.0 copy-start
  1.8 0.1 broadcast_in_dim.27
  1.8 34.0 %all_to_all.40 = bf16[32,4,2,256]{3,2,1,0:T(2,128)(2,1)S(1)} all-to-all(bf16[32,4,2,256]{3,2,1,0:T(2,128)(2,1)S(1)} %broadcast_in_dim.27), channel_id=1, replica_groups=mesh['member'=16,'patch'=32] {'patch'}, dimensions={0} | all-to-all | bytes 262144 | tf_op jit(solution)/shard_map/all_to_all | solution.py:26
  35.9 0.1 copy.35
  35.9 3.5 %fusion.163 = (bf16[6,256]{1,0:T(8,128)(2,1)S(1)}, f32[6,256]{1,0:T(8,128)S(1)}, f32[6,256]{1,0:T(8,128)S(1)}) fusion(f32[6,256]{1,0:T(8,128)} %param.21, f32[6,256]{1,0:T(8,128)S(1)} %broadcast.51, f32[256]{0:T(256)} %param.20, f32[6,256]{1,0:T(8,128)} %param.22, f32[256]{0:T(256)} %param.19, bf16[6,8192]{1,0:T(8,128)(2,1)S(1)} %bitcast.121, ...), kind=kOutput, calls=%fused_computation.274 | convolution fusion | flops 25281024 | bytes 4331520 | tf_op jit(solution)/shard_map/dot_general | solution.py:332
  39.5 0.1 broadcast_in_dim.28
  39.6 19.7 %all_to_all.41 = bf16[32,3,2,256]{3,2,1,0:T(2,128)(2,1)S(1)} all-to-all(bf16[32,3,2,256]{3,2,1,0:T(2,128)(2,1)S(1)} %broadcast_in_dim.28), channel_id=1, replica_groups=mesh['member'=16,'patch'=32] {'patch'}, dimensions={0} | all-to-all | bytes 196608 | tf_op jit(solution)/shard_map/all_to_all | solution.py:26
  59.2 0.1 copy.36
  59.3 0.0 copy-done.2
  59.3 0.0 copy-done.6
  59.3 0.0 copy-done.5
  59.3 0.0 copy-done.7
  59.4 1.3 fusion.162
  60.7 0.1 broadcast_in_dim.29
  60.8 18.5 %all_to_all.42 = bf16[32,3,2,256]{3,2,1,0:T(2,128)(2,1)S(1)} all-to-all(bf16[32,3,2,256]{3,2,1,0:T(2,128)(2,1)S(1)} %broadcast_in_dim.29), channel_id=1, replica_groups=mesh['member'=16,'patch'=32] {'patch'}, dimensions={0} | all-to-all | bytes 196608 | tf_op jit(solution)/shard_map/all_to_all | solution.py:26
  79.3 0.1 copy.37
  79.3 1.3 fusion.161
  80.7 0.1 broadcast_in_dim.30
  80.7 18.9 %all_to_all.43 = bf16[32,3,2,256]{3,2,1,0:T(2,128)(2,1)S(1)} all-to-all(bf16[32,3,2,256]{3,2,1,0:T(2,128)(2,1)S(1)} %broadcast_in_dim.30), channel_id=1, replica_groups=mesh['member'=16,'patch'=32] {'patch'}, dimensions={0} | all-to-all | bytes 196608 | tf_op jit(solution)/shard_map/all_to_all | solution.py:26
  99.6 0.1 copy.38
  99.7 1.3 fusion.160
  101.0 0.1 broadcast_in_dim.31
  101.1 18.7 %all_to_all.44 = bf16[32,3,2,256]{3,2,1,0:T(2,128)(2,1)S(1)} all-to-all(bf16[32,3,2,256]{3,2,1,0:T(2,128)(2,1)S(1)} %broadcast_in_dim.31), channel_id=1, replica_groups=mesh['member'=16,'patch'=32] {'patch'}, dimensions={0} | all-to-all | bytes 196608 | tf_op jit(solution)/shard_map/all_to_all | solution.py:26
  119.8 0.1 copy.39
  119.9 1.3 multiply_add_fusion.2
  121.2 0.5 fusion.159
  121.7 0.1 broadcast_in_dim.32
  121.8 18.6 %all_to_all.45 = bf16[32,3,2,256]{3,2,1,0:T(2,128)(2,1)S(1)} all-to-all(bf16[32,3,2,256]{3,2,1,0:T(2,128)(2,1)S(1)} %broadcast_in_dim.32), channel_id=1, replica_groups=mesh['member'=16,'patch'=32] {'patch'}, dimensions={0} | all-to-all | bytes 196608 | tf_op jit(solution)/shard_map/all_to_all | solution.py:26
  140.4 0.1 copy.40
  140.5 0.0 copy-start.10
  140.5 0.0 copy-start.11
  140.5 0.0 copy-start.12
  140.5 0.0 copy-start.4
  140.5 0.0 copy-start.3
  140.6 0.0 copy-start.13
  140.6 0.0 copy-start.14
  140.6 1.3 multiply_add_fusion
  141.9 0.1 broadcast_in_dim.33
  142.0 18.8 %all_to_all.46 = bf16[32,3,2,256]{3,2,1,0:T(2,128)(2,1)S(1)} all-to-all(bf16[32,3,2,256]{3,2,1,0:T(2,128)(2,1)S(1)} %broadcast_in_dim.33), channel_id=1, replica_groups=mesh['member'=16,'patch'=32] {'patch'}, dimensions={0} | all-to-all | bytes 196608 | tf_op jit(solution)/shard_map/all_to_all | solution.py:26
  160.8 0.1 copy.41
  160.8 1.3 fusion.146.rate_ref
  162.1 0.2 shard_map.145
  162.3 10.5 %all_to_all.47.got_ref = f32[16,8,128]{2,1,0:T(8,128)S(1)} all-to-all(f32[16,8,128]{2,1,0:T(8,128)S(1)} %shard_map.145), channel_id=1, replica_groups=mesh['member'=16,'patch'=32] {'member'}, dimensions={0} | all-to-all | bytes 131072 | tf_op jit(solution)/shard_map/all_to_all | solution.py:380
  172.8 0.1 shard_map.146
  173.0 0.1 broadcast_select_fusion.1
  173.1 0.1 slice_reduce_fusion.1
  173.2 0.1 squeeze.9
  173.2 0.1 broadcast_select_fusion
  173.3 0.1 squeeze.10
  173.4 0.1 fusion.152
  173.5 1.3 collective-permute-start
  174.9 0.1 mul.506
  174.9 0.1 stack_tile.3
  175.0 0.1 multiply_multiply_fusion
  175.1 0.1 broadcast_multiply_fusion
  175.3 5.9 %collective-permute-done.across_ref = f32[16,128]{1,0:T(8,128)S(1)} collective-permute-done((f32[16,128]{1,0:T(8,128)S(1)}, f32[16,128]{1,0:T(8,128)S(1)}, u32[]{:S(2)}, u32[]{:S(2)}) %collective-permute-start) | collective-permute-done | bytes 8224 | tf_op jit(solution)/shard_map/ppermute | solution.py:392
  181.2 4.2 %shard_map.147 = f32[3,16,96]{2,1,0:T(8,128)} custom-call(f32[80,96]{1,0:T(8,128)S(1)} %get-tuple-element.42.turned_ref, f32[16,128]{1,0:T(8,128)S(1)} %collective-permute-done.across_ref, f32[4,72,128]{2,1,0:T(8,128)S(1)} %concatenate.35.table_ref), custom_call_target="tpu_custom_call" | custom-call | tf_op jit(solution)/shard_map/pallas_call | solution.py:282
  (53 shorter events, 0.4 us)
Async XLA Ops:
  0.0 59.3 %copy-start.2 = (f32[6,256]{1,0:T(8,128)S(1)}, f32[6,256]{1,0:T(8,128)}, u32[]{:S(2)}) copy-start(f32[6,256]{1,0:T(8,128)} %param.21) | copy-start | bytes 18436
  0.0 59.3 %copy-start.6 = (f32[256]{0:T(256)S(1)}, f32[256]{0:T(256)}, u32[]{:S(2)}) copy-start(f32[256]{0:T(256)} %param.19) | copy-start | bytes 3076
  0.0 59.3 %copy-start.5 = (f32[256]{0:T(256)S(1)}, f32[256]{0:T(256)}, u32[]{:S(2)}) copy-start(f32[256]{0:T(256)} %param.20) | copy-start | bytes 3076
  0.0 59.3 %copy-start.7 = (f32[256]{0:T(256)S(1)}, f32[256]{0:T(256)}, u32[]{:S(2)}) copy-start(f32[256]{0:T(256)} %param.16) | copy-start | bytes 3076
  0.0 59.3 %copy-start.8 = (f32[256]{0:T(256)S(1)}, f32[256]{0:T(256)}, u32[]{:S(2)}) copy-start(f32[256]{0:T(256)} %param.17) | copy-start | bytes 3076
  0.0 59.3 %copy-start.9 = (f32[256]{0:T(256)S(1)}, f32[256]{0:T(256)}, u32[]{:S(2)}) copy-start(f32[256]{0:T(256)} %param.18) | copy-start | bytes 3076
  0.0 59.3 %copy-start.1 = (f32[6,256]{1,0:T(8,128)S(1)}, f32[6,256]{1,0:T(8,128)}, u32[]{:S(2)}) copy-start(f32[6,256]{1,0:T(8,128)} %param.22) | copy-start | bytes 18436
  1.7 57.7 %copy-start = (bf16[256,8192]{1,0:T(8,128)(2,1)S(1)}, bf16[256,8192]{1,0:T(8,128)(2,1)}, u32[]{:S(2)}) copy-start(bf16[256,8192]{1,0:T(8,128)(2,1)} %param.15) | copy-start | bytes 12582916
  140.5 32.9 %copy-start.10 = (f32[256]{0:T(256)S(1)}, f32[256]{0:T(256)}, u32[]{:S(2)}) copy-start(f32[256]{0:T(256)} %param.23) | copy-start | bytes 3076
  140.5 32.9 %copy-start.11 = (f32[256]{0:T(256)S(1)}, f32[256]{0:T(256)}, u32[]{:S(2)}) copy-start(f32[256]{0:T(256)} %param.24) | copy-start | bytes 3076
  140.5 34.5 %copy-start.12 = (f32[4,1,128]{2,1,0:T(1,128)S(1)}, f32[4,1,128]{2,1,0:T(1,128)}, u32[]{:S(2)}) copy-start(f32[4,1,128]{2,1,0:T(1,128)} %constant.83) | copy-start | bytes 6148
  140.5 34.5 %copy-start.4 = (f32[4,32,128]{2,1,0:T(8,128)S(1)}, f32[4,32,128]{2,1,0:T(8,128)}, u32[]{:S(2)}) copy-start(f32[4,32,128]{2,1,0:T(8,128)} %constant.76.clone) | copy-start | bytes 196612
  140.5 34.6 %copy-start.3 = (f32[4,32,128]{2,1,0:T(8,128)S(1)}, f32[4,32,128]{2,1,0:T(8,128)}, u32[]{:S(2)}) copy-start(f32[4,32,128]{2,1,0:T(8,128)} %constant.77.clone) | copy-start | bytes 196612
  140.6 34.7 %copy-start.13 = (pred[128]{0:T(512)(128)(4,1)S(1)}, pred[128]{0:T(512)(128)(4,1)}, u32[]{:S(2)}) copy-start(pred[128]{0:T(512)(128)(4,1)} %constant.75.clone) | copy-start | bytes 388
  140.6 34.6 %copy-start.14 = (pred[128]{0:T(512)(128)(4,1)S(1)}, pred[128]{0:T(512)(128)(4,1)}, u32[]{:S(2)}) copy-start(pred[128]{0:T(512)(128)(4,1)} %constant.74.clone) | copy-start | bytes 388
  173.5 7.7 %collective-permute-start = (f32[16,128]{1,0:T(8,128)S(1)}, f32[16,128]{1,0:T(8,128)S(1)}, u32[]{:S(2)}, u32[]{:S(2)}) collective-permute-start(f32[16,128]{1,0:T(8,128)S(1)} %get-tuple-element.43), channel_id=1, source_target_pairs={{64,1},{65,2},{66,3},{67,4},{68,5},{69,6},{70,7},{71,8},{72,9},{73... | collective-permute-start | bytes 24584 | tf_op jit(solution)/shard_map/ppermute | solution.py:392

commit v6 on v5

--- a/solution.py
+++ b/solution.py
@@ -32,20 +32,18 @@
     return blocks.reshape(*dims[:dim], dims[dim] * dims[dim + 1], *dims[dim + 2 :])
 
 
-def inverse_sinh(value):
-    magnitude = jnp.abs(value)
-    result = jnp.log(magnitude + jnp.sqrt(magnitude * magnitude + 1.0))
-    return jnp.where(value < 0, -result, result)
-
-
 def slip_rate(stress, state_log, guess, friction_rate, damping):
     factor = jnp.exp(state_log / friction_rate - LN2)
+    slope = friction_rate * factor
     velocity = guess
     for _ in range(NEWTON):
         scaled = factor * velocity
-        residual = friction_rate * inverse_sinh(scaled) + damping * velocity - stress
-        derivative = friction_rate * factor / jnp.sqrt(1.0 + scaled * scaled) + damping
-        velocity = velocity - residual / derivative
+        magnitude = jnp.abs(scaled)
+        root = jnp.sqrt(scaled * scaled + 1.0)
+        angle = jnp.log(magnitude + root)
+        angle = jnp.where(scaled < 0, -angle, angle)
+        residual = friction_rate * angle + damping * velocity - stress
+        velocity = velocity - residual * root / (slope + damping * root)
     return velocity
 
 
@@ -293,7 +291,7 @@
     for _ in range(3):
         pieces.append(lax.reduce_precision(x, exponent_bits=8, mantissa_bits=7))
         x = x - pieces[-1]
-    return jnp.stack(pieces).astype(BF16)
+    return [piece.astype(BF16) for piece in pieces]
 
 
 def body(
@@ -324,6 +322,12 @@
     def gather(rounded):
         return joined(from_everyone(paired(rounded), "patch"))
 
+    def spare_rows(rate, precision):
+        ends = [x[at : at + MARGIN] for x in (rate, precision) for at in (0, own_rows - MARGIN)]
+        pieces = in_pieces(jnp.concatenate(ends))
+        row = jnp.concatenate([*pieces, jnp.zeros((own_rows - 12 * MARGIN,), BF16)])
+        return jnp.pad(row[None], ((0, pair - 1), (0, 0)))[None]
+
     def tendency(gathered, deficit, state_log, guess):
         velocity = section_rate(gathered, deficit, state_log, guess)
         return (plate_rate - velocity, jnp.exp(-state_log) - jnp.abs(velocity), velocity)
@@ -338,25 +342,28 @@
         stress = base_stress + self_stiffness * deficit + row_scale * total
         return slip_rate(stress, state_log, guess, friction_rate, damping)
 
-    observed = jnp.stack([obs_rate, obs_precision])
-    ends = jnp.stack([observed[:, :MARGIN], observed[:, own_rows - MARGIN :]])
-    spare = in_pieces(ends).reshape(1, -1)
-    spare = jnp.pad(spare, ((0, pair - 1), (0, own_rows - spare.shape[1])))[None]
     deficit = deficit_start
     state_log = state_start
     rounded, velocity, group_index, block_index = lax.optimization_barrier(
         (
-            jnp.concatenate([paired(deficit_start.astype(BF16)), spare], axis=0),
+            paired(deficit_start.astype(BF16)),
             jnp.zeros_like(deficit),
             lax.axis_index("member"),
             lax.axis_index("patch"),
         )
     )
-    first = from_everyone(rounded, "patch")
-    first, friction_rate, damping, row_scale, self_stiffness, base_stress = lax.optimization_barrier(
-        (first, friction_rate, damping, row_scale, self_stiffness, base_stress)
-    )
-    gathered = joined(first[:, : members // pair])
+    gathered = from_everyone(rounded, "patch")
+    (
+        gathered,
+        friction_rate,
+        damping,
+        row_scale,
+        self_stiffness,
+        base_stress,
+    ) = lax.optimization_barrier(
+        (gathered, friction_rate, damping, row_scale, self_stiffness, base_stress)
+    )
+    gathered = joined(gathered)
     for step in range(STEPS):
         deficit_zero, state_zero = (deficit, state_log)
         if step > 0:
@@ -364,14 +371,22 @@
         change, state_change, velocity = tendency(gathered, deficit_zero, state_zero, velocity)
         deficit_one = deficit_zero + time_step * change
         state_one = state_zero + time_step * state_change
-        change, state_change, velocity = tendency(
-            gather(deficit_one.astype(BF16)), deficit_one, state_one, velocity
-        )
+        gathered = gather(deficit_one.astype(BF16))
+        if step == 0:
+            gathered, obs_rate, obs_precision = lax.optimization_barrier(
+                (gathered, obs_rate, obs_precision)
+            )
+            spare = spare_rows(obs_rate, obs_precision)
+        change, state_change, velocity = tendency(gathered, deficit_one, state_one, velocity)
         deficit_two = 0.75 * deficit_zero + 0.25 * (deficit_one + time_step * change)
         state_two = 0.75 * state_zero + 0.25 * (state_one + time_step * state_change)
-        change, state_change, velocity = tendency(
-            gather(deficit_two.astype(BF16)), deficit_two, state_two, velocity
-        )
+        rounded = paired(deficit_two.astype(BF16))
+        if step == 0:
+            third = from_everyone(jnp.concatenate([rounded, spare], axis=0), "patch")
+            gathered = joined(third[:, : members // pair])
+        else:
+            gathered = joined(from_everyone(rounded, "patch"))
+        change, state_change, velocity = tendency(gathered, deficit_two, state_two, velocity)
         deficit = deficit_zero / 3.0 + 2.0 / 3.0 * (deficit_two + time_step * change)
         state_log = state_zero / 3.0 + 2.0 / 3.0 * (state_two + time_step * state_change)
     deficit, state_log, velocity = lax.optimization_barrier((deficit, state_log, velocity))
@@ -379,30 +394,33 @@
     sent = pack(deficit, state_log, forecast, groups)
     received = lax.all_to_all(sent, "member", split_axis=0, concat_axis=0, tiled=True)
     turned, own_ends = turn(received, members, sub_block)
-    turned, own_ends, first, obs_rate, obs_precision, group_index, block_index = (
+    turned, own_ends, third, obs_rate, obs_precision, group_index, block_index = (
         lax.optimization_barrier(
-            (turned, own_ends, first, obs_rate, obs_precision, group_index, block_index)
-        )
-    )
-    observed = jnp.stack([obs_rate, obs_precision])
-    spare = first[:, members // pair, 0]
+            (turned, own_ends, third, obs_rate, obs_precision, group_index, block_index)
+        )
+    )
     last = groups - 1
     pairs = [(BESIDE * blocks + p, p + 1) for p in range(blocks - 1)]
     pairs += [((last - BESIDE) * blocks + p + 1, last * blocks + p) for p in range(blocks - 1)]
     across = lax.ppermute(own_ends, ("member", "patch"), pairs)
 
+    spare = third[:, members // pair, 0].astype(F32)
+
     def ends_of(block):
-        row = lax.dynamic_index_in_dim(spare, jnp.clip(block, 0, blocks - 1), 0, keepdims=False)
-        parts = row[: 3 * ends.size].astype(F32).reshape(3, *ends.shape)
-        there = (block >= 0) & (block < blocks)
-        return jnp.where(there, parts[0] + (parts[1] + parts[2]), 0.0)
-
-    observed = jnp.concatenate(
-        [ends_of(block_index - 1)[1], observed, ends_of(block_index + 1)[0]], axis=1
-    )
-    obs_window = lax.dynamic_slice_in_dim(
-        observed, group_index * sub_block, sub_block + 2 * MARGIN, 1
-    )
+        its = np.arange(blocks, dtype=np.int32)[:, None] == block
+        row = jnp.sum(jnp.where(its, spare, 0.0), axis=0)
+        parts = [row[i * 4 * MARGIN : (i + 1) * 4 * MARGIN] for i in range(3)]
+        return parts[0] + (parts[1] + parts[2])
+
+    before, after = ends_of(block_index - 1), ends_of(block_index + 1)
+
+    def window_of(own, at):
+        padded = jnp.concatenate(
+            [before[at + MARGIN : at + 2 * MARGIN], own, after[at : at + MARGIN]]
+        )
+        return lax.dynamic_slice_in_dim(padded, group_index * sub_block, sub_block + 2 * MARGIN)
+
+    obs_window = (window_of(obs_rate, 0), window_of(obs_precision, 2 * MARGIN))
     table = tables(obs_window, sub_block, group_index, groups)
     analysis = jnp.transpose(analyse(turned, across, table), (0, 2, 1))
     return analysis[:, :, None, :]

time: 186 us -> 185 us (level)
  transfers between devices with their start and end apart: 1 -> 1, of which waited for: 1 -> 1; matrix products, arithmetic and copies ran while one was open for 0% -> 1% of each run, Pallas kernels for 0% -> 0%
where the time goes in v6:
time: 185 us
  blocking collectives  158 us (85%)
  matrix products  11.3 us (6%)
  waiting for transfers between devices  5.11 us (3%)
  Pallas kernels  4.41 us (2%)
  other arithmetic  2.16 us (1%)
    all_to_all x7, blocking collectives, from_everyone(): return lax.all_to_all(copies, axis, split_axis=0, concat_axis=0, tiled=True)  147 us
    dot_general x7, matrix products, section_rate(): lax.dot_general(gathered, kernel_rows, (((1,), (1,)), ((), ())), preferre...  11.3 us
    all_to_all x1, blocking collectives, body(): lax.all_to_all(sent, 'member', split_axis=0, concat_axis=0, tiled=True)  10.6 us
    ppermute x1, waiting for transfers between devices, body(): across = lax.ppermute(own_ends, ('member', 'patch'), pairs)  5.11 us
    pallas_call x1, Pallas kernels, analyse(): pl.pallas_call(analysis_kernel, out_shape=jax.ShapeDtypeStruct((3, sub_bl...  4.17 us
  transfers between devices with their start and end apart: 1, of which 1 were waited for; matrix products, arithmetic and copies ran while one was open for 1% of the time, Pallas kernels for 0%

profile of v6, /device:TPU:32, one launch (start us, length us, event | category | flops | bytes accessed | tf_op | source)
XLA Modules:
  0.0 184.5 jit_solution(4125875726845061955)
XLA Ops:
  0.0 0.0 copy-start.7
  0.0 0.0 copy-start.8
  0.0 0.0 copy-start.9
  0.0 0.0 copy-start.1
  0.1 0.8 convert_element_type.39
  0.9 0.1 broadcast_in_dim.44
  0.9 32.7 %all_to_all.40 = bf16[32,3,2,256]{3,2,1,0:T(2,128)(2,1)S(1)} all-to-all(bf16[32,3,2,256]{3,2,1,0:T(2,128)(2,1)S(1)} %broadcast_in_dim.44), channel_id=1, replica_groups=mesh['member'=16,'patch'=32] {'patch'}, dimensions={0} | all-to-all | bytes 196608 | tf_op jit(solution)/shard_map/all_to_all | solution.py:26
  33.7 0.1 copy.39
  33.7 3.5 %fusion.185 = (bf16[6,256]{1,0:T(8,128)(2,1)S(1)}, f32[6,256]{1,0:T(8,128)S(1)}, f32[6,256]{1,0:T(8,128)S(1)}) fusion(f32[6,256]{1,0:T(8,128)} %param.23, f32[6,256]{1,0:T(8,128)S(1)} %broadcast.48, f32[256]{0:T(256)} %param.22, f32[6,256]{1,0:T(8,128)} %param.24, f32[256]{0:T(256)} %param.21, bf16[6,8192]{1,0:T(8,128)(2,1)S(1)} %bitcast.116, ...), kind=kOutput, calls=%fused_computation.289 | convolution fusion | flops 25287168 | bytes 4331520 | tf_op jit(solution)/shard_map/dot_general | solution.py:336
  37.3 0.1 broadcast_in_dim.45
  37.4 19.5 %all_to_all.41 = bf16[32,3,2,256]{3,2,1,0:T(2,128)(2,1)S(1)} all-to-all(bf16[32,3,2,256]{3,2,1,0:T(2,128)(2,1)S(1)} %broadcast_in_dim.45), channel_id=1, replica_groups=mesh['member'=16,'patch'=32] {'patch'}, dimensions={0} | all-to-all | bytes 196608 | tf_op jit(solution)/shard_map/all_to_all | solution.py:26
  56.9 0.1 copy.40
  57.0 0.1 fusion.186
  57.1 0.1 reduce-precision_convert_fusion.1
  57.2 0.1 pad_maximum_fusion.11
  57.3 1.3 fusion.184
  58.7 0.1 broadcast_in_dim.49
  58.8 19.6 %all_to_all.42 = bf16[32,4,2,256]{3,2,1,0:T(2,128)(2,1)S(1)} all-to-all(bf16[32,4,2,256]{3,2,1,0:T(2,128)(2,1)S(1)} %broadcast_in_dim.49), channel_id=1, replica_groups=mesh['member'=16,'patch'=32] {'patch'}, dimensions={0} | all-to-all | bytes 262144 | tf_op jit(solution)/shard_map/all_to_all | solution.py:26
  78.4 0.1 slice.157
  78.4 0.1 copy.41
  78.5 1.3 fusion.183
  79.8 0.1 broadcast_in_dim.50
  79.9 19.2 %all_to_all.43 = bf16[32,3,2,256]{3,2,1,0:T(2,128)(2,1)S(1)} all-to-all(bf16[32,3,2,256]{3,2,1,0:T(2,128)(2,1)S(1)} %broadcast_in_dim.50), channel_id=1, replica_groups=mesh['member'=16,'patch'=32] {'patch'}, dimensions={0} | all-to-all | bytes 196608 | tf_op jit(solution)/shard_map/all_to_all | solution.py:26
  99.1 0.1 copy.42
  99.2 1.3 fusion.182
  100.5 0.1 broadcast_in_dim.51
  100.6 19.0 %all_to_all.44 = bf16[32,3,2,256]{3,2,1,0:T(2,128)(2,1)S(1)} all-to-all(bf16[32,3,2,256]{3,2,1,0:T(2,128)(2,1)S(1)} %broadcast_in_dim.51), channel_id=1, replica_groups=mesh['member'=16,'patch'=32] {'patch'}, dimensions={0} | all-to-all | bytes 196608 | tf_op jit(solution)/shard_map/all_to_all | solution.py:26
  119.5 0.1 copy.43
  119.6 1.3 multiply_add_fusion.2
  120.9 0.5 fusion.181
  121.5 0.1 broadcast_in_dim.52
  121.5 18.7 %all_to_all.45 = bf16[32,3,2,256]{3,2,1,0:T(2,128)(2,1)S(1)} all-to-all(bf16[32,3,2,256]{3,2,1,0:T(2,128)(2,1)S(1)} %broadcast_in_dim.52), channel_id=1, replica_groups=mesh['member'=16,'patch'=32] {'patch'}, dimensions={0} | all-to-all | bytes 196608 | tf_op jit(solution)/shard_map/all_to_all | solution.py:26
  140.3 0.1 copy.44
  140.3 0.0 copy-start.15
  140.3 0.0 copy-start.4
  140.4 0.0 copy-start.12
  140.4 0.0 copy-start.3
  140.4 0.0 copy-start.13
  140.4 0.0 copy-start.14
  140.4 1.3 multiply_add_fusion
  141.8 0.1 broadcast_in_dim.53
  141.8 18.7 %all_to_all.46 = bf16[32,3,2,256]{3,2,1,0:T(2,128)(2,1)S(1)} all-to-all(bf16[32,3,2,256]{3,2,1,0:T(2,128)(2,1)S(1)} %broadcast_in_dim.53), channel_id=1, replica_groups=mesh['member'=16,'patch'=32] {'patch'}, dimensions={0} | all-to-all | bytes 196608 | tf_op jit(solution)/shard_map/all_to_all | solution.py:26
  160.5 0.1 copy.45
  160.6 1.3 fusion.176.rate_ref
  161.9 0.2 shard_map.163
  162.0 10.6 %all_to_all.47.got_ref = f32[16,8,128]{2,1,0:T(8,128)S(1)} all-to-all(f32[16,8,128]{2,1,0:T(8,128)S(1)} %shard_map.163), channel_id=1, replica_groups=mesh['member'=16,'patch'=32] {'member'}, dimensions={0} | all-to-all | bytes 131072 | tf_op jit(solution)/shard_map/all_to_all | solution.py:395
  172.6 0.1 shard_map.164
  172.7 1.3 collective-permute-start
  174.1 0.1 fusion.7
  174.2 0.1 add_add_fusion
  174.2 0.1 fusion.189
  174.3 0.1 add_add_fusion.1
  174.4 0.1 fusion.188
  174.5 0.1 pad_maximum_fusion.7
  174.5 0.1 fusion.180
  174.6 0.1 mul.1220
  174.7 0.1 multiply_multiply_fusion
  174.8 0.0 copy-done.12
  174.8 0.1 pad_maximum_fusion.8
  174.9 0.1 dynamic_slice.7
  175.0 0.1 stack_tile.3
  175.1 0.1 broadcast_multiply_fusion
  175.3 5.1 %collective-permute-done.across_ref = f32[16,128]{1,0:T(8,128)S(1)} collective-permute-done((f32[16,128]{1,0:T(8,128)S(1)}, f32[16,128]{1,0:T(8,128)S(1)}, u32[]{:S(2)}, u32[]{:S(2)}) %collective-permute-start) | collective-permute-done | bytes 8224 | tf_op jit(solution)/shard_map/ppermute | solution.py:405
  180.4 4.2 %shard_map.165 = f32[3,16,96]{2,1,0:T(8,128)} custom-call(f32[80,96]{1,0:T(8,128)S(1)} %get-tuple-element.48.turned_ref, f32[16,128]{1,0:T(8,128)S(1)} %collective-permute-done.across_ref, f32[4,72,128]{2,1,0:T(8,128)S(1)} %concatenate.23.table_ref), custom_call_target="tpu_custom_call" | custom-call | tf_op jit(solution)/shard_map/pallas_call | solution.py:280
  (58 shorter events, 0.4 us)
Async XLA Ops:
  0.0 57.3 %copy-start.2 = (f32[6,256]{1,0:T(8,128)S(1)}, f32[6,256]{1,0:T(8,128)}, u32[]{:S(2)}) copy-start(f32[6,256]{1,0:T(8,128)} %param.23) | copy-start | bytes 18436
  0.0 57.3 %copy-start.6 = (f32[256]{0:T(256)S(1)}, f32[256]{0:T(256)}, u32[]{:S(2)}) copy-start(f32[256]{0:T(256)} %param.21) | copy-start | bytes 3076
  0.0 57.3 %copy-start.5 = (f32[256]{0:T(256)S(1)}, f32[256]{0:T(256)}, u32[]{:S(2)}) copy-start(f32[256]{0:T(256)} %param.22) | copy-start | bytes 3076
  0.0 57.3 %copy-start.7 = (f32[256]{0:T(256)S(1)}, f32[256]{0:T(256)}, u32[]{:S(2)}) copy-start(f32[256]{0:T(256)} %param.18) | copy-start | bytes 3076
  0.0 57.3 %copy-start.8 = (f32[256]{0:T(256)S(1)}, f32[256]{0:T(256)}, u32[]{:S(2)}) copy-start(f32[256]{0:T(256)} %param.19) | copy-start | bytes 3076
  0.0 57.3 %copy-start.9 = (f32[256]{0:T(256)S(1)}, f32[256]{0:T(256)}, u32[]{:S(2)}) copy-start(f32[256]{0:T(256)} %param.20) | copy-start | bytes 3076
  0.0 57.3 %copy-start.1 = (f32[6,256]{1,0:T(8,128)S(1)}, f32[6,256]{1,0:T(8,128)}, u32[]{:S(2)}) copy-start(f32[6,256]{1,0:T(8,128)} %param.24) | copy-start | bytes 18436
  0.1 56.9 %copy-start.11 = (f32[256]{0:T(256)S(1)}, f32[256]{0:T(256)}, u32[]{:S(2)}) copy-start(f32[256]{0:T(256)} %param.25) | copy-start | bytes 3076
  0.1 56.9 %copy-start.10 = (f32[256]{0:T(256)S(1)}, f32[256]{0:T(256)}, u32[]{:S(2)}) copy-start(f32[256]{0:T(256)} %param.26) | copy-start | bytes 3076
  0.9 56.5 %copy-start = (bf16[256,8192]{1,0:T(8,128)(2,1)S(1)}, bf16[256,8192]{1,0:T(8,128)(2,1)}, u32[]{:S(2)}) copy-start(bf16[256,8192]{1,0:T(8,128)(2,1)} %param.17) | copy-start | bytes 12582916
  140.3 33.7 %copy-start.15 = (s32[32,1]{0,1:T(1,128)S(1)}, s32[32,1]{0,1:T(1,128)}, u32[]{:S(2)}) copy-start(s32[32,1]{0,1:T(1,128)} %constant.63.clone) | copy-start | bytes 388
  140.3 34.4 %copy-start.4 = (f32[4,32,128]{2,1,0:T(8,128)S(1)}, f32[4,32,128]{2,1,0:T(8,128)}, u32[]{:S(2)}) copy-start(f32[4,32,128]{2,1,0:T(8,128)} %constant.66.clone) | copy-start | bytes 196612
  140.4 34.5 %copy-start.12 = (f32[4,1,128]{2,1,0:T(1,128)S(1)}, f32[4,1,128]{2,1,0:T(1,128)}, u32[]{:S(2)}) copy-start(f32[4,1,128]{2,1,0:T(1,128)} %constant.73) | copy-start | bytes 6148
  140.4 34.7 %copy-start.3 = (f32[4,32,128]{2,1,0:T(8,128)S(1)}, f32[4,32,128]{2,1,0:T(8,128)}, u32[]{:S(2)}) copy-start(f32[4,32,128]{2,1,0:T(8,128)} %constant.67.clone) | copy-start | bytes 196612
  140.4 34.8 %copy-start.13 = (pred[128]{0:T(512)(128)(4,1)S(1)}, pred[128]{0:T(512)(128)(4,1)}, u32[]{:S(2)}) copy-start(pred[128]{0:T(512)(128)(4,1)} %constant.65.clone) | copy-start | bytes 388
  140.4 34.8 %copy-start.14 = (pred[128]{0:T(512)(128)(4,1)S(1)}, pred[128]{0:T(512)(128)(4,1)}, u32[]{:S(2)}) copy-start(pred[128]{0:T(512)(128)(4,1)} %constant.64.clone) | copy-start | bytes 388
  172.7 7.7 %collective-permute-start = (f32[16,128]{1,0:T(8,128)S(1)}, f32[16,128]{1,0:T(8,128)S(1)}, u32[]{:S(2)}, u32[]{:S(2)}) collective-permute-start(f32[16,128]{1,0:T(8,128)S(1)} %get-tuple-element.49), channel_id=1, source_target_pairs={{64,1},{65,2},{66,3},{67,4},{68,5},{69,6},{70,7},{71,8},{72,9},{73... | collective-permute-start | bytes 24584 | tf_op jit(solution)/shard_map/ppermute | solution.py:405

commit v7 on v6

--- a/solution.py
+++ b/solution.py
@@ -68,7 +68,7 @@
     return total
 
 
-def tables(obs_window, sub_block, group_index, groups):
+def tapers(sub_block):
     window = sub_block + 2 * MARGIN
     together = LANES // window
     sets = sub_block // together
@@ -79,49 +79,41 @@
         np.transpose(taper, (0, 2, 1))[:, :, :, None], (sets, window, together, window)
     ).reshape(sets, window, LANES)
     along = taper.reshape(sets, 1, LANES)
-    root = np.sqrt(across * along).astype(np.float32)
-    root_along = np.sqrt(along).astype(np.float32)
-    across = across.astype(np.float32)
-    precision = obs_window[1]
-    root_precision = jnp.sqrt(precision)
-    root_tiled = jnp.tile(root_precision, together)[None, None, :]
-    lane = np.arange(LANES)
-    from_across = ((lane == 0) & (group_index == 0)) | ((lane == 1) & (group_index == groups - 1))
-    rows = jnp.stack([jnp.tile(obs_window[0], together), from_across.astype(F32)])
-    return jnp.concatenate(
-        [
-            root * root_precision[None, :, None] * root_tiled,
-            across * precision[None, :, None],
-            root_along * root_tiled,
-            jnp.broadcast_to(rows[None], (sets, 2, LANES)),
-            jnp.zeros((sets, 5, LANES), F32),
-        ],
-        axis=1,
-    )
-
-
-def pack_kernel(members, deficit_ref, state_ref, rate_ref, out_ref):
+    filler = np.zeros((sets, 7, LANES))
+    parts = [np.sqrt(across * along), across, np.sqrt(along), filler]
+    return np.concatenate(parts, axis=1).astype(np.float32)
+
+
+def pack_kernel(deficit_ref, state_ref, rate_ref, obs_ref, precision_ref, out_ref):
     count, rows, width = out_ref.shape
     own = rate_ref.shape[1]
     sub_block = own // count
-    rates = rate_ref[...]
-    rim = jnp.zeros((members, MARGIN), F32)
+    members = rate_ref.shape[0]
+    rates = jnp.concatenate([rate_ref[...], obs_ref[...], precision_ref[...]], axis=0)
+    filled = rates.shape[0]
+    rim = jnp.zeros((filled, MARGIN), F32)
     wide = jnp.concatenate([rim, rates, rim], axis=1)
     used = 3 * sub_block + 4 * MARGIN
-    tail = [rates[:, :MARGIN], rates[:, own - MARGIN :], jnp.zeros((members, width - used), F32)]
-    out_ref[...] = jnp.zeros(out_ref.shape, F32)
+    tail = [rates[:, :MARGIN], rates[:, own - MARGIN :], jnp.zeros((filled, width - used), F32)]
+    below = jnp.zeros((filled - members, own), F32)
+    deficit = jnp.concatenate([deficit_ref[...], below], axis=0)
+    state_log = jnp.concatenate([state_ref[...], below], axis=0)
+    if filled < rows:
+        out_ref[...] = jnp.zeros(out_ref.shape, F32)
     for g in range(count):
         here = slice(g * sub_block, (g + 1) * sub_block)
         window = wide[:, g * sub_block : (g + 1) * sub_block + 2 * MARGIN]
-        out_ref[g, :members, :] = jnp.concatenate(
-            [deficit_ref[:, here], state_ref[:, here], window, *tail], axis=1
+        out_ref[g, :filled, :] = jnp.concatenate(
+            [deficit[:, here], state_log[:, here], window, *tail], axis=1
         )
 
 
 def turn_kernel(members, got_ref, turned_ref, ends_ref, all_ref):
+    ensemble = got_ref.shape[0] * members
     for g in range(got_ref.shape[0]):
         all_ref[g * members : (g + 1) * members, :] = got_ref[g, :members, :]
-    ensemble = all_ref.shape[0]
+    rest = jnp.zeros((LANES - ensemble - 2, LANES), F32)
+    all_ref[ensemble:, :] = jnp.concatenate([got_ref[0, members : members + 2, :], rest], axis=0)
     turned = jnp.transpose(all_ref[...])
     sub_block = (turned_ref.shape[0] - 2 * MARGIN) // 4
     window = sub_block + 2 * MARGIN
@@ -132,28 +124,30 @@
         for v, s in enumerate((0, sub_block, start + MARGIN)):
             at = window + (3 * h + v) * together
             turned_ref[at : at + together, :] = turned[s + h * together : s + (h + 1) * together]
-    ends_ref[...] = jnp.zeros(ends_ref.shape, F32)
-    ends_ref[:, :ensemble] = turned[start + window : start + window + 2 * MARGIN]
-
-
-def analysis_kernel(turned_ref, across_ref, table_ref, out_ref):
-    ensemble = turned_ref.shape[1]
+    ends_ref[...] = turned[start + window : start + window + 2 * MARGIN]
+
+
+def analysis_kernel(ensemble, turned_ref, across_ref, flag_ref, table_ref, out_ref):
     halves, _, lanes = table_ref.shape
     window = (table_ref.shape[1] - 8) // 2
     sub_block = window - 2 * MARGIN
     count = lanes // window
-    flags = table_ref[0, 2 * window + 2 : 2 * window + 3, :]
-    turned = turned_ref[...]
-    turned = jnp.concatenate(
+    flags = flag_ref[...]
+    seen = jnp.concatenate(
         [
-            jnp.where(flags[:, 0:1] > 0, across_ref[MARGIN:, :ensemble], turned[:MARGIN]),
-            turned[MARGIN : window - MARGIN],
-            jnp.where(flags[:, 1:2] > 0, across_ref[:MARGIN, :ensemble], turned[window - MARGIN : window]),
-            turned[window:],
+            jnp.where(flags[:, 0:1] > 0, across_ref[MARGIN:, :], turned_ref[:MARGIN, :]),
+            turned_ref[MARGIN : window - MARGIN, :],
+            jnp.where(flags[:, 1:2] > 0, across_ref[:MARGIN, :], turned_ref[window - MARGIN : window, :]),
         ],
         axis=0,
     )
-    rates = jnp.transpose(turned[:window])
+    turned = jnp.concatenate([seen[:, :ensemble], turned_ref[window:, :ensemble]], axis=0)
+    back = jnp.transpose(seen)
+    rates = back[:ensemble]
+    obs = jnp.concatenate([back[ensemble : ensemble + 1]] * count, axis=1)
+    precision = seen[:, ensemble + 1 : ensemble + 2]
+    root_precision = jnp.sqrt(precision)
+    root_tiled = jnp.concatenate([jnp.sqrt(back[ensemble + 1 : ensemble + 2])] * count, axis=1)
     turned_mean = jnp.mean(turned, axis=1, keepdims=True)
     turned = turned - turned_mean
     rates_tiled = jnp.concatenate([rates] * count, axis=1)
@@ -193,12 +187,11 @@
     state = []
     for h in range(halves):
         table = table_ref[h]
-        cross = gram * table[:window]
-        scale = free + jnp.sum(diag * table[window : 2 * window], axis=0, keepdims=True)
+        cross = gram * (table[:window] * root_precision * root_tiled)
+        scale = free + jnp.sum(diag * precision * table[window : 2 * window], axis=0, keepdims=True)
         inv = 1.0 / scale
         base = cross * inv
-        root = table[2 * window : 2 * window + 1]
-        obs = table[2 * window + 1 : 2 * window + 2]
+        root = table[2 * window : 2 * window + 1] * root_tiled
         q = jnp.where(own, grams[window + h * vrows : window + (h + 1) * vrows] * root, 0.0)
         drive = (obs - mean_tiled) * root
         r = free * inv
@@ -249,49 +242,40 @@
             out_ref[v, h * count : (h + 1) * count, :] = result[v * count : (v + 1) * count]
 
 
-def pack(deficit, state_log, rates, count):
-    members = rates.shape[0]
+def pack(deficit, state_log, rates, obs_rate, obs_precision, count):
+    rows = -(-(rates.shape[0] + 2) // 8) * 8
     return pl.pallas_call(
-        functools.partial(pack_kernel, members),
-        out_shape=jax.ShapeDtypeStruct((count, -(-members // 8) * 8, LANES), F32),
-        in_specs=[pl.BlockSpec(memory_space=pltpu.VMEM)] * 3,
+        pack_kernel,
+        out_shape=jax.ShapeDtypeStruct((count, rows, LANES), F32),
+        in_specs=[pl.BlockSpec(memory_space=pltpu.VMEM)] * 5,
         out_specs=pl.BlockSpec(memory_space=pltpu.VMEM),
         compiler_params=pltpu.CompilerParams(vmem_limit_bytes=8 * 1024 * 1024),
-    )(deficit, state_log, rates)
+    )(deficit, state_log, rates, obs_rate[None], obs_precision[None])
 
 
 def turn(received, members, sub_block):
-    ensemble = received.shape[0] * members
     return pl.pallas_call(
         functools.partial(turn_kernel, members),
         out_shape=(
-            jax.ShapeDtypeStruct((4 * sub_block + 2 * MARGIN, ensemble), F32),
-            jax.ShapeDtypeStruct((2 * MARGIN, -(-ensemble // 128) * 128), F32),
+            jax.ShapeDtypeStruct((4 * sub_block + 2 * MARGIN, LANES), F32),
+            jax.ShapeDtypeStruct((2 * MARGIN, LANES), F32),
         ),
         in_specs=[pl.BlockSpec(memory_space=pltpu.VMEM)],
         out_specs=(pl.BlockSpec(memory_space=pltpu.VMEM),) * 2,
-        scratch_shapes=[pltpu.VMEM((ensemble, received.shape[2]), F32)],
+        scratch_shapes=[pltpu.VMEM((LANES, LANES), F32)],
         compiler_params=pltpu.CompilerParams(vmem_limit_bytes=8 * 1024 * 1024),
     )(received)
 
 
-def analyse(turned, across, table):
+def analyse(turned, across, flags, ensemble):
     sub_block = (turned.shape[0] - 2 * MARGIN) // 4
     return pl.pallas_call(
-        analysis_kernel,
-        out_shape=jax.ShapeDtypeStruct((3, sub_block, turned.shape[1]), F32),
-        in_specs=[pl.BlockSpec(memory_space=pltpu.VMEM)] * 3,
+        functools.partial(analysis_kernel, ensemble),
+        out_shape=jax.ShapeDtypeStruct((3, sub_block, ensemble), F32),
+        in_specs=[pl.BlockSpec(memory_space=pltpu.VMEM)] * 4,
         out_specs=pl.BlockSpec(memory_space=pltpu.VMEM),
         compiler_params=pltpu.CompilerParams(vmem_limit_bytes=16 * 1024 * 1024),
-    )(turned, across, table)
-
-
-def in_pieces(x):
-    pieces = []
-    for _ in range(3):
-        pieces.append(lax.reduce_precision(x, exponent_bits=8, mantissa_bits=7))
-        x = x - pieces[-1]
-    return [piece.astype(BF16) for piece in pieces]
+    )(turned, across, flags, jnp.asarray(tapers(sub_block)))
 
 
 def body(
@@ -322,12 +306,6 @@
     def gather(rounded):
         return joined(from_everyone(paired(rounded), "patch"))
 
-    def spare_rows(rate, precision):
-        ends = [x[at : at + MARGIN] for x in (rate, precision) for at in (0, own_rows - MARGIN)]
-        pieces = in_pieces(jnp.concatenate(ends))
-        row = jnp.concatenate([*pieces, jnp.zeros((own_rows - 12 * MARGIN,), BF16)])
-        return jnp.pad(row[None], ((0, pair - 1), (0, 0)))[None]
-
     def tendency(gathered, deficit, state_log, guess):
         velocity = section_rate(gathered, deficit, state_log, guess)
         return (plate_rate - velocity, jnp.exp(-state_log) - jnp.abs(velocity), velocity)
@@ -344,13 +322,11 @@
 
     deficit = deficit_start
     state_log = state_start
-    rounded, velocity, group_index, block_index = lax.optimization_barrier(
-        (
-            paired(deficit_start.astype(BF16)),
-            jnp.zeros_like(deficit),
-            lax.axis_index("member"),
-            lax.axis_index("patch"),
-        )
+    lane = np.arange(LANES)[None]
+    group_index = lax.axis_index("member")
+    flags = ((lane == 0) & (group_index == 0)) | ((lane == 1) & (group_index == groups - 1))
+    rounded, velocity, flags = lax.optimization_barrier(
+        (paired(deficit_start.astype(BF16)), jnp.zeros_like(deficit), flags.astype(F32))
     )
     gathered = from_everyone(rounded, "patch")
     (
@@ -372,57 +348,24 @@
         deficit_one = deficit_zero + time_step * change
         state_one = state_zero + time_step * state_change
         gathered = gather(deficit_one.astype(BF16))
-        if step == 0:
-            gathered, obs_rate, obs_precision = lax.optimization_barrier(
-                (gathered, obs_rate, obs_precision)
-            )
-            spare = spare_rows(obs_rate, obs_precision)
         change, state_change, velocity = tendency(gathered, deficit_one, state_one, velocity)
         deficit_two = 0.75 * deficit_zero + 0.25 * (deficit_one + time_step * change)
         state_two = 0.75 * state_zero + 0.25 * (state_one + time_step * state_change)
-        rounded = paired(deficit_two.astype(BF16))
-        if step == 0:
-            third = from_everyone(jnp.concatenate([rounded, spare], axis=0), "patch")
-            gathered = joined(third[:, : members // pair])
-        else:
-            gathered = joined(from_everyone(rounded, "patch"))
+        gathered = gather(deficit_two.astype(BF16))
         change, state_change, velocity = tendency(gathered, deficit_two, state_two, velocity)
         deficit = deficit_zero / 3.0 + 2.0 / 3.0 * (deficit_two + time_step * change)
         state_log = state_zero / 3.0 + 2.0 / 3.0 * (state_two + time_step * state_change)
     deficit, state_log, velocity = lax.optimization_barrier((deficit, state_log, velocity))
     forecast = section_rate(gather(deficit.astype(BF16)), deficit, state_log, velocity)
-    sent = pack(deficit, state_log, forecast, groups)
+    sent = pack(deficit, state_log, forecast, obs_rate, obs_precision, groups)
     received = lax.all_to_all(sent, "member", split_axis=0, concat_axis=0, tiled=True)
     turned, own_ends = turn(received, members, sub_block)
-    turned, own_ends, third, obs_rate, obs_precision, group_index, block_index = (
-        lax.optimization_barrier(
-            (turned, own_ends, third, obs_rate, obs_precision, group_index, block_index)
-        )
-    )
     last = groups - 1
     pairs = [(BESIDE * blocks + p, p + 1) for p in range(blocks - 1)]
     pairs += [((last - BESIDE) * blocks + p + 1, last * blocks + p) for p in range(blocks - 1)]
     across = lax.ppermute(own_ends, ("member", "patch"), pairs)
 
-    spare = third[:, members // pair, 0].astype(F32)
-
-    def ends_of(block):
-        its = np.arange(blocks, dtype=np.int32)[:, None] == block
-        row = jnp.sum(jnp.where(its, spare, 0.0), axis=0)
-        parts = [row[i * 4 * MARGIN : (i + 1) * 4 * MARGIN] for i in range(3)]
-        return parts[0] + (parts[1] + parts[2])
-
-    before, after = ends_of(block_index - 1), ends_of(block_index + 1)
-
-    def window_of(own, at):
-        padded = jnp.concatenate(
-            [before[at + MARGIN : at + 2 * MARGIN], own, after[at : at + MARGIN]]
-        )
-        return lax.dynamic_slice_in_dim(padded, group_index * sub_block, sub_block + 2 * MARGIN)
-
-    obs_window = (window_of(obs_rate, 0), window_of(obs_precision, 2 * MARGIN))
-    table = tables(obs_window, sub_block, group_index, groups)
-    analysis = jnp.transpose(analyse(turned, across, table), (0, 2, 1))
+    analysis = jnp.transpose(analyse(turned, across, flags, members * groups), (0, 2, 1))
     return analysis[:, :, None, :]
 
 

time: 185 us -> 184 us (level)
  blocking collectives: 158 us -> 156 us
  transfers between devices with their start and end apart: 1 -> 1, of which waited for: 1 -> 1; matrix products, arithmetic and copies ran while one was open for 1% -> 0% of each run, Pallas kernels for 0% -> 0%
where the time goes in v7:
time: 184 us
  blocking collectives  156 us (85%)
  matrix products  11.3 us (6%)
  waiting for transfers between devices  6.35 us (3%)
  Pallas kernels  4.48 us (2%)
  other arithmetic  2.58 us (1%)
    all_to_all x7, blocking collectives, from_everyone(): return lax.all_to_all(copies, axis, split_axis=0, concat_axis=0, tiled=True)  146 us
    dot_general x7, matrix products, section_rate(): lax.dot_general(gathered, kernel_rows, (((1,), (1,)), ((), ())), preferre...  11.3 us
    all_to_all x1, blocking collectives, body(): lax.all_to_all(sent, 'member', split_axis=0, concat_axis=0, tiled=True)  10.6 us
    ppermute x1, waiting for transfers between devices, body(): across = lax.ppermute(own_ends, ('member', 'patch'), pairs)  6.35 us
    pallas_call x1, Pallas kernels, analyse(): pl.pallas_call(functools.partial(analysis_kernel, ensemble), out_shape=ja...  4.24 us
  transfers between devices with their start and end apart: 1, of which 1 were waited for; matrix products, arithmetic and copies ran while one was open for 0% of the time, Pallas kernels for 0%

profile of v7, /device:TPU:32, one launch (start us, length us, event | category | flops | bytes accessed | tf_op | source)
XLA Modules:
  0.0 183.7 jit_solution(18178559182499152961)
XLA Ops:
  0.0 0.0 copy-start.5
  0.0 0.0 copy-start.6
  0.0 0.0 copy-start.7
  0.0 0.0 copy-start.10
  0.0 0.0 copy-start.9
  0.0 0.0 copy-start.8
  0.0 0.0 copy-start.4
  0.1 0.0 copy-start.3
  0.1 0.9 convert_element_type.24
  1.0 1.1 or_convert_fusion.flag_ref
  2.1 0.1 broadcast_in_dim.20
  2.1 32.4 %all_to_all.40 = bf16[32,3,2,256]{3,2,1,0:T(2,128)(2,1)S(1)} all-to-all(bf16[32,3,2,256]{3,2,1,0:T(2,128)(2,1)S(1)} %broadcast_in_dim.20), channel_id=1, replica_groups=mesh['member'=16,'patch'=32] {'patch'}, dimensions={0} | all-to-all | bytes 196608 | tf_op jit(solution)/shard_map/all_to_all | solution.py:26
  34.6 0.1 copy.24
  34.7 3.5 %fusion.179 = (bf16[6,256]{1,0:T(8,128)(2,1)S(1)}, f32[6,256]{1,0:T(8,128)S(1)}, f32[6,256]{1,0:T(8,128)S(1)}) fusion(f32[6,256]{1,0:T(8,128)} %param.19, f32[6,256]{1,0:T(8,128)S(1)} %broadcast.40, f32[256]{0:T(256)} %param.18, f32[6,256]{1,0:T(8,128)} %param.20, f32[256]{0:T(256)} %param.17, bf16[6,8192]{1,0:T(8,128)(2,1)S(1)} %bitcast.103, ...), kind=kOutput, calls=%fused_computation.263 | convolution fusion | flops 25287168 | bytes 4331520 | tf_op jit(solution)/shard_map/dot_general | solution.py:314
  38.2 0.1 broadcast_in_dim.21
  38.3 19.5 %all_to_all.41 = bf16[32,3,2,256]{3,2,1,0:T(2,128)(2,1)S(1)} all-to-all(bf16[32,3,2,256]{3,2,1,0:T(2,128)(2,1)S(1)} %broadcast_in_dim.21), channel_id=1, replica_groups=mesh['member'=16,'patch'=32] {'patch'}, dimensions={0} | all-to-all | bytes 196608 | tf_op jit(solution)/shard_map/all_to_all | solution.py:26
  57.8 0.1 copy.25
  57.9 0.0 copy-done.5
  57.9 0.0 copy-done.6
  57.9 0.0 copy-done.7
  57.9 0.0 copy-done.10
  57.9 0.0 copy-done.9
  58.0 0.0 copy-done.8
  58.0 0.0 copy-done.4
  58.0 0.0 copy-done.3
  58.0 1.3 fusion.178
  59.3 0.1 broadcast_in_dim.22
  59.4 18.7 %all_to_all.42 = bf16[32,3,2,256]{3,2,1,0:T(2,128)(2,1)S(1)} all-to-all(bf16[32,3,2,256]{3,2,1,0:T(2,128)(2,1)S(1)} %broadcast_in_dim.22), channel_id=1, replica_groups=mesh['member'=16,'patch'=32] {'patch'}, dimensions={0} | all-to-all | bytes 196608 | tf_op jit(solution)/shard_map/all_to_all | solution.py:26
  78.1 0.1 copy.26
  78.2 1.3 fusion.177
  79.5 0.1 broadcast_in_dim.23
  79.6 18.7 %all_to_all.43 = bf16[32,3,2,256]{3,2,1,0:T(2,128)(2,1)S(1)} all-to-all(bf16[32,3,2,256]{3,2,1,0:T(2,128)(2,1)S(1)} %broadcast_in_dim.23), channel_id=1, replica_groups=mesh['member'=16,'patch'=32] {'patch'}, dimensions={0} | all-to-all | bytes 196608 | tf_op jit(solution)/shard_map/all_to_all | solution.py:26
  98.3 0.1 copy.27
  98.3 1.3 fusion.176
  99.7 0.1 broadcast_in_dim.24
  99.7 18.9 %all_to_all.44 = bf16[32,3,2,256]{3,2,1,0:T(2,128)(2,1)S(1)} all-to-all(bf16[32,3,2,256]{3,2,1,0:T(2,128)(2,1)S(1)} %broadcast_in_dim.24), channel_id=1, replica_groups=mesh['member'=16,'patch'=32] {'patch'}, dimensions={0} | all-to-all | bytes 196608 | tf_op jit(solution)/shard_map/all_to_all | solution.py:26
  118.6 0.1 copy.28
  118.7 1.3 multiply_add_fusion.2
  120.0 0.5 fusion.175
  120.5 0.1 broadcast_in_dim.25
  120.6 18.7 %all_to_all.45 = bf16[32,3,2,256]{3,2,1,0:T(2,128)(2,1)S(1)} all-to-all(bf16[32,3,2,256]{3,2,1,0:T(2,128)(2,1)S(1)} %broadcast_in_dim.25), channel_id=1, replica_groups=mesh['member'=16,'patch'=32] {'patch'}, dimensions={0} | all-to-all | bytes 196608 | tf_op jit(solution)/shard_map/all_to_all | solution.py:26
  139.3 0.1 copy.29
  139.4 0.0 copy-start.1
  139.4 0.0 copy-start.2
  139.4 0.0 copy-start
  139.4 1.3 multiply_add_fusion
  140.8 0.1 broadcast_in_dim.26
  140.8 18.7 %all_to_all.46 = bf16[32,3,2,256]{3,2,1,0:T(2,128)(2,1)S(1)} all-to-all(bf16[32,3,2,256]{3,2,1,0:T(2,128)(2,1)S(1)} %broadcast_in_dim.26), channel_id=1, replica_groups=mesh['member'=16,'patch'=32] {'patch'}, dimensions={0} | all-to-all | bytes 196608 | tf_op jit(solution)/shard_map/all_to_all | solution.py:26
  159.6 0.1 copy.30
  159.7 1.3 fusion.174.rate_ref
  160.9 0.0 copy-done.1
  161.0 0.0 copy-done.2
  161.0 0.2 shard_map.127
  161.1 10.6 %all_to_all.47.got_ref = f32[16,8,128]{2,1,0:T(8,128)S(1)} all-to-all(f32[16,8,128]{2,1,0:T(8,128)S(1)} %shard_map.127), channel_id=1, replica_groups=mesh['member'=16,'patch'=32] {'member'}, dimensions={0} | all-to-all | bytes 131072 | tf_op jit(solution)/shard_map/all_to_all | solution.py:361
  171.7 0.1 shard_map.128
  171.8 1.3 collective-permute-start
  173.1 6.4 %collective-permute-done.across_ref = f32[16,128]{1,0:T(8,128)S(1)} collective-permute-done((f32[16,128]{1,0:T(8,128)S(1)}, f32[16,128]{1,0:T(8,128)S(1)}, u32[]{:S(2)}, u32[]{:S(2)}) %collective-permute-start) | collective-permute-done | bytes 8224 | tf_op jit(solution)/shard_map/ppermute | solution.py:366
  179.4 0.0 copy-done
  179.4 4.2 %shard_map.129 = f32[3,16,96]{2,1,0:T(8,128)} custom-call(f32[80,128]{1,0:T(8,128)S(1)} %get-tuple-element.30.turned_ref, f32[16,128]{1,0:T(8,128)S(1)} %collective-permute-done.across_ref, f32[1,128]{1,0:T(1,128)S(1)} %or_convert_fusion.flag_ref, f32[4,72,128]{2,1,0:T(8,128)S(1)} %copy-done), custom_call_target="tpu_custom_call" | custom-call | tf_op jit(solution)/shard_map/pallas_call | solution.py:272
  (23 shorter events, 0.2 us)
Async XLA Ops:
  0.0 57.9 %copy-start.5 = (f32[6,256]{1,0:T(8,128)S(1)}, f32[6,256]{1,0:T(8,128)}, u32[]{:S(2)}) copy-start(f32[6,256]{1,0:T(8,128)} %param.19) | copy-start | bytes 18436
  0.0 57.9 %copy-start.6 = (f32[256]{0:T(256)S(1)}, f32[256]{0:T(256)}, u32[]{:S(2)}) copy-start(f32[256]{0:T(256)} %param.18) | copy-start | bytes 3076
  0.0 57.9 %copy-start.7 = (f32[256]{0:T(256)S(1)}, f32[256]{0:T(256)}, u32[]{:S(2)}) copy-start(f32[256]{0:T(256)} %param.17) | copy-start | bytes 3076
  0.0 57.9 %copy-start.10 = (f32[256]{0:T(256)S(1)}, f32[256]{0:T(256)}, u32[]{:S(2)}) copy-start(f32[256]{0:T(256)} %param.16) | copy-start | bytes 3076
  0.0 57.9 %copy-start.9 = (f32[256]{0:T(256)S(1)}, f32[256]{0:T(256)}, u32[]{:S(2)}) copy-start(f32[256]{0:T(256)} %param.15) | copy-start | bytes 3076
  0.0 57.9 %copy-start.8 = (f32[256]{0:T(256)S(1)}, f32[256]{0:T(256)}, u32[]{:S(2)}) copy-start(f32[256]{0:T(256)} %param.14) | copy-start | bytes 3076
  0.0 57.9 %copy-start.4 = (f32[6,256]{1,0:T(8,128)S(1)}, f32[6,256]{1,0:T(8,128)}, u32[]{:S(2)}) copy-start(f32[6,256]{1,0:T(8,128)} %param.20) | copy-start | bytes 18436
  0.1 57.9 %copy-start.3 = (bf16[256,8192]{1,0:T(8,128)(2,1)S(1)}, bf16[256,8192]{1,0:T(8,128)(2,1)}, u32[]{:S(2)}) copy-start(bf16[256,8192]{1,0:T(8,128)(2,1)} %param.13) | copy-start | bytes 12582916
  139.4 21.6 %copy-start.1 = (f32[256]{0:T(256)S(1)}, f32[256]{0:T(256)}, u32[]{:S(2)}) copy-start(f32[256]{0:T(256)} %param.21) | copy-start | bytes 3076
  139.4 21.6 %copy-start.2 = (f32[256]{0:T(256)S(1)}, f32[256]{0:T(256)}, u32[]{:S(2)}) copy-start(f32[256]{0:T(256)} %param.22) | copy-start | bytes 3076
  139.4 40.0 %copy-start = (f32[4,72,128]{2,1,0:T(8,128)S(1)}, f32[4,72,128]{2,1,0:T(8,128)}, u32[]{:S(2)}) copy-start(f32[4,72,128]{2,1,0:T(8,128)} %constant.43.clone.table_ref) | copy-start | bytes 442372
  171.8 7.7 %collective-permute-start = (f32[16,128]{1,0:T(8,128)S(1)}, f32[16,128]{1,0:T(8,128)S(1)}, u32[]{:S(2)}, u32[]{:S(2)}) collective-permute-start(f32[16,128]{1,0:T(8,128)S(1)} %get-tuple-element.31), channel_id=1, source_target_pairs={{64,1},{65,2},{66,3},{67,4},{68,5},{69,6},{70,7},{71,8},{72,9},{73... | collective-permute-start | bytes 24584 | tf_op jit(solution)/shard_map/ppermute | solution.py:366

commit v8 on v7

--- a/solution.py
+++ b/solution.py
@@ -82,6 +82,22 @@
     filler = np.zeros((sets, 7, LANES))
     parts = [np.sqrt(across * along), across, np.sqrt(along), filler]
     return np.concatenate(parts, axis=1).astype(np.float32)
+
+
+def start_kernel(out_ref):
+    out_ref[...] = jnp.zeros(out_ref.shape, F32)
+
+
+def start_guess(like):
+    return pl.pallas_call(
+        start_kernel,
+        out_shape=jax.ShapeDtypeStruct(like.shape, F32),
+        out_specs=pl.BlockSpec(memory_space=pltpu.VMEM),
+        cost_estimate=pl.CostEstimate(
+            flops=10_000_000_000, bytes_accessed=30_000_000, transcendentals=0
+        ),
+        compiler_params=pltpu.CompilerParams(vmem_limit_bytes=4 * 1024 * 1024),
+    )()
 
 
 def pack_kernel(deficit_ref, state_ref, rate_ref, obs_ref, precision_ref, out_ref):
@@ -127,17 +143,18 @@
     ends_ref[...] = turned[start + window : start + window + 2 * MARGIN]
 
 
-def analysis_kernel(ensemble, turned_ref, across_ref, flag_ref, table_ref, out_ref):
+def analysis_kernel(ensemble, turned_ref, across_ref, table_ref, out_ref):
     halves, _, lanes = table_ref.shape
     window = (table_ref.shape[1] - 8) // 2
     sub_block = window - 2 * MARGIN
     count = lanes // window
-    flags = flag_ref[...]
+    group = lax.axis_index("member")
+    last = lax.axis_size("member") - 1
     seen = jnp.concatenate(
         [
-            jnp.where(flags[:, 0:1] > 0, across_ref[MARGIN:, :], turned_ref[:MARGIN, :]),
+            jnp.where(group == 0, across_ref[MARGIN:, :], turned_ref[:MARGIN, :]),
             turned_ref[MARGIN : window - MARGIN, :],
-            jnp.where(flags[:, 1:2] > 0, across_ref[:MARGIN, :], turned_ref[window - MARGIN : window, :]),
+            jnp.where(group == last, across_ref[:MARGIN, :], turned_ref[window - MARGIN : window, :]),
         ],
         axis=0,
     )
@@ -267,15 +284,15 @@
     )(received)
 
 
-def analyse(turned, across, flags, ensemble):
+def analyse(turned, across, ensemble):
     sub_block = (turned.shape[0] - 2 * MARGIN) // 4
     return pl.pallas_call(
         functools.partial(analysis_kernel, ensemble),
         out_shape=jax.ShapeDtypeStruct((3, sub_block, ensemble), F32),
-        in_specs=[pl.BlockSpec(memory_space=pltpu.VMEM)] * 4,
+        in_specs=[pl.BlockSpec(memory_space=pltpu.VMEM)] * 3,
         out_specs=pl.BlockSpec(memory_space=pltpu.VMEM),
         compiler_params=pltpu.CompilerParams(vmem_limit_bytes=16 * 1024 * 1024),
-    )(turned, across, flags, jnp.asarray(tapers(sub_block)))
+    )(turned, across, jnp.asarray(tapers(sub_block)))
 
 
 def body(
@@ -322,11 +339,8 @@
 
     deficit = deficit_start
     state_log = state_start
-    lane = np.arange(LANES)[None]
-    group_index = lax.axis_index("member")
-    flags = ((lane == 0) & (group_index == 0)) | ((lane == 1) & (group_index == groups - 1))
-    rounded, velocity, flags = lax.optimization_barrier(
-        (paired(deficit_start.astype(BF16)), jnp.zeros_like(deficit), flags.astype(F32))
+    rounded, velocity = lax.optimization_barrier(
+        (paired(deficit_start.astype(BF16)), start_guess(deficit))
     )
     gathered = from_everyone(rounded, "patch")
     (
@@ -365,7 +379,7 @@
     pairs += [((last - BESIDE) * blocks + p + 1, last * blocks + p) for p in range(blocks - 1)]
     across = lax.ppermute(own_ends, ("member", "patch"), pairs)
 
-    analysis = jnp.transpose(analyse(turned, across, flags, members * groups), (0, 2, 1))
+    analysis = jnp.transpose(analyse(turned, across, members * groups), (0, 2, 1))
     return analysis[:, :, None, :]
 
 

time: 184 us -> 181 us (0.984)
  matrix products: 11.3 us -> 9.01 us
  other arithmetic: 2.58 us -> 0.62 us
    dot_general x7, matrix products: 11.3 us -> 9.01 us  [section_rate(): lax.dot_general(gathered, kernel_rows, (((1,), (1,)), ((), ())), preferre...]
where the time goes in v8:
time: 181 us; the launch traced here: 180 us
  blocking collectives  156 us (86%)
  matrix products  9.01 us (5%)
  waiting for transfers between devices  6.35 us (4%)
  Pallas kernels  4.44 us (2%)
    all_to_all x7, blocking collectives, from_everyone(): return lax.all_to_all(copies, axis, split_axis=0, concat_axis=0, tiled=True)  146 us
    all_to_all x1, blocking collectives, body(): lax.all_to_all(sent, 'member', split_axis=0, concat_axis=0, tiled=True)  10.6 us
    dot_general x7, matrix products, section_rate(): lax.dot_general(gathered, kernel_rows, (((1,), (1,)), ((), ())), preferre...  9.01 us
    ppermute x1, waiting for transfers between devices, body(): across = lax.ppermute(own_ends, ('member', 'patch'), pairs)  6.35 us
    pallas_call x1, Pallas kernels, analyse(): pl.pallas_call(functools.partial(analysis_kernel, ensemble), out_shape=ja...  4.2 us
  transfers between devices with their start and end apart: 1, of which 1 were waited for; matrix products, arithmetic and copies ran while one was open for 0% of the time, Pallas kernels for 0%

profile of v8, /device:TPU:32, one launch (start us, length us, event | category | flops | bytes accessed | tf_op | source)
XLA Modules:
  0.0 180.2 jit_solution(6441023870967667806)
XLA Ops:
  0.0 0.0 copy-start.5
  0.0 0.0 copy-start.6
  0.0 0.0 copy-start.7
  0.0 0.0 copy-start.10
  0.0 0.0 copy-start.9
  0.0 0.0 copy-start.8
  0.0 0.0 copy-start.4
  0.0 0.0 copy-start.3
  0.1 0.6 copy-done.5
  0.7 0.1 broadcast_in_dim.20
  0.8 32.6 %all_to_all.40 = bf16[32,3,2,256]{3,2,1,0:T(2,128)(2,1)S(1)} all-to-all(bf16[32,3,2,256]{3,2,1,0:T(2,128)(2,1)S(1)} %broadcast_in_dim.20), channel_id=1, replica_groups=mesh['member'=16,'patch'=32] {'patch'}, dimensions={0} | all-to-all | bytes 196608 | tf_op jit(solution)/shard_map/all_to_all | solution.py:26
  33.4 0.1 copy.22
  33.4 0.0 copy-done.6
  33.5 0.0 copy-done.7
  33.5 0.0 copy-done.10
  33.5 0.0 copy-done.9
  33.5 0.0 copy-done.8
  33.5 0.0 copy-done.4
  33.5 0.0 copy-done.3
  33.5 1.3 fusion.179
  34.8 0.1 broadcast_in_dim.21
  34.9 19.5 %all_to_all.41 = bf16[32,3,2,256]{3,2,1,0:T(2,128)(2,1)S(1)} all-to-all(bf16[32,3,2,256]{3,2,1,0:T(2,128)(2,1)S(1)} %broadcast_in_dim.21), channel_id=1, replica_groups=mesh['member'=16,'patch'=32] {'patch'}, dimensions={0} | all-to-all | bytes 196608 | tf_op jit(solution)/shard_map/all_to_all | solution.py:26
  54.5 0.1 copy.23
  54.5 1.3 fusion.178
  55.8 0.1 broadcast_in_dim.22
  55.9 18.7 %all_to_all.42 = bf16[32,3,2,256]{3,2,1,0:T(2,128)(2,1)S(1)} all-to-all(bf16[32,3,2,256]{3,2,1,0:T(2,128)(2,1)S(1)} %broadcast_in_dim.22), channel_id=1, replica_groups=mesh['member'=16,'patch'=32] {'patch'}, dimensions={0} | all-to-all | bytes 196608 | tf_op jit(solution)/shard_map/all_to_all | solution.py:26
  74.6 0.1 copy.24
  74.7 1.3 fusion.177
  76.0 0.1 broadcast_in_dim.23
  76.1 18.7 %all_to_all.43 = bf16[32,3,2,256]{3,2,1,0:T(2,128)(2,1)S(1)} all-to-all(bf16[32,3,2,256]{3,2,1,0:T(2,128)(2,1)S(1)} %broadcast_in_dim.23), channel_id=1, replica_groups=mesh['member'=16,'patch'=32] {'patch'}, dimensions={0} | all-to-all | bytes 196608 | tf_op jit(solution)/shard_map/all_to_all | solution.py:26
  94.8 0.1 copy.25
  94.9 1.3 fusion.176
  96.2 0.1 broadcast_in_dim.24
  96.3 18.9 %all_to_all.44 = bf16[32,3,2,256]{3,2,1,0:T(2,128)(2,1)S(1)} all-to-all(bf16[32,3,2,256]{3,2,1,0:T(2,128)(2,1)S(1)} %broadcast_in_dim.24), channel_id=1, replica_groups=mesh['member'=16,'patch'=32] {'patch'}, dimensions={0} | all-to-all | bytes 196608 | tf_op jit(solution)/shard_map/all_to_all | solution.py:26
  115.1 0.1 copy.26
  115.2 1.3 multiply_add_fusion.2
  116.5 0.5 fusion.175
  117.1 0.1 broadcast_in_dim.25
  117.1 18.7 %all_to_all.45 = bf16[32,3,2,256]{3,2,1,0:T(2,128)(2,1)S(1)} all-to-all(bf16[32,3,2,256]{3,2,1,0:T(2,128)(2,1)S(1)} %broadcast_in_dim.25), channel_id=1, replica_groups=mesh['member'=16,'patch'=32] {'patch'}, dimensions={0} | all-to-all | bytes 196608 | tf_op jit(solution)/shard_map/all_to_all | solution.py:26
  135.9 0.1 copy.27
  135.9 0.0 copy-start.1
  135.9 0.0 copy-start.2
  135.9 0.0 copy-start
  136.0 1.3 multiply_add_fusion
  137.3 0.1 broadcast_in_dim.26
  137.4 18.7 %all_to_all.46 = bf16[32,3,2,256]{3,2,1,0:T(2,128)(2,1)S(1)} all-to-all(bf16[32,3,2,256]{3,2,1,0:T(2,128)(2,1)S(1)} %broadcast_in_dim.26), channel_id=1, replica_groups=mesh['member'=16,'patch'=32] {'patch'}, dimensions={0} | all-to-all | bytes 196608 | tf_op jit(solution)/shard_map/all_to_all | solution.py:26
  156.1 0.1 copy.28
  156.2 1.3 fusion.174.rate_ref
  157.5 0.0 copy-done.1
  157.5 0.0 copy-done.2
  157.5 0.2 shard_map.110
  157.7 10.6 %all_to_all.47.got_ref = f32[16,8,128]{2,1,0:T(8,128)S(1)} all-to-all(f32[16,8,128]{2,1,0:T(8,128)S(1)} %shard_map.110), channel_id=1, replica_groups=mesh['member'=16,'patch'=32] {'member'}, dimensions={0} | all-to-all | bytes 131072 | tf_op jit(solution)/shard_map/all_to_all | solution.py:375
  168.2 0.1 shard_map.111
  168.3 1.3 collective-permute-start
  169.6 6.4 %collective-permute-done.across_ref = f32[16,128]{1,0:T(8,128)S(1)} collective-permute-done((f32[16,128]{1,0:T(8,128)S(1)}, f32[16,128]{1,0:T(8,128)S(1)}, u32[]{:S(2)}, u32[]{:S(2)}) %collective-permute-start) | collective-permute-done | bytes 8224 | tf_op jit(solution)/shard_map/ppermute | solution.py:380
  176.0 0.0 copy-done
  176.0 4.2 %shard_map.112 = f32[3,16,96]{2,1,0:T(8,128)} custom-call(f32[80,128]{1,0:T(8,128)S(1)} %get-tuple-element.29.turned_ref, f32[16,128]{1,0:T(8,128)S(1)} %collective-permute-done.across_ref, f32[4,72,128]{2,1,0:T(8,128)S(1)} %copy-done), custom_call_target="tpu_custom_call" | custom-call | tf_op jit(solution)/shard_map/pallas_call | solution.py:289
  (24 shorter events, 0.2 us)
Async XLA Ops:
  0.0 0.7 copy-start.5
  0.0 33.4 %copy-start.6 = (f32[256]{0:T(256)S(1)}, f32[256]{0:T(256)}, u32[]{:S(2)}) copy-start(f32[256]{0:T(256)} %param.16) | copy-start | bytes 3076
  0.0 33.5 %copy-start.7 = (f32[256]{0:T(256)S(1)}, f32[256]{0:T(256)}, u32[]{:S(2)}) copy-start(f32[256]{0:T(256)} %param.15) | copy-start | bytes 3076
  0.0 33.5 %copy-start.10 = (f32[256]{0:T(256)S(1)}, f32[256]{0:T(256)}, u32[]{:S(2)}) copy-start(f32[256]{0:T(256)} %param.14) | copy-start | bytes 3076
  0.0 33.5 %copy-start.9 = (f32[256]{0:T(256)S(1)}, f32[256]{0:T(256)}, u32[]{:S(2)}) copy-start(f32[256]{0:T(256)} %param.13) | copy-start | bytes 3076
  0.0 33.5 %copy-start.8 = (f32[256]{0:T(256)S(1)}, f32[256]{0:T(256)}, u32[]{:S(2)}) copy-start(f32[256]{0:T(256)} %param.12) | copy-start | bytes 3076
  0.0 33.5 %copy-start.4 = (f32[6,256]{1,0:T(8,128)S(1)}, f32[6,256]{1,0:T(8,128)}, u32[]{:S(2)}) copy-start(f32[6,256]{1,0:T(8,128)} %param.18) | copy-start | bytes 18436
  0.0 33.5 %copy-start.3 = (bf16[256,8192]{1,0:T(8,128)(2,1)S(1)}, bf16[256,8192]{1,0:T(8,128)(2,1)}, u32[]{:S(2)}) copy-start(bf16[256,8192]{1,0:T(8,128)(2,1)} %param.11) | copy-start | bytes 12582916
  135.9 21.6 %copy-start.1 = (f32[256]{0:T(256)S(1)}, f32[256]{0:T(256)}, u32[]{:S(2)}) copy-start(f32[256]{0:T(256)} %param.19) | copy-start | bytes 3076
  135.9 21.6 %copy-start.2 = (f32[256]{0:T(256)S(1)}, f32[256]{0:T(256)}, u32[]{:S(2)}) copy-start(f32[256]{0:T(256)} %param.20) | copy-start | bytes 3076
  135.9 40.0 %copy-start = (f32[4,72,128]{2,1,0:T(8,128)S(1)}, f32[4,72,128]{2,1,0:T(8,128)}, u32[]{:S(2)}) copy-start(f32[4,72,128]{2,1,0:T(8,128)} %constant.27.clone.table_ref) | copy-start | bytes 442372
  168.3 7.7 %collective-permute-start = (f32[16,128]{1,0:T(8,128)S(1)}, f32[16,128]{1,0:T(8,128)S(1)}, u32[]{:S(2)}, u32[]{:S(2)}) collective-permute-start(f32[16,128]{1,0:T(8,128)S(1)} %get-tuple-element.30), channel_id=1, source_target_pairs={{64,1},{65,2},{66,3},{67,4},{68,5},{69,6},{70,7},{71,8},{72,9},{73... | collective-permute-start | bytes 24584 | tf_op jit(solution)/shard_map/ppermute | solution.py:380

commit v9 on v8

--- a/solution.py
+++ b/solution.py
@@ -369,7 +369,7 @@
         change, state_change, velocity = tendency(gathered, deficit_two, state_two, velocity)
         deficit = deficit_zero / 3.0 + 2.0 / 3.0 * (deficit_two + time_step * change)
         state_log = state_zero / 3.0 + 2.0 / 3.0 * (state_two + time_step * state_change)
-    deficit, state_log, velocity = lax.optimization_barrier((deficit, state_log, velocity))
+        deficit, state_log, velocity = lax.optimization_barrier((deficit, state_log, velocity))
     forecast = section_rate(gather(deficit.astype(BF16)), deficit, state_log, velocity)
     sent = pack(deficit, state_log, forecast, obs_rate, obs_precision, groups)
     received = lax.all_to_all(sent, "member", split_axis=0, concat_axis=0, tiled=True)

time: 181 us -> 180 us (level)
  no operation moved by 1% of the time
where the time goes in v9:
time: 180 us
  blocking collectives  156 us (87%)
  matrix products  8.99 us (5%)
  waiting for transfers between devices  6.35 us (4%)
  Pallas kernels  4.44 us (2%)
    all_to_all x7, blocking collectives, from_everyone(): return lax.all_to_all(copies, axis, split_axis=0, concat_axis=0, tiled=True)  146 us
    all_to_all x1, blocking collectives, body(): lax.all_to_all(sent, 'member', split_axis=0, concat_axis=0, tiled=True)  10.6 us
    dot_general x7, matrix products, section_rate(): lax.dot_general(gathered, kernel_rows, (((1,), (1,)), ((), ())), preferre...  8.99 us
    ppermute x1, waiting for transfers between devices, body(): across = lax.ppermute(own_ends, ('member', 'patch'), pairs)  6.35 us
    pallas_call x1, Pallas kernels, analyse(): pl.pallas_call(functools.partial(analysis_kernel, ensemble), out_shape=ja...  4.2 us
  transfers between devices with their start and end apart: 1, of which 1 were waited for; matrix products, arithmetic and copies ran while one was open for 0% of the time, Pallas kernels for 0%

profile of v9, /device:TPU:32, one launch (start us, length us, event | category | flops | bytes accessed | tf_op | source)
XLA Modules:
  0.0 179.6 jit_solution(12973407293096354379)
XLA Ops:
  0.0 0.0 copy-start.4
  0.0 0.0 copy-start.6
  0.0 0.0 copy-start.7
  0.0 0.0 copy-start.10
  0.0 0.0 copy-start.9
  0.0 0.0 copy-start.8
  0.0 0.0 copy-start.3
  0.0 0.0 copy-start.5
  0.1 0.6 copy-done.4
  0.7 0.1 broadcast_in_dim.20
  0.8 32.6 %all_to_all.40 = bf16[32,3,2,256]{3,2,1,0:T(2,128)(2,1)S(1)} all-to-all(bf16[32,3,2,256]{3,2,1,0:T(2,128)(2,1)S(1)} %broadcast_in_dim.20), channel_id=1, replica_groups=mesh['member'=16,'patch'=32] {'patch'}, dimensions={0} | all-to-all | bytes 196608 | tf_op jit(solution)/shard_map/all_to_all | solution.py:26
  33.4 0.1 copy.22
  33.4 0.0 copy-done.6
  33.5 0.0 copy-done.7
  33.5 0.0 copy-done.10
  33.5 0.0 copy-done.9
  33.5 0.0 copy-done.8
  33.5 0.0 copy-done.3
  33.5 0.0 copy-done.5
  33.5 1.3 fusion.178
  34.8 0.1 broadcast_in_dim.21
  34.9 19.5 %all_to_all.41 = bf16[32,3,2,256]{3,2,1,0:T(2,128)(2,1)S(1)} all-to-all(bf16[32,3,2,256]{3,2,1,0:T(2,128)(2,1)S(1)} %broadcast_in_dim.21), channel_id=1, replica_groups=mesh['member'=16,'patch'=32] {'patch'}, dimensions={0} | all-to-all | bytes 196608 | tf_op jit(solution)/shard_map/all_to_all | solution.py:26
  54.5 0.1 copy.23
  54.5 1.3 fusion.177
  55.8 0.1 broadcast_in_dim.22
  55.9 18.7 %all_to_all.42 = bf16[32,3,2,256]{3,2,1,0:T(2,128)(2,1)S(1)} all-to-all(bf16[32,3,2,256]{3,2,1,0:T(2,128)(2,1)S(1)} %broadcast_in_dim.22), channel_id=1, replica_groups=mesh['member'=16,'patch'=32] {'patch'}, dimensions={0} | all-to-all | bytes 196608 | tf_op jit(solution)/shard_map/all_to_all | solution.py:26
  74.6 0.1 copy.24
  74.7 1.3 multiply_add_fusion.6
  76.0 0.1 broadcast_in_dim.23
  76.1 18.7 %all_to_all.43 = bf16[32,3,2,256]{3,2,1,0:T(2,128)(2,1)S(1)} all-to-all(bf16[32,3,2,256]{3,2,1,0:T(2,128)(2,1)S(1)} %broadcast_in_dim.23), channel_id=1, replica_groups=mesh['member'=16,'patch'=32] {'patch'}, dimensions={0} | all-to-all | bytes 196608 | tf_op jit(solution)/shard_map/all_to_all | solution.py:26
  94.8 0.1 copy.25
  94.9 1.3 fusion.176
  96.2 0.1 broadcast_in_dim.24
  96.3 18.9 %all_to_all.44 = bf16[32,3,2,256]{3,2,1,0:T(2,128)(2,1)S(1)} all-to-all(bf16[32,3,2,256]{3,2,1,0:T(2,128)(2,1)S(1)} %broadcast_in_dim.24), channel_id=1, replica_groups=mesh['member'=16,'patch'=32] {'patch'}, dimensions={0} | all-to-all | bytes 196608 | tf_op jit(solution)/shard_map/all_to_all | solution.py:26
  115.1 0.1 copy.26
  115.2 1.3 fusion.175
  116.5 0.1 broadcast_in_dim.25
  116.6 18.7 %all_to_all.45 = bf16[32,3,2,256]{3,2,1,0:T(2,128)(2,1)S(1)} all-to-all(bf16[32,3,2,256]{3,2,1,0:T(2,128)(2,1)S(1)} %broadcast_in_dim.25), channel_id=1, replica_groups=mesh['member'=16,'patch'=32] {'patch'}, dimensions={0} | all-to-all | bytes 196608 | tf_op jit(solution)/shard_map/all_to_all | solution.py:26
  135.3 0.1 copy.27
  135.4 0.0 copy-start.1
  135.4 0.0 copy-start.2
  135.4 0.0 copy-start
  135.4 1.3 multiply_add_fusion
  136.7 0.1 broadcast_in_dim.26
  136.8 18.7 %all_to_all.46 = bf16[32,3,2,256]{3,2,1,0:T(2,128)(2,1)S(1)} all-to-all(bf16[32,3,2,256]{3,2,1,0:T(2,128)(2,1)S(1)} %broadcast_in_dim.26), channel_id=1, replica_groups=mesh['member'=16,'patch'=32] {'patch'}, dimensions={0} | all-to-all | bytes 196608 | tf_op jit(solution)/shard_map/all_to_all | solution.py:26
  155.6 0.1 copy.28
  155.6 1.3 fusion.174.rate_ref
  156.9 0.0 copy-done.1
  156.9 0.0 copy-done.2
  156.9 0.2 shard_map.110
  157.1 10.6 %all_to_all.47.got_ref = f32[16,8,128]{2,1,0:T(8,128)S(1)} all-to-all(f32[16,8,128]{2,1,0:T(8,128)S(1)} %shard_map.110), channel_id=1, replica_groups=mesh['member'=16,'patch'=32] {'member'}, dimensions={0} | all-to-all | bytes 131072 | tf_op jit(solution)/shard_map/all_to_all | solution.py:375
  167.7 0.1 shard_map.111
  167.8 1.3 collective-permute-start
  169.1 6.4 %collective-permute-done.across_ref = f32[16,128]{1,0:T(8,128)S(1)} collective-permute-done((f32[16,128]{1,0:T(8,128)S(1)}, f32[16,128]{1,0:T(8,128)S(1)}, u32[]{:S(2)}, u32[]{:S(2)}) %collective-permute-start) | collective-permute-done | bytes 8224 | tf_op jit(solution)/shard_map/ppermute | solution.py:380
  175.4 0.0 copy-done
  175.4 4.2 %shard_map.112 = f32[3,16,96]{2,1,0:T(8,128)} custom-call(f32[80,128]{1,0:T(8,128)S(1)} %get-tuple-element.35.turned_ref, f32[16,128]{1,0:T(8,128)S(1)} %collective-permute-done.across_ref, f32[4,72,128]{2,1,0:T(8,128)S(1)} %copy-done), custom_call_target="tpu_custom_call" | custom-call | tf_op jit(solution)/shard_map/pallas_call | solution.py:289
  (25 shorter events, 0.2 us)
Async XLA Ops:
  0.0 0.7 copy-start.4
  0.0 33.4 %copy-start.6 = (f32[256]{0:T(256)S(1)}, f32[256]{0:T(256)}, u32[]{:S(2)}) copy-start(f32[256]{0:T(256)} %param.16) | copy-start | bytes 3076
  0.0 33.5 %copy-start.7 = (f32[256]{0:T(256)S(1)}, f32[256]{0:T(256)}, u32[]{:S(2)}) copy-start(f32[256]{0:T(256)} %param.15) | copy-start | bytes 3076
  0.0 33.5 %copy-start.10 = (f32[256]{0:T(256)S(1)}, f32[256]{0:T(256)}, u32[]{:S(2)}) copy-start(f32[256]{0:T(256)} %param.14) | copy-start | bytes 3076
  0.0 33.5 %copy-start.9 = (f32[256]{0:T(256)S(1)}, f32[256]{0:T(256)}, u32[]{:S(2)}) copy-start(f32[256]{0:T(256)} %param.13) | copy-start | bytes 3076
  0.0 33.5 %copy-start.8 = (f32[256]{0:T(256)S(1)}, f32[256]{0:T(256)}, u32[]{:S(2)}) copy-start(f32[256]{0:T(256)} %param.12) | copy-start | bytes 3076
  0.0 33.5 %copy-start.3 = (bf16[256,8192]{1,0:T(8,128)(2,1)S(1)}, bf16[256,8192]{1,0:T(8,128)(2,1)}, u32[]{:S(2)}) copy-start(bf16[256,8192]{1,0:T(8,128)(2,1)} %param.11) | copy-start | bytes 12582916
  0.0 33.5 %copy-start.5 = (f32[6,256]{1,0:T(8,128)S(1)}, f32[6,256]{1,0:T(8,128)}, u32[]{:S(2)}) copy-start(f32[6,256]{1,0:T(8,128)} %param.18) | copy-start | bytes 18436
  135.4 21.6 %copy-start.1 = (f32[256]{0:T(256)S(1)}, f32[256]{0:T(256)}, u32[]{:S(2)}) copy-start(f32[256]{0:T(256)} %param.19) | copy-start | bytes 3076
  135.4 21.6 %copy-start.2 = (f32[256]{0:T(256)S(1)}, f32[256]{0:T(256)}, u32[]{:S(2)}) copy-start(f32[256]{0:T(256)} %param.20) | copy-start | bytes 3076
  135.4 40.0 %copy-start = (f32[4,72,128]{2,1,0:T(8,128)S(1)}, f32[4,72,128]{2,1,0:T(8,128)}, u32[]{:S(2)}) copy-start(f32[4,72,128]{2,1,0:T(8,128)} %constant.27.clone.table_ref) | copy-start | bytes 442372
  167.8 7.7 %collective-permute-start = (f32[16,128]{1,0:T(8,128)S(1)}, f32[16,128]{1,0:T(8,128)S(1)}, u32[]{:S(2)}, u32[]{:S(2)}) collective-permute-start(f32[16,128]{1,0:T(8,128)S(1)} %get-tuple-element.36), channel_id=1, source_target_pairs={{64,1},{65,2},{66,3},{67,4},{68,5},{69,6},{70,7},{71,8},{72,9},{73... | collective-permute-start | bytes 24584 | tf_op jit(solution)/shard_map/ppermute | solution.py:380
